TPU v7x, 32 devices: a whole 2x2x4 slice. The times are simulated.
32 devices in a mesh: seq: 8 (over z, y), ch: 4 (over x, core).
Axes of the slice: x: 2, y: 2, z: 4, core: 2. Of those that a mesh axis runs over, the one named last changes fastest.
Arguments:
- inputs: bfloat16 [1024, 1024], P('ch', 'seq'), may hold values from -6 to 6
- out_grad: bfloat16 [1024, 1024], P('ch', 'seq'), may hold values from -6 to 6
- readout: float32 [2, 1024, 64], P(None, 'ch'), may hold values from -4 to 4
- log_step: float32 [1024], P('ch'), may hold values from -10.5 to -3
- decay_log: float32 [64], replicated, may hold values from -1.4 to 0
- rotation: float32 [64], replicated, may hold values from 0 to 200
Outputs:
- kernel_grad: float32 [1024, 1024], P('ch', 'seq')
- readout_grad: float32 [2, 1024, 64], P(None, 'ch')
- step_grad: float32 [1024], P('ch')
- state_grad: float32 [2, 64], replicated
All inputs are finite; a program needn't handle non-finite values.
Results may differ from a plain program's by a relative error of at most 0.0005.
Values may be sent and summed in bfloat16 or wider, within the bound.
No kernel may reach another device: no remote copies, remote signals or barrier semaphores. Data moves between devices by JAX's collectives and lax.ppermute only.
A program may use at most 64 MiB of HBM per device.

v0:
```python
import math

import jax
import jax.numpy as jnp
from jax import lax
from jax.sharding import PartitionSpec as P

precise = lax.Precision.HIGHEST
two_pi = 2.0 * math.pi


def angle_table(left_index, right_index, modulus, orient):
    product = left_index[:, None] * right_index[None, :] % modulus
    return orient * two_pi * product.astype(jnp.float32) / modulus


def rotate(real_part, imag_part, angles):
    cosine_table = jnp.cos(angles)
    sine_table = jnp.sin(angles)
    return (
        real_part * cosine_table - imag_part * sine_table,
        real_part * sine_table + imag_part * cosine_table,
    )


def last_transform(real_part, imag_part, orient):
    length = real_part.shape[-1]
    counter = jnp.arange(length, dtype=jnp.int32)
    angles = angle_table(counter, counter, length, orient)
    cosine_table = jnp.cos(angles)
    sine_table = jnp.sin(angles)
    out_real = jnp.dot(
        real_part, cosine_table, precision=precise, preferred_element_type=jnp.float32
    ) - jnp.dot(imag_part, sine_table, precision=precise, preferred_element_type=jnp.float32)
    out_imag = jnp.dot(
        imag_part, cosine_table, precision=precise, preferred_element_type=jnp.float32
    ) + jnp.dot(real_part, sine_table, precision=precise, preferred_element_type=jnp.float32)
    return (out_real, out_imag)


def correlation_spectrum(in_real, in_imag, out_real, out_imag):
    return (out_real * in_real + out_imag * in_imag, out_imag * in_real - out_real * in_imag)


def discretize(readout, log_step, decay_log, rotation):
    step_size = jnp.exp(log_step)[:, None]
    pole_real = -jnp.exp(decay_log)[None, :]
    pole_imag = rotation[None, :]
    rate_real = step_size * pole_real
    rate_imag = step_size * pole_imag
    lift_real = jnp.expm1(rate_real) * jnp.cos(rate_imag) - 2.0 * jnp.sin(0.5 * rate_imag) ** 2
    lift_imag = jnp.exp(rate_real) * jnp.sin(rate_imag)
    pole_norm = pole_real * pole_real + pole_imag * pole_imag
    ratio_real = (lift_real * pole_real + lift_imag * pole_imag) / pole_norm
    ratio_imag = (lift_imag * pole_real - lift_real * pole_imag) / pole_norm
    coef_real = readout[0] * ratio_real - readout[1] * ratio_imag
    coef_imag = readout[0] * ratio_imag + readout[1] * ratio_real
    return (coef_real, coef_imag, rate_real, rate_imag)


def parameter_grads(primal, backward, totals):
    coef_real, coef_imag = (primal[0], primal[1])
    cotangents = (
        2.0 * totals[0],
        -2.0 * totals[1],
        2.0 * (coef_real * totals[2] - coef_imag * totals[3]),
        -2.0 * (coef_real * totals[3] + coef_imag * totals[2]),
    )
    return backward(cotangents)


def shifted_totals(raw_sums, rate_real, rate_imag, block_start, norm_scale):
    decays = jnp.exp(rate_real * block_start)
    phases = rate_imag * block_start
    base_real = decays * jnp.cos(phases)
    base_imag = decays * jnp.sin(phases)
    near_real = block_start * raw_sums[0] + raw_sums[2]
    near_imag = block_start * raw_sums[1] + raw_sums[3]
    return jnp.stack(
        [
            norm_scale * (base_real * raw_sums[0] - base_imag * raw_sums[1]),
            norm_scale * (base_real * raw_sums[1] + base_imag * raw_sums[0]),
            norm_scale * (base_real * near_real - base_imag * near_imag),
            norm_scale * (base_real * near_imag + base_imag * near_real),
        ]
    )


def whole_channel_totals(lag_rows, rate_real, rate_imag, norm_scale):
    owners, length = (lag_rows.shape[1], lag_rows.shape[2])
    offsets = jnp.arange(length, dtype=jnp.int32).astype(jnp.float32)
    decays = jnp.exp(rate_real[:, :, None] * offsets)
    phases = rate_imag[:, :, None] * offsets
    power_real = decays * jnp.cos(phases)
    power_imag = decays * jnp.sin(phases)
    weighted = lag_rows * offsets
    raw_sums = jnp.stack(
        [
            jnp.einsum("cbj,cnj->cnb", lag_rows, power_real, precision=precise),
            jnp.einsum("cbj,cnj->cnb", lag_rows, power_imag, precision=precise),
            jnp.einsum("cbj,cnj->cnb", weighted, power_real, precision=precise),
            jnp.einsum("cbj,cnj->cnb", weighted, power_imag, precision=precise),
        ]
    )
    starts = (jnp.arange(owners, dtype=jnp.int32) * length).astype(jnp.float32)
    totals = shifted_totals(
        raw_sums, rate_real[:, :, None], rate_imag[:, :, None], starts, norm_scale
    )
    return jnp.sum(totals, axis=-1)


def per_device(inputs, out_grad, readout, log_step, decay_log, rotation):
    owners = lax.axis_size("seq")
    self_index = lax.axis_index("seq")
    channels, length = inputs.shape
    freq_width = 2 * owners
    modulus = freq_width * length
    norm_scale = 1.0 / math.sqrt(owners * length)
    part_count = channels // owners
    stacked = jnp.stack([inputs, out_grad])
    whole = lax.all_to_all(stacked, "seq", split_axis=1, concat_axis=2, tiled=True).astype(
        jnp.float32
    )
    whole = whole.reshape(2, part_count, owners, length)
    row_index = jnp.arange(owners, dtype=jnp.int32)
    outer_index = jnp.arange(freq_width, dtype=jnp.int32)
    inner_index = jnp.arange(length, dtype=jnp.int32)
    first = angle_table(row_index, outer_index, freq_width, -1.0)
    spec_real = jnp.einsum("scba,bk->scka", whole, jnp.cos(first), precision=precise)
    spec_imag = jnp.einsum("scba,bk->scka", whole, jnp.sin(first), precision=precise)
    spec_real, spec_imag = rotate(
        spec_real, spec_imag, angle_table(outer_index, inner_index, modulus, -1.0)
    )
    freq_real, freq_imag = last_transform(spec_real, spec_imag, -1.0)
    prod_real, prod_imag = correlation_spectrum(
        freq_real[0], freq_imag[0], freq_real[1], freq_imag[1]
    )
    back_real, back_imag = last_transform(prod_real, prod_imag, 1.0)
    back_real, back_imag = rotate(
        back_real, back_imag, angle_table(outer_index, inner_index, modulus, 1.0)
    )
    final = angle_table(outer_index, row_index, freq_width, 1.0)
    lag_rows = jnp.einsum("cka,kb->cba", back_real, jnp.cos(final), precision=precise) - jnp.einsum(
        "cka,kb->cba", back_imag, jnp.sin(final), precision=precise
    )
    lag_rows = lag_rows * (norm_scale / modulus)
    kernel_grad = lax.all_to_all(
        lag_rows.reshape(part_count, owners * length),
        "seq",
        split_axis=1,
        concat_axis=0,
        tiled=True,
    )
    first_channel = self_index * part_count
    own_readout = lax.dynamic_slice_in_dim(readout, first_channel, part_count, 1)
    own_step = lax.dynamic_slice_in_dim(log_step, first_channel, part_count, 0)
    primal, backward = jax.vjp(discretize, own_readout, own_step, decay_log, rotation)
    totals = whole_channel_totals(lag_rows, primal[2], primal[3], norm_scale)
    readout_part, step_part, decay_part, rotation_part = parameter_grads(primal, backward, totals)
    readout_grad, step_grad = (
        lax.all_gather(readout_part, "seq", axis=1, tiled=True),
        lax.all_gather(step_part, "seq", axis=0, tiled=True),
    )
    state_grad = lax.psum(jnp.stack([decay_part, rotation_part]), ("seq", "ch"))
    return (kernel_grad, readout_grad, step_grad, state_grad)


def solution(mesh):
    return jax.shard_map(
        per_device,
        mesh=mesh,
        in_specs=(P("ch", "seq"), P("ch", "seq"), P(None, "ch", None), P("ch"), P(), P()),
        out_specs=(P("ch", "seq"), P(None, "ch", None), P("ch"), P()),
        check_vma=False,
    )
```

profile of v0, /device:TPU:0, one launch (start us, length us, event | category | flops | bytes accessed | tf_op | source)
XLA Modules:
  0.0 145.0 jit_solution(11516750346020152685)
XLA Ops:
  0.6 0.9 pad_maximum_fusion
  1.5 0.8 copy.26
  2.3 7.4 %all-to-all-start = ((bf16[2,256,128]{2,0,1:T(2,128)(2,1)}), bf16[2,256,128]{2,0,1:T(2,128)(2,1)S(1)}, u32[]{:S(2)}, u32[]{:S(2)}) async-start(bf16[2,256,128]{2,0,1:T(2,128)(2,1)} %copy.26), calls=%async_computation | async-start | bytes 262144 | tf_op jit(solution)/shard_map/all_to_all | solution.py:121
  9.7 0.1 multiply_sine_fusion.11
  9.8 0.1 multiply_sine_fusion.10
  9.9 0.0 copy-start.1
  9.9 0.0 copy-start.2
  9.9 0.6 copy-done.1
  10.6 0.0 copy-done.2
  10.6 0.0 copy-start.3
  10.6 0.1 constant_dynamic-slice_fusion
  10.7 0.6 copy-done.3
  11.3 0.1 dynamic-slice_exponential_fusion
  11.3 0.1 copy.40
  11.4 0.1 copy.41
  11.5 0.7 copy-done.4
  12.2 0.6 dynamic-slice
  13.4 0.1 broadcast_multiply_fusion.1
  13.5 3.6 %all-to-all-done = bf16[2,256,128]{2,0,1:T(2,128)(2,1)S(1)} async-done(((bf16[2,256,128]{2,0,1:T(2,128)(2,1)}), bf16[2,256,128]{2,0,1:T(2,128)(2,1)S(1)}, u32[]{:S(2)}, u32[]{:S(2)}) %all-to-all-start) | async-done | bytes 131104 | tf_op jit(solution)/shard_map/all_to_all | solution.py:121
  17.1 0.5 fusion.43
  17.6 0.5 fusion.45
  18.1 0.8 fusion.12
  18.9 0.8 fusion.8
  19.7 0.8 convolution_subtract_fusion
  20.6 0.8 convolution_add_fusion
  21.4 0.1 multiply_add_fusion.1
  21.5 0.6 fusion.30
  22.1 0.6 fusion.26
  22.7 0.6 convolution_subtract_fusion.1
  23.3 0.6 convolution_add_fusion.1
  23.9 0.3 fusion.35
  24.3 0.3 convolution_subtract_fusion.2
  24.6 5.4 %fusion.3 = f32[32,64,8]{1,2,0:T(8,128)S(1)} fusion(f32[32,64]{1,0:T(8,128)S(1)} %get-tuple-element.52, f32[128]{0:T(128)S(1)} %iota_convert_fusion, f32[32,64]{1,0:T(8,128)S(1)} %get-tuple-element.51, f32[8,32,128]{2,0,1:T(8,128)S(1)} %convolution_subtract_fusion.2), kind=kOutput, calls=%fused_computation.12 | convolution fusion | flops 25985024 | bytes 213504 | tf_op jit(solution)/shard_map/cbj,cnj->cnb/dot_general | solution.py:100
  30.0 5.2 %fusion.6 = f32[32,64,8]{1,2,0:T(8,128)S(1)} fusion(f32[32,64]{1,0:T(8,128)S(1)} %get-tuple-element.52, f32[128]{0:T(128)S(1)} %iota_convert_fusion, f32[32,64]{1,0:T(8,128)S(1)} %get-tuple-element.51, f32[8,32,128]{2,0,1:T(8,128)S(1)} %convolution_subtract_fusion.2), kind=kOutput, calls=%fused_computation.13 | convolution fusion | flops 25985024 | bytes 213504 | tf_op jit(solution)/shard_map/cbj,cnj->cnb/dot_general | solution.py:99
  35.3 5.3 %convolution_add_fusion.2 = f32[32,64,8]{1,2,0:T(8,128)S(1)} fusion(f32[32,64]{1,0:T(8,128)S(1)} %get-tuple-element.52, f32[128]{0:T(128)S(1)} %iota_convert_fusion, f32[32,64]{1,0:T(8,128)S(1)} %get-tuple-element.51, f32[32,64,8]{1,2,0:T(8,128)S(1)} %fusion.3, f32[8,32,128]{2,0,1:T(8,128)S(1)} %convolution_subtract_fusion.2, ...), kind=kOutput, calls=%fused_computation.6 | convolution fusion | flops 26017792 | bytes 279584 | tf_op jit(solution)/shard_map/cbj,cnj->cnb/dot_general | solution.py:102
  40.5 5.7 %multiply_bitcast_fusion.3 = (f32[1,32,64,8]{2,3,1,0:T(8,128)S(1)}, f32[1,32,64,8]{2,3,1,0:T(8,128)S(1)}, f32[1,32,64,8]{2,3,1,0:T(8,128)S(1)}, f32[1,32,64,8]{2,3,1,0:T(8,128)S(1)}) fusion(f32[32,64,8]{1,2,0:T(8,128)S(1)} %fusion.3, f32[32,64,8]{1,2,0:T(8,128)S(1)} %fusion.6, f32[32,64]{1,0:T(8,128)S(1)} %get-tuple-element.52, ...), kind=kOutput, calls=%fused_computation.64 | convolution fusion | flops 26345472 | bytes 607264 | tf_op jit(solution)/shard_map/cbj,cnj->cnb/dot_general | solution.py:101
  46.2 0.2 maximum_reduce_fusion
  46.4 0.2 fusion.126
  46.7 0.7 copy.29
  47.4 3.4 %all-to-all-start.1 = ((f32[32,8,128]{2,0,1:T(8,128)}), f32[32,8,128]{2,0,1:T(8,128)S(1)}, u32[]{:S(2)}, u32[]{:S(2)}) async-start(f32[32,8,128]{2,0,1:T(8,128)} %copy.29), calls=%async_computation.1 | async-start | bytes 262144 | tf_op jit(solution)/shard_map/all_to_all | solution.py:147
  50.7 0.2 fusion.102
  51.0 0.4 multiply_reduce_fusion.7
  51.4 31.3 %all_gather.6 = f32[2,256,64]{2,0,1:T(2,128)S(1)} all-gather(f32[2,32,64]{2,0,1:T(2,128)S(1)} %copy.30), channel_id=1, replica_groups=mesh['seq'=8,'ch'=4] {'seq'}, dimensions={1}, use_global_device_ids=true | all-gather | bytes 147456 | tf_op jit(solution)/shard_map/all_gather | solution.py:161
  82.6 0.8 copy.32
  83.4 39.6 %psum.7 = f32[2,64]{1,0:T(2,128)} all-reduce(f32[2,64]{1,0:T(2,128)S(1)} %pad_maximum_fusion.1), channel_id=1, replica_groups=mesh['seq'=8,'ch'=4] {'seq','ch'}, use_global_device_ids=true, to_apply=%region_11.12 | all-reduce | flops 128 | bytes 1024 | tf_op jit(solution)/shard_map/psum | solution.py:164
  123.0 0.2 multiply_dynamic-update-slice_fusion
  123.1 21.2 %all-reduce.4 = f32[256]{0:T(256)} all-reduce(f32[256]{0:T(256)S(1)} %multiply_dynamic-update-slice_fusion), channel_id=1, replica_groups=mesh['seq'=8,'ch'=4] {'seq'}, use_global_device_ids=true, to_apply=%add.4 | all-reduce | flops 256 | bytes 2048
  144.3 0.7 copy.52
  (14 shorter events, 0.1 us)
Async XLA Ops:
  2.3 8.3 %copy-start = (f32[2,256,64]{1,2,0:T(8,128)S(1)}, f32[2,256,64]{1,2,0:T(8,128)}, u32[]{:S(2)}) copy-start(f32[2,256,64]{1,2,0:T(8,128)} %param.8) | copy-start | bytes 393220
  2.3 14.8 %all-to-all-start = ((bf16[2,256,128]{2,0,1:T(2,128)(2,1)}), bf16[2,256,128]{2,0,1:T(2,128)(2,1)S(1)}, u32[]{:S(2)}, u32[]{:S(2)}) async-start(bf16[2,256,128]{2,0,1:T(2,128)(2,1)} %copy.26), calls=%async_computation | async-start | bytes 262144 | tf_op jit(solution)/shard_map/all_to_all | solution.py:121
  9.9 0.7 copy-start.1
  9.9 0.7 copy-start.2
  10.6 0.7 copy-start.3
  11.5 0.7 copy-start.4
  47.4 96.9 %all-to-all-start.1 = ((f32[32,8,128]{2,0,1:T(8,128)}), f32[32,8,128]{2,0,1:T(8,128)S(1)}, u32[]{:S(2)}, u32[]{:S(2)}) async-start(f32[32,8,128]{2,0,1:T(8,128)} %copy.29), calls=%async_computation.1 | async-start | bytes 262144 | tf_op jit(solution)/shard_map/all_to_all | solution.py:147
where the time goes:
time: 146 us; the launch traced here: 145 us
  blocking collectives  92 us (63%)
  matrix products  29 us (20%)
  starting transfers between devices  10.8 us (7%)
  local copies, waits for them, and re-layouts  5.74 us (4%)
  waiting for transfers between devices  3.6 us (2%)
  other arithmetic  2.35 us (2%)
  between operations  1.52 us (1%)
    psum x1, blocking collectives, per_device(): state_grad = lax.psum(jnp.stack([decay_part, rotation_part]), ('seq', 'ch'))  39.6 us
    all_gather x1, blocking collectives, per_device(): lax.all_gather(readout_part, 'seq', axis=1, tiled=True)  31.3 us
    unnamed x1, blocking collectives  21.2 us
    all_to_all x1, starting transfers between devices, per_device(): lax.all_to_all(stacked, 'seq', split_axis=1, concat_axis=2, tiled=True)  7.41 us
    dot_general x1, matrix products, whole_channel_totals(): jnp.einsum('cbj,cnj->cnb', weighted, power_real, precision=precise)  5.7 us
    dot_general x1, matrix products, whole_channel_totals(): jnp.einsum('cbj,cnj->cnb', lag_rows, power_imag, precision=precise)  5.42 us
    dot_general x1, matrix products, whole_channel_totals(): jnp.einsum('cbj,cnj->cnb', weighted, power_imag, precision=precise)  5.26 us
    dot_general x1, matrix products, whole_channel_totals(): jnp.einsum('cbj,cnj->cnb', lag_rows, power_real, precision=precise)  5.22 us
  transfers between devices with their start and end apart: 2, of which 1 were waited for; matrix products, arithmetic and copies ran while one was open for 2% of the time, Pallas kernels for 0%

commit v1 on v0

--- a/solution.py
+++ b/solution.py
@@ -1,12 +1,18 @@
+import functools
 import math
 
 import jax
 import jax.numpy as jnp
+import numpy as np
 from jax import lax
+from jax.experimental import pallas as pl
+from jax.experimental.pallas import tpu as pltpu
 from jax.sharding import PartitionSpec as P
 
 precise = lax.Precision.HIGHEST
 two_pi = 2.0 * math.pi
+LANES = 128
+SUBLANES = 8
 
 
 def angle_table(left_index, right_index, modulus, orient):
@@ -29,17 +35,11 @@
     angles = angle_table(counter, counter, length, orient)
     cosine_table = jnp.cos(angles)
     sine_table = jnp.sin(angles)
-    out_real = jnp.dot(
-        real_part, cosine_table, precision=precise, preferred_element_type=jnp.float32
-    ) - jnp.dot(imag_part, sine_table, precision=precise, preferred_element_type=jnp.float32)
-    out_imag = jnp.dot(
-        imag_part, cosine_table, precision=precise, preferred_element_type=jnp.float32
-    ) + jnp.dot(real_part, sine_table, precision=precise, preferred_element_type=jnp.float32)
-    return (out_real, out_imag)
-
-
-def correlation_spectrum(in_real, in_imag, out_real, out_imag):
-    return (out_real * in_real + out_imag * in_imag, out_imag * in_real - out_real * in_imag)
+    dot = functools.partial(jnp.dot, precision=precise, preferred_element_type=jnp.float32)
+    return (
+        dot(real_part, cosine_table) - dot(imag_part, sine_table),
+        dot(imag_part, cosine_table) + dot(real_part, sine_table),
+    )
 
 
 def discretize(readout, log_step, decay_log, rotation):
@@ -109,19 +109,10 @@
     return jnp.sum(totals, axis=-1)
 
 
-def per_device(inputs, out_grad, readout, log_step, decay_log, rotation):
-    owners = lax.axis_size("seq")
-    self_index = lax.axis_index("seq")
-    channels, length = inputs.shape
+def general_lags(whole, norm_scale):
+    part_count, owners, length = whole.shape[1:]
     freq_width = 2 * owners
     modulus = freq_width * length
-    norm_scale = 1.0 / math.sqrt(owners * length)
-    part_count = channels // owners
-    stacked = jnp.stack([inputs, out_grad])
-    whole = lax.all_to_all(stacked, "seq", split_axis=1, concat_axis=2, tiled=True).astype(
-        jnp.float32
-    )
-    whole = whole.reshape(2, part_count, owners, length)
     row_index = jnp.arange(owners, dtype=jnp.int32)
     outer_index = jnp.arange(freq_width, dtype=jnp.int32)
     inner_index = jnp.arange(length, dtype=jnp.int32)
@@ -132,9 +123,8 @@
         spec_real, spec_imag, angle_table(outer_index, inner_index, modulus, -1.0)
     )
     freq_real, freq_imag = last_transform(spec_real, spec_imag, -1.0)
-    prod_real, prod_imag = correlation_spectrum(
-        freq_real[0], freq_imag[0], freq_real[1], freq_imag[1]
-    )
+    prod_real = freq_real[1] * freq_real[0] + freq_imag[1] * freq_imag[0]
+    prod_imag = freq_imag[1] * freq_real[0] - freq_real[1] * freq_imag[0]
     back_real, back_imag = last_transform(prod_real, prod_imag, 1.0)
     back_real, back_imag = rotate(
         back_real, back_imag, angle_table(outer_index, inner_index, modulus, 1.0)
@@ -143,33 +133,408 @@
     lag_rows = jnp.einsum("cka,kb->cba", back_real, jnp.cos(final), precision=precise) - jnp.einsum(
         "cka,kb->cba", back_imag, jnp.sin(final), precision=precise
     )
-    lag_rows = lag_rows * (norm_scale / modulus)
-    kernel_grad = lax.all_to_all(
-        lag_rows.reshape(part_count, owners * length),
-        "seq",
-        split_axis=1,
-        concat_axis=0,
-        tiled=True,
-    )
-    first_channel = self_index * part_count
+    return lag_rows * (norm_scale / modulus)
+
+
+def general_device(inputs, out_grad, readout, log_step, decay_log, rotation):
+    owners = lax.axis_size("seq")
+    channels, length = inputs.shape
+    states = decay_log.shape[0]
+    part_count = channels // owners
+    norm_scale = 1.0 / math.sqrt(owners * length)
+    pieces = jnp.concatenate(
+        [a.reshape(owners, part_count, length) for a in (inputs, out_grad)], axis=1
+    )
+    pieces = lax.all_to_all(pieces, "seq", split_axis=0, concat_axis=0, tiled=True)
+    whole = pieces.astype(jnp.float32).reshape(owners, 2, part_count, length)
+    lag_rows = general_lags(whole.transpose(1, 2, 0, 3), norm_scale)
+    first_channel = lax.axis_index("seq") * part_count
     own_readout = lax.dynamic_slice_in_dim(readout, first_channel, part_count, 1)
     own_step = lax.dynamic_slice_in_dim(log_step, first_channel, part_count, 0)
     primal, backward = jax.vjp(discretize, own_readout, own_step, decay_log, rotation)
     totals = whole_channel_totals(lag_rows, primal[2], primal[3], norm_scale)
     readout_part, step_part, decay_part, rotation_part = parameter_grads(primal, backward, totals)
-    readout_grad, step_grad = (
-        lax.all_gather(readout_part, "seq", axis=1, tiled=True),
-        lax.all_gather(step_part, "seq", axis=0, tiled=True),
-    )
-    state_grad = lax.psum(jnp.stack([decay_part, rotation_part]), ("seq", "ch"))
-    return (kernel_grad, readout_grad, step_grad, state_grad)
+    shared = jnp.concatenate(
+        [readout_part.reshape(-1), step_part, decay_part, rotation_part]
+    )
+    sent = jnp.concatenate(
+        [
+            lag_rows.transpose(1, 0, 2).reshape(owners, -1),
+            jnp.broadcast_to(shared, (owners, shared.shape[0])),
+        ],
+        axis=1,
+    )
+    got = lax.all_to_all(sent, "seq", split_axis=0, concat_axis=0, tiled=True)
+    cuts = np.cumsum([part_count * length, 2 * part_count * states, part_count])
+    lags, readouts, steps, state = jnp.split(got, cuts, axis=1)
+    readouts = readouts.reshape(owners, 2, part_count, states).transpose(1, 0, 2, 3)
+    return (
+        lags.reshape(channels, length),
+        readouts.reshape(2, channels, states),
+        steps.reshape(channels),
+        lax.psum(jnp.sum(state, axis=0), "ch").reshape(2, states),
+    )
+
+
+def split_halves(value):
+    high = value.astype(jnp.bfloat16)
+    return high, (value - high.astype(jnp.float32)).astype(jnp.bfloat16)
+
+
+def cos_sin(angle):
+    turns = jnp.floor(angle * (2.0 / math.pi) + 0.5)
+    rest = angle - turns * 1.5703125
+    rest = rest - turns * 4.837512969970703125e-4
+    rest = rest - turns * 7.54978995489188216e-8
+    quarter = turns.astype(jnp.int32)
+    square = rest * rest
+    sine = rest + rest * square * (
+        -1.6666654611e-1 + square * (8.3321608736e-3 - square * 1.9515295891e-4)
+    )
+    cosine = (
+        1.0
+        - 0.5 * square
+        + square
+        * square
+        * (
+            4.166664568298827e-2
+            + square * (-1.388731625493765e-3 + square * 2.443315711809948e-5)
+        )
+    )
+    odd = (quarter & 1) == 1
+    out_cos = jnp.where(odd, sine, cosine)
+    out_sin = jnp.where(odd, cosine, sine)
+    out_cos = jnp.where(((quarter + 1) & 2) == 2, -out_cos, out_cos)
+    out_sin = jnp.where((quarter & 2) == 2, -out_sin, out_sin)
+    return out_cos, out_sin
+
+
+def grow(value):
+    series = 1.0
+    for term in range(9, 1, -1):
+        series = 1.0 + series * value * (1.0 / term)
+    return jnp.where(jnp.abs(value) < 0.35, series * value, jnp.exp(value) - 1.0)
+
+
+def power(rate_real, rate_imag, offset):
+    size = jnp.exp(rate_real * offset)
+    cosine, sine = cos_sin(rate_imag * offset)
+    return size * cosine, size * sine
+
+
+def times(left, right):
+    return (
+        left[0] * right[0] - left[1] * right[1],
+        left[0] * right[1] + left[1] * right[0],
+    )
+
+
+RATE, RATIO, COEF, READ, LIFTED, POLE, INVERSE, STEP = range(8)
+
+
+def table_kernel(owners, length, readout, log_step, decay_log, rotation, powers, bases, params):
+    pairs = log_step.shape[0]
+    step = jnp.exp(log_step[...])
+    pole = (jnp.broadcast_to(-jnp.exp(decay_log[...]), step.shape), jnp.broadcast_to(rotation[...], step.shape))
+    rate = (step * pole[0], step * pole[1])
+    size = jnp.exp(rate[0])
+    cosine, sine = cos_sin(rate[1])
+    half = cos_sin(0.5 * rate[1])[1]
+    lift = (grow(rate[0]) * cosine - 2.0 * half * half, size * sine)
+    norm = 1.0 / (pole[0] * pole[0] + pole[1] * pole[1])
+    inverse = (pole[0] * norm, -pole[1] * norm)
+    ratio = times(lift, inverse)
+    read = (readout[0], readout[1])
+    lifted = times((size * cosine, size * sine), inverse)
+    zero = jnp.zeros_like(step)
+    for place, value in (
+        (RATE, rate),
+        (RATIO, ratio),
+        (COEF, times(read, ratio)),
+        (READ, read),
+        (LIFTED, lifted),
+        (POLE, pole),
+        (INVERSE, inverse),
+        (STEP, (step, zero)),
+    ):
+        params[2 * place] = value[0]
+        params[2 * place + 1] = value[1]
+    row = lax.broadcasted_iota(jnp.int32, (SUBLANES, LANES), 0).astype(jnp.float32)
+    doublings = []
+    size = SUBLANES
+    while size < length:
+        doublings.append(size)
+        size *= 2
+
+    @pl.loop(0, pairs)
+    def _(pair):
+        rate_real = params[2 * RATE, pl.ds(pair, 1), :]
+        rate_imag = params[2 * RATE + 1, pl.ds(pair, 1), :]
+        steps = [power(rate_real, rate_imag, float(size)) for size in doublings]
+        table = [power(rate_real, rate_imag, row)]
+        for shift in steps:
+            table += [times(block, shift) for block in table]
+        for place in range(0, len(table), 2):
+            spot = place * SUBLANES
+            for side in range(2):
+                value = jnp.concatenate([table[place][side], table[place + 1][side]], axis=0)
+                high, low = split_halves(value)
+                lanes = slice(side * LANES, (side + 1) * LANES)
+                powers[pair, spot : spot + 2 * SUBLANES, lanes] = high
+                powers[pair, length + spot : length + spot + 2 * SUBLANES, lanes] = low
+        for spot in range(0, owners, SUBLANES):
+            real, imag = power(rate_real, rate_imag, (row + spot) * float(length))
+            bases[pair, spot : spot + SUBLANES, 0:LANES] = real
+            bases[pair, spot : spot + SUBLANES, LANES : 2 * LANES] = imag
+
+
+def weighted_sum(terms):
+    total = None
+    for weight, value in terms:
+        if abs(weight) < 1e-12:
+            continue
+        if abs(abs(weight) - 1.0) < 1e-12:
+            term = value if weight > 0 else -value
+        else:
+            term = value * weight
+        total = term if total is None else total + term
+    return total
+
+
+def turn(count, width):
+    angle = two_pi * (count % width) / width
+    return math.cos(angle), math.sin(angle)
+
+
+def precise_dot(value, matrix):
+    high, low = split_halves(value)
+    dot = functools.partial(jnp.dot, preferred_element_type=jnp.float32)
+    return dot(high, matrix[0]) + dot(low, matrix[0]) + dot(high, matrix[1])
+
+
+def main_kernel(
+    part_count, norm_scale, got, matrix, twiddle, powers, bases, params, sent, lags, sums
+):
+    owners, rows, length = got.shape
+    width = 2 * owners
+    pairs = part_count // 2
+
+    blocks = [got[s].astype(jnp.float32) for s in range(owners)]
+    spectra = []
+    for k in range(owners + 1):
+        real = weighted_sum([(turn(k * s, width)[0], blocks[s]) for s in range(owners)])
+        imag = weighted_sum([(-turn(k * s, width)[1], blocks[s]) for s in range(owners)])
+        if imag is None:
+            imag = jnp.zeros_like(real)
+        if k:
+            real, imag = times((real, imag), (twiddle[k, 0:1], twiddle[k, 1:2]))
+        spectra.append(jnp.concatenate([real, imag], axis=1))
+    freq = precise_dot(jnp.concatenate(spectra, axis=0), matrix)
+
+    products = []
+    for k in range(owners + 1):
+        at_in = freq[k * rows : k * rows + part_count]
+        at_out = freq[k * rows + part_count : (k + 1) * rows]
+        ur, ui = at_in[:, :length], at_in[:, length:]
+        gr, gi = at_out[:, :length], at_out[:, length:]
+        products.append(jnp.concatenate([gr * ur + gi * ui, gr * ui - gi * ur], axis=1))
+    back = precise_dot(jnp.concatenate(products, axis=0), matrix)
+
+    turned = []
+    for k in range(owners + 1):
+        value = back[k * part_count : (k + 1) * part_count]
+        value = (value[:, :length], value[:, length:])
+        if k:
+            value = times(value, (twiddle[k, 0:1], twiddle[k, 1:2]))
+        turned.append(value)
+    scale = norm_scale / (width * length)
+    for b in range(owners):
+        terms = []
+        for k in range(owners + 1):
+            weight = scale if k in (0, owners) else 2.0 * scale
+            cosine, sine = turn(k * b, width)
+            terms += [(weight * cosine, turned[k][0]), (weight * sine, turned[k][1])]
+        block = weighted_sum(terms)
+        sent[b, 0:part_count] = block
+        lags[b * part_count : (b + 1) * part_count] = block
+
+    offset = lax.broadcasted_iota(jnp.int32, (owners, length), 1).astype(jnp.float32)
+    start = lax.broadcasted_iota(jnp.int32, (owners, LANES), 0).astype(jnp.float32) * float(length)
+    first = lax.broadcasted_iota(jnp.int32, (owners, LANES), 1) < LANES // 2
+    for p in range(pairs):
+        one = lags[pl.ds(2 * p, owners, stride=part_count), :]
+        two = lags[pl.ds(2 * p + 1, owners, stride=part_count), :]
+        high, low = split_halves(
+            jnp.concatenate([one, two, one * offset, two * offset], axis=0)
+        )
+        left = jnp.concatenate(
+            [
+                jnp.concatenate([high, high], axis=1),
+                jnp.concatenate([low, jnp.zeros_like(low)], axis=1),
+            ],
+            axis=0,
+        )
+        raw = jnp.dot(left, powers[p], preferred_element_type=jnp.float32)
+        raw = raw[: 4 * owners] + raw[4 * owners :]
+
+        def pick(place, side):
+            lanes = slice(side * LANES, (side + 1) * LANES)
+            top = raw[2 * place * owners : (2 * place + 1) * owners, lanes]
+            bottom = raw[(2 * place + 1) * owners : (2 * place + 2) * owners, lanes]
+            return jnp.where(first, top, bottom)
+
+        plain = (pick(0, 0), pick(0, 1))
+        near = (start * plain[0] + pick(1, 0), start * plain[1] + pick(1, 1))
+        base = (bases[p, :, 0:LANES], bases[p, :, LANES : 2 * LANES])
+        for place, value in enumerate(times(base, plain) + times(base, near)):
+            sums[place, p : p + 1] = jnp.sum(value, axis=0, keepdims=True)
+
+    def param(place):
+        return params[2 * place], params[2 * place + 1]
+
+    total = (sums[0] * (2.0 * norm_scale), sums[1] * (2.0 * norm_scale))
+    lag_total = (sums[2] * (2.0 * norm_scale), sums[3] * (2.0 * norm_scale))
+    on_read = times(total, param(RATIO))
+    on_rate = times(param(COEF), lag_total)
+    through = times(times(total, param(READ)), param(LIFTED))
+    on_rate = (on_rate[0] + through[0], on_rate[1] + through[1])
+    direct = times(times(total, param(COEF)), param(INVERSE))
+    step = params[2 * STEP]
+    on_pole = (step * on_rate[0] - direct[0], step * on_rate[1] - direct[1])
+    on_step = times(on_rate, param(RATE))[0]
+    on_decay = on_pole[0] * params[2 * POLE]
+    on_rotation = -on_pole[1]
+
+    lane = lax.broadcasted_iota(jnp.int32, (pairs, LANES), 1)
+    pair = lax.broadcasted_iota(jnp.int32, (pairs, LANES), 0)
+    even = jnp.sum(jnp.where(lane < LANES // 2, on_step, 0.0), axis=1, keepdims=True)
+    odd = jnp.sum(jnp.where(lane < LANES // 2, 0.0, on_step), axis=1, keepdims=True)
+    spread = jnp.where(lane == 2 * pair, even, jnp.where(lane == 2 * pair + 1, odd, 0.0))
+    step_row = jnp.sum(spread, axis=0, keepdims=True)
+    decay_row = jnp.sum(on_decay, axis=0, keepdims=True)
+    rotation_row = jnp.sum(on_rotation, axis=0, keepdims=True)
+    decay_row = decay_row + pltpu.roll(decay_row, LANES // 2, 1)
+    rotation_row = rotation_row + pltpu.roll(rotation_row, LANES // 2, 1)
+    state_row = jnp.where(lane[0:1] < LANES // 2, decay_row, rotation_row)
+    place = lax.broadcasted_iota(jnp.int32, (SUBLANES, LANES), 0)
+    tail = jnp.where(place == 0, step_row, jnp.where(place == 1, state_row, 0.0))
+    for b in range(owners):
+        sent[b, part_count : part_count + pairs] = on_read[0]
+        sent[b, part_count + pairs : 2 * part_count] = -on_read[1]
+        sent[b, 2 * part_count : 2 * part_count + SUBLANES] = tail
+
+
+def transform_tables(owners, length):
+    width = 2 * owners
+    counter = np.arange(length)
+    angles = two_pi * (counter[:, None] * counter[None, :] % length) / length
+    cosine, sine = np.cos(angles), np.sin(angles)
+    matrix = np.block([[cosine, -sine], [sine, cosine]]).astype(np.float32)
+    high = matrix.astype(jnp.bfloat16)
+    low = (matrix - high.astype(np.float32)).astype(jnp.bfloat16)
+    outer = np.arange(owners + 1)
+    angles = two_pi * (outer[:, None] * counter[None, :]) / (width * length)
+    twiddle = np.stack([np.cos(angles), -np.sin(angles)], axis=1).astype(np.float32)
+    return np.stack([high, low]), twiddle
+
+
+def sum_over(value, axis):
+    size = lax.axis_size(axis)
+    if size & (size - 1):
+        return lax.psum(value, axis)
+    reach = 1
+    while reach < size:
+        value = value + lax.ppermute(value, axis, [(i, i ^ reach) for i in range(size)])
+        reach *= 2
+    return value
+
+
+def kernel_device(inputs, out_grad, readout, log_step, decay_log, rotation):
+    owners = lax.axis_size("seq")
+    channels, length = inputs.shape
+    states = decay_log.shape[0]
+    part_count = channels // owners
+    pairs = part_count // 2
+    norm_scale = 1.0 / math.sqrt(owners * length)
+    vmem = pl.BlockSpec(memory_space=pltpu.VMEM)
+    memory = pltpu.CompilerParams(vmem_limit_bytes=32 * 1024 * 1024)
+
+    pieces = jnp.concatenate(
+        [a.reshape(owners, part_count, length) for a in (inputs, out_grad)], axis=1
+    )
+    got = lax.all_to_all(pieces, "seq", split_axis=0, concat_axis=0, tiled=True)
+
+    first_channel = lax.axis_index("seq") * part_count
+    own_readout = lax.dynamic_slice_in_dim(readout, first_channel, part_count, 1)
+    own_step = lax.dynamic_slice_in_dim(log_step, first_channel, part_count, 0)
+    powers, bases, params = pl.pallas_call(
+        functools.partial(table_kernel, owners, length),
+        out_shape=[
+            jax.ShapeDtypeStruct((pairs, 2 * length, 2 * LANES), jnp.bfloat16),
+            jax.ShapeDtypeStruct((pairs, owners, 2 * LANES), jnp.float32),
+            jax.ShapeDtypeStruct((16, pairs, LANES), jnp.float32),
+        ],
+        in_specs=[vmem] * 4,
+        out_specs=[vmem] * 3,
+        compiler_params=memory,
+        cost_estimate=pl.CostEstimate(
+            flops=pairs * length * LANES * 8, bytes_accessed=2**21, transcendentals=2**17
+        ),
+    )(
+        own_readout.reshape(2, pairs, LANES),
+        jnp.repeat(own_step.reshape(pairs, 2), states, axis=1),
+        jnp.tile(decay_log, 2)[None],
+        jnp.tile(rotation, 2)[None],
+    )
+
+    matrix, twiddle = transform_tables(owners, length)
+    sent_rows = 2 * part_count + SUBLANES
+    sent = pl.pallas_call(
+        functools.partial(main_kernel, part_count, norm_scale),
+        out_shape=jax.ShapeDtypeStruct((owners, sent_rows, LANES), jnp.float32),
+        in_specs=[vmem] * 6,
+        out_specs=vmem,
+        scratch_shapes=[
+            pltpu.VMEM((owners * part_count, length), jnp.float32),
+            pltpu.VMEM((4, pairs, LANES), jnp.float32),
+        ],
+        compiler_params=memory,
+        cost_estimate=pl.CostEstimate(
+            flops=2**28, bytes_accessed=2**22, transcendentals=0
+        ),
+    )(got, jnp.asarray(matrix), jnp.asarray(twiddle), powers, bases, params)
+    back = lax.all_to_all(sent, "seq", split_axis=0, concat_axis=0, tiled=True)
+
+    kernel_grad = back[:, :part_count].reshape(channels, length)
+    readout_grad = back[:, part_count : 2 * part_count].reshape(owners, 2, pairs, LANES)
+    readout_grad = readout_grad.transpose(1, 0, 2, 3).reshape(2, channels, states)
+    step_grad = back[:, 2 * part_count, :part_count].reshape(channels)
+    state = jnp.sum(back[:, 2 * part_count + 1], axis=0).reshape(2, states)
+    return kernel_grad, readout_grad, step_grad, sum_over(state, "ch")
+
+
+def kernel_fits(mesh, inputs, decay_log):
+    owners = mesh.shape["seq"]
+    channels = inputs.shape[0] // mesh.shape["ch"]
+    part_count = channels // owners
+    return (
+        inputs.shape[1] == owners * LANES
+        and 2 * decay_log.shape[0] == LANES
+        and owners in (SUBLANES, 2 * SUBLANES)
+        and part_count % (2 * SUBLANES) == 0
+        and part_count <= LANES
+    )
 
 
 def solution(mesh):
-    return jax.shard_map(
-        per_device,
-        mesh=mesh,
-        in_specs=(P("ch", "seq"), P("ch", "seq"), P(None, "ch", None), P("ch"), P(), P()),
-        out_specs=(P("ch", "seq"), P(None, "ch", None), P("ch"), P()),
-        check_vma=False,
-    )
+    def whole(inputs, out_grad, readout, log_step, decay_log, rotation):
+        fits = kernel_fits(mesh, inputs, decay_log)
+        return jax.shard_map(
+            kernel_device if fits else general_device,
+            mesh=mesh,
+            in_specs=(P("ch", "seq"), P("ch", "seq"), P(None, "ch", None), P("ch"), P(), P()),
+            out_specs=(P("ch", "seq"), P(None, "ch", None), P("ch"), P()),
+            check_vma=False,
+        )(inputs, out_grad, readout, log_step, decay_log, rotation)
+
+    return whole

time: 146 us -> 38.4 us (0.26)
  blocking collectives: 92 us -> 12.3 us
  matrix products: 29 us -> 0 us
  Pallas kernels: 0 us -> 3.09 us
  starting transfers between devices: 10.8 us -> 8.77 us
    psum x1 -> x0, blocking collectives: 39.6 us -> none  [per_device(): state_grad = lax.psum(jnp.stack([decay_part, rotation_part]), ('seq', 'ch'))]
    all_gather x1 -> x0, blocking collectives: 31.3 us -> none  [per_device(): lax.all_gather(readout_part, 'seq', axis=1, tiled=True)]
    dot_general x16 -> x0, matrix products: 29 us -> none  [the longest x1 5.7 us: whole_channel_totals(): jnp.einsum('cbj,cnj->cnb', weighted, power_real, precision=precise)]
    unnamed x1 -> x0, blocking collectives: 21.2 us -> none
    all_to_all x0 -> x1, blocking collectives: none -> 12.3 us  [kernel_device(): back = lax.all_to_all(sent, 'seq', split_axis=0, concat_axis=0, tiled=True)]
    all_to_all x2 -> x1, starting transfers between devices: 10.8 us -> 7.28 us  [kernel_device(): got = lax.all_to_all(pieces, 'seq', split_axis=0, concat_axis=0, tiled=True)]
    pallas_call x0 -> x2, Pallas kernels: none -> 3.09 us  [the longest x1 1.74 us: kernel_device(): pl.pallas_call(functools.partial(main_kernel, part_count, norm_scale), ou...]
    unnamed x16 -> x7, local copies, waits for them, and re-layouts: 4.08 us -> 2.43 us
  transfers between devices with their start and end apart: 2 -> 3, of which waited for: 1 -> 3; matrix products, arithmetic and copies ran while one was open for 2% -> 13% of each run, Pallas kernels for 0% -> 4%
where the time goes in v1:
time: 38.4 us; the launch traced here: 38 us
  blocking collectives  12.3 us (32%)
  starting transfers between devices  8.77 us (23%)
  local copies, waits for them, and re-layouts  6.68 us (17%)
  waiting for transfers between devices  4.24 us (11%)
  Pallas kernels  3.09 us (8%)
  other arithmetic  2.17 us (6%)
  between operations  0.69 us (2%)
    all_to_all x1, blocking collectives, kernel_device(): back = lax.all_to_all(sent, 'seq', split_axis=0, concat_axis=0, tiled=True)  12.3 us
    all_to_all x1, starting transfers between devices, kernel_device(): got = lax.all_to_all(pieces, 'seq', split_axis=0, concat_axis=0, tiled=True)  7.28 us
    all_to_all x1, waiting for transfers between devices, kernel_device(): got = lax.all_to_all(pieces, 'seq', split_axis=0, concat_axis=0, tiled=True)  3.26 us
    unnamed x7, local copies, waits for them, and re-layouts  2.43 us
    pallas_call x1, Pallas kernels, kernel_device(): pl.pallas_call(functools.partial(main_kernel, part_count, norm_scale), ou...  1.74 us
    concatenate x1, other arithmetic, kernel_device(): jnp.concatenate([a.reshape(owners, part_count, length) for a in (inputs,...  1.57 us
    ppermute x2, starting transfers between devices, sum_over(): lax.ppermute(value, axis, [(i, i ^ reach) for i in range(size)])  1.49 us
    pallas_call x1, Pallas kernels, kernel_device(): pl.pallas_call(functools.partial(table_kernel, owners, length), out_shape...  1.34 us
  transfers between devices with their start and end apart: 3, of which 3 were waited for; matrix products, arithmetic and copies ran while one was open for 13% of the time, Pallas kernels for 4%

profile of v1, /device:TPU:0, one launch (start us, length us, event | category | flops | bytes accessed | tf_op | source)
XLA Modules:
  0.0 38.0 jit_solution(7004962516557062180)
XLA Ops:
  0.6 0.0 copy-start
  0.6 1.6 %pad_maximum_fusion = bf16[8,64,128]{2,1,0:T(8,128)(2,1)} fusion(bf16[8,32,128]{2,1,0:T(8,128)(2,1)} %bitcast.12, bf16[8,32,128]{2,1,0:T(8,128)(2,1)} %bitcast.13), kind=kLoop, calls=%fused_computation | loop fusion | flops 262144 | bytes 262144 | tf_op jit(solution)/shard_map/concatenate | solution.py:462
  2.2 7.3 %all-to-all-start = ((bf16[8,64,128]{2,1,0:T(8,128)(2,1)}), bf16[8,64,128]{2,1,0:T(8,128)(2,1)S(1)}, u32[]{:S(2)}, u32[]{:S(2)}) async-start(bf16[8,64,128]{2,1,0:T(8,128)(2,1)} %pad_maximum_fusion), calls=%async_computation | async-start | bytes 262144 | tf_op jit(solution)/shard_map/all_to_all | solution.py:465
  9.5 0.7 %tile.4 = f32[2,64]{1,0:T(2,128)S(1)} broadcast(f32[64]{0:T(128)} %param.12), dimensions={1} | broadcast | bytes 768 | tf_op jit(solution)/shard_map/tile | solution.py:486
  10.2 0.1 broadcast_in_dim_tile.6.decay_log
  10.2 0.7 %tile.5 = f32[2,64]{1,0:T(2,128)S(1)} broadcast(f32[64]{0:T(128)} %param.13), dimensions={1} | broadcast | bytes 768 | tf_op jit(solution)/shard_map/tile | solution.py:487
  10.9 0.1 broadcast_in_dim_tile.7.rotation
  11.0 0.8 %dynamic_slice.7 = f32[32]{0:T(128)S(1)} dynamic-slice(f32[256]{0:T(256)} %param.11, s32[]{:T(128)S(6)} %select_n.4), dynamic_slice_sizes={32} | dynamic-slice | bytes 260 | tf_op jit(solution)/shard_map/dynamic_slice | solution.py:469
  11.7 0.1 reshape.40
  11.8 0.1 broadcast_in_dim.3
  11.9 0.1 reshape.41.log_step
  12.0 0.0 copy-done
  12.0 0.1 constant_dynamic-slice_fusion
  12.1 0.1 copy.13
  12.2 0.1 reshape.39.readout
  12.2 1.3 %shard_map.111 = (bf16[16,256,256]{2,1,0:T(8,128)(2,1)S(1)}, f32[16,8,256]{2,1,0:T(8,128)S(1)}, f32[16,16,128]{2,1,0:T(8,128)S(1)}) custom-call(f32[2,16,128]{2,1,0:T(8,128)S(1)} %reshape.39.readout, f32[16,128]{1,0:T(8,128)S(1)} %reshape.41.log_step, f32[1,128]{1,0:T(1,128)S(1)} %broadcast_in_dim_tile.6.decay_log, f32[1,128]{1,0:T(1,128)S(1)} %broadcast_in_dim_tile.7.rotation), custom_call_target="tpu_custom_call" | custom-call | flops 2097152 | bytes 2097152 | tf_op jit(solution)/shard_map/pallas_call | solution.py:470
  13.6 3.3 %all-to-all-done.got = bf16[8,64,128]{2,1,0:T(8,128)(2,1)S(1)} async-done(((bf16[8,64,128]{2,1,0:T(8,128)(2,1)}), bf16[8,64,128]{2,1,0:T(8,128)(2,1)S(1)}, u32[]{:S(2)}, u32[]{:S(2)}) %all-to-all-start) | async-done | bytes 131104 | tf_op jit(solution)/shard_map/all_to_all | solution.py:465
  16.8 0.0 copy-start.1
  16.8 0.9 %copy-done.1 = bf16[2,256,256]{2,1,0:T(8,128)(2,1)S(1)} copy-done((bf16[2,256,256]{2,1,0:T(8,128)(2,1)S(1)}, bf16[2,256,256]{2,1,0:T(8,128)(2,1)}, u32[]{:S(2)}) %copy-start.1) | copy-done | bytes 262168
  17.8 0.0 copy-start.2
  17.8 0.7 %copy-done.2 = f32[9,2,128]{2,1,0:T(2,128)S(1)} copy-done((f32[9,2,128]{2,1,0:T(2,128)S(1)}, f32[9,2,128]{2,1,0:T(2,128)}, u32[]{:S(2)}) %copy-start.2) | copy-done | bytes 9240
  18.5 1.7 %shard_map.112 = f32[8,72,128]{2,1,0:T(8,128)S(1)} custom-call(bf16[8,64,128]{2,1,0:T(8,128)(2,1)S(1)} %all-to-all-done.got, bf16[2,256,256]{2,1,0:T(8,128)(2,1)S(1)} %copy-done.1, f32[9,2,128]{2,1,0:T(2,128)S(1)} %copy-done.2, bf16[16,256,256]{2,1,0:T(8,128)(2,1)S(1)} %get-tuple-element.7.powers, f32[16,8,256]{2,1,0:T(8,128)S(1)} %get-tuple-element.8.bases, ...), custom_call_target="tpu_custom_call" | custom-call | flops 268435456 | bytes 4194304 | tf_op jit(solution)/shard_map/pallas_call | solution.py:492
  20.2 12.3 %all_to_all.10 = f32[8,72,128]{2,1,0:T(8,128)S(1)} all-to-all(f32[8,72,128]{2,1,0:T(8,128)S(1)} %shard_map.112), channel_id=1, replica_groups=mesh['seq'=8,'ch'=4] {'seq'}, dimensions={0} | all-to-all | bytes 589824 | tf_op jit(solution)/shard_map/all_to_all | solution.py:506
  32.6 0.1 reshape.45
  32.7 0.0 collective-permute-start
  32.7 0.7 %fusion = (f32[8,32,128]{2,1,0:T(8,128)S(1)}, f32[8,32,128]{2,1,0:T(8,128)}) fusion(f32[8,72,128]{2,1,0:T(8,128)S(1)} %all_to_all.10), kind=kLoop, calls=%fused_computation.5 | loop fusion | bytes 524288 | tf_op jit(solution)/shard_map/slice | solution.py:509
  33.4 0.5 %collective-permute-done = f32[2,64]{1,0:T(2,128)S(1)} collective-permute-done((f32[2,64]{1,0:T(2,128)S(1)}, f32[2,64]{1,0:T(2,128)S(1)}, u32[]{:S(2)}, u32[]{:S(2)}) %collective-permute-start) | collective-permute-done | bytes 544 | tf_op jit(solution)/shard_map/ppermute | solution.py:447
  33.8 1.5 %collective-permute-start.1 = (f32[2,64]{1,0:T(2,128)S(1)}, f32[2,64]{1,0:T(2,128)S(1)}, u32[]{:S(2)}, u32[]{:S(2)}) collective-permute-start(f32[2,64]{1,0:T(2,128)S(1)} %add.11), channel_id=1, source_target_pairs={{0,2},{1,3},{2,0},{3,1},{4,6},{5,7},{6,4},{7,5},{8,10},{9,11},{10,... | collective-permute-start | bytes 1544 | tf_op jit(solution)/shard_map/ppermute | solution.py:447
  35.4 0.6 %reshape_squeeze.3 = f32[256]{0:T(256)} reshape(f32[8,32]{1,0:T(8,128)S(1)} %slice_reduce_fusion.1) | data formatting | bytes 2048 | tf_op jit(solution)/shard_map/reshape;squeeze | solution.py:511
  36.0 0.1 reshape.44
  36.1 0.8 %copy.15 = f32[2,256,64]{1,2,0:T(8,128)} copy(f32[2,256,64]{2,1,0:T(8,128)S(1)} %reshape.44) | data formatting | bytes 262144
  36.9 0.5 %collective-permute-done.1 = f32[2,64]{1,0:T(2,128)S(1)} collective-permute-done((f32[2,64]{1,0:T(2,128)S(1)}, f32[2,64]{1,0:T(2,128)S(1)}, u32[]{:S(2)}, u32[]{:S(2)}) %collective-permute-start.1) | collective-permute-done | bytes 544 | tf_op jit(solution)/shard_map/ppermute | solution.py:447
  37.4 0.6 %add.12 = f32[2,64]{1,0:T(2,128)} add(f32[2,64]{1,0:T(2,128)S(1)} %add.11, f32[2,64]{1,0:T(2,128)S(1)} %collective-permute-done.1) | non-fusion elementwise | flops 128 | bytes 1536 | tf_op jit(solution)/shard_map/add | solution.py:447
  (4 shorter events, 0.1 us)
Async XLA Ops:
  0.6 11.4 %copy-start = (f32[2,256,64]{1,2,0:T(8,128)S(1)}, f32[2,256,64]{1,2,0:T(8,128)}, u32[]{:S(2)}) copy-start(f32[2,256,64]{1,2,0:T(8,128)} %param.10) | copy-start | bytes 393220
  2.2 14.6 %all-to-all-start = ((bf16[8,64,128]{2,1,0:T(8,128)(2,1)}), bf16[8,64,128]{2,1,0:T(8,128)(2,1)S(1)}, u32[]{:S(2)}, u32[]{:S(2)}) async-start(bf16[8,64,128]{2,1,0:T(8,128)(2,1)} %pad_maximum_fusion), calls=%async_computation | async-start | bytes 262144 | tf_op jit(solution)/shard_map/all_to_all | solution.py:465
  16.8 1.0 %copy-start.1 = (bf16[2,256,256]{2,1,0:T(8,128)(2,1)S(1)}, bf16[2,256,256]{2,1,0:T(8,128)(2,1)}, u32[]{:S(2)}) copy-start(bf16[2,256,256]{2,1,0:T(8,128)(2,1)} %constant.18.clone.matrix) | copy-start | bytes 786436
  17.8 0.7 %copy-start.2 = (f32[9,2,128]{2,1,0:T(2,128)S(1)}, f32[9,2,128]{2,1,0:T(2,128)}, u32[]{:S(2)}) copy-start(f32[9,2,128]{2,1,0:T(2,128)} %constant.19.clone.twiddle) | copy-start | bytes 27652
  32.7 1.1 %collective-permute-start = (f32[2,64]{1,0:T(2,128)S(1)}, f32[2,64]{1,0:T(2,128)S(1)}, u32[]{:S(2)}, u32[]{:S(2)}) collective-permute-start(f32[2,64]{1,0:T(2,128)S(1)} %reshape.45), channel_id=1, source_target_pairs={{0,1},{1,0},{2,3},{3,2},{4,5},{5,4},{6,7},{7,6},{8,9},{9,8},{10,11... | collective-permute-start | bytes 1544 | tf_op jit(solution)/shard_map/ppermute | solution.py:447
  33.8 3.6 %collective-permute-start.1 = (f32[2,64]{1,0:T(2,128)S(1)}, f32[2,64]{1,0:T(2,128)S(1)}, u32[]{:S(2)}, u32[]{:S(2)}) collective-permute-start(f32[2,64]{1,0:T(2,128)S(1)} %add.11), channel_id=1, source_target_pairs={{0,2},{1,3},{2,0},{3,1},{4,6},{5,7},{6,4},{7,5},{8,10},{9,11},{10,... | collective-permute-start | bytes 1544 | tf_op jit(solution)/shard_map/ppermute | solution.py:447

commit v2 on v1

--- a/solution.py
+++ b/solution.py
@@ -229,65 +229,6 @@
     )
 
 
-RATE, RATIO, COEF, READ, LIFTED, POLE, INVERSE, STEP = range(8)
-
-
-def table_kernel(owners, length, readout, log_step, decay_log, rotation, powers, bases, params):
-    pairs = log_step.shape[0]
-    step = jnp.exp(log_step[...])
-    pole = (jnp.broadcast_to(-jnp.exp(decay_log[...]), step.shape), jnp.broadcast_to(rotation[...], step.shape))
-    rate = (step * pole[0], step * pole[1])
-    size = jnp.exp(rate[0])
-    cosine, sine = cos_sin(rate[1])
-    half = cos_sin(0.5 * rate[1])[1]
-    lift = (grow(rate[0]) * cosine - 2.0 * half * half, size * sine)
-    norm = 1.0 / (pole[0] * pole[0] + pole[1] * pole[1])
-    inverse = (pole[0] * norm, -pole[1] * norm)
-    ratio = times(lift, inverse)
-    read = (readout[0], readout[1])
-    lifted = times((size * cosine, size * sine), inverse)
-    zero = jnp.zeros_like(step)
-    for place, value in (
-        (RATE, rate),
-        (RATIO, ratio),
-        (COEF, times(read, ratio)),
-        (READ, read),
-        (LIFTED, lifted),
-        (POLE, pole),
-        (INVERSE, inverse),
-        (STEP, (step, zero)),
-    ):
-        params[2 * place] = value[0]
-        params[2 * place + 1] = value[1]
-    row = lax.broadcasted_iota(jnp.int32, (SUBLANES, LANES), 0).astype(jnp.float32)
-    doublings = []
-    size = SUBLANES
-    while size < length:
-        doublings.append(size)
-        size *= 2
-
-    @pl.loop(0, pairs)
-    def _(pair):
-        rate_real = params[2 * RATE, pl.ds(pair, 1), :]
-        rate_imag = params[2 * RATE + 1, pl.ds(pair, 1), :]
-        steps = [power(rate_real, rate_imag, float(size)) for size in doublings]
-        table = [power(rate_real, rate_imag, row)]
-        for shift in steps:
-            table += [times(block, shift) for block in table]
-        for place in range(0, len(table), 2):
-            spot = place * SUBLANES
-            for side in range(2):
-                value = jnp.concatenate([table[place][side], table[place + 1][side]], axis=0)
-                high, low = split_halves(value)
-                lanes = slice(side * LANES, (side + 1) * LANES)
-                powers[pair, spot : spot + 2 * SUBLANES, lanes] = high
-                powers[pair, length + spot : length + spot + 2 * SUBLANES, lanes] = low
-        for spot in range(0, owners, SUBLANES):
-            real, imag = power(rate_real, rate_imag, (row + spot) * float(length))
-            bases[pair, spot : spot + SUBLANES, 0:LANES] = real
-            bases[pair, spot : spot + SUBLANES, LANES : 2 * LANES] = imag
-
-
 def weighted_sum(terms):
     total = None
     for weight, value in terms:
@@ -312,14 +253,152 @@
     return dot(high, matrix[0]) + dot(low, matrix[0]) + dot(high, matrix[1])
 
 
+def transform_tables(owners, length):
+    width = 2 * owners
+    counter = np.arange(length)
+    angles = two_pi * (counter[:, None] * counter[None, :] % length) / length
+    cosine, sine = np.cos(angles), np.sin(angles)
+    matrix = np.block([[cosine, -sine], [sine, cosine]]).astype(np.float32)
+    high = matrix.astype(jnp.bfloat16)
+    low = (matrix - high.astype(np.float32)).astype(jnp.bfloat16)
+    outer = np.arange(owners + 1)
+    angles = two_pi * (outer[:, None] * counter[None, :]) / (width * length)
+    twiddle = np.stack([np.cos(angles), -np.sin(angles)], axis=1).astype(np.float32)
+    return np.stack([high, low]), twiddle
+
+
+def three_pieces(value):
+    pieces = []
+    for _ in range(3):
+        piece = value.astype(jnp.bfloat16).astype(jnp.float32)
+        pieces.append(piece)
+        value = value - piece
+    return pieces
+
+
+def transposed(value):
+    return jnp.concatenate(
+        [value[:, spot : spot + LANES].T for spot in range(0, value.shape[1], LANES)], axis=0
+    )
+
+
+SIGNALS, READ, STEP, OUT_ROWS = 0, 16, 19, 24
+LAGS, GRADS, STATE, STEPS, SCALES, BACK_ROWS = 0, 8, 16, 18, 20, 24
+
+
+def pack_kernel(axis, inputs, out_grad, readout, log_step, out, rows, turned, peers_rows):
+    peers = out.shape[0]
+    own = lax.axis_index(axis)
+    for place, signal in enumerate((inputs, out_grad)):
+        value = signal[...].astype(jnp.float32).reshape(peers, SUBLANES, LANES)
+        peers_rows[:, SIGNALS + place * SUBLANES : SIGNALS + (place + 1) * SUBLANES] = value
+    turned[0] = transposed(readout[...])
+    turned[1] = transposed(jnp.broadcast_to(log_step[...], (LANES, log_step.shape[1])))
+    extra = []
+    for place in range(2):
+        value = turned[place, pl.ds(own, peers, stride=SUBLANES), :]
+        extra += three_pieces(value)
+    for place, value in enumerate(extra):
+        rows[pl.ds(place, peers, stride=SUBLANES), :] = value
+    zero = jnp.zeros((peers, LANES), jnp.float32)
+    for place in range(len(extra), SUBLANES):
+        rows[pl.ds(place, peers, stride=SUBLANES), :] = zero
+    peers_rows[:, READ:OUT_ROWS] = rows[...].reshape(peers, SUBLANES, LANES)
+    out[...] = peers_rows[...].astype(jnp.bfloat16)
+
+
+def hold_kernel(matrix, twiddle, out_matrix, out_twiddle):
+    out_matrix[...] = matrix[...]
+    out_twiddle[...] = twiddle[...]
+
+
+def scaled(value):
+    most = jnp.max(jnp.max(jnp.abs(value), axis=1, keepdims=True), axis=0, keepdims=True)
+    exponent = jnp.floor(jnp.log(jnp.maximum(most, 1e-30)) * (1.0 / math.log(2.0))) + 1.0
+    return value * jnp.exp2(-exponent), exponent
+
+
+def two_pieces(value):
+    high = value.astype(jnp.bfloat16).astype(jnp.float32)
+    return high, (value - high) * 256.0
+
+
 def main_kernel(
-    part_count, norm_scale, got, matrix, twiddle, powers, bases, params, sent, lags, sums
+    owners, norm_scale, got, matrix, twiddle, decay_log, rotation, sent, extra, lags, powers, sums
 ):
-    owners, rows, length = got.shape
+    peers, length = got.shape[0], got.shape[2]
+    groups = peers // owners
+    part_count = groups * SUBLANES
+    rows = 2 * part_count
     width = 2 * owners
     pairs = part_count // 2
-
-    blocks = [got[s].astype(jnp.float32) for s in range(owners)]
+    half = pairs // SUBLANES
+    got_rows = got[...].astype(jnp.float32)
+    extra[...] = got_rows[:, READ:OUT_ROWS].reshape(peers * SUBLANES, LANES)
+
+    def collect(first):
+        tiles = []
+        for group in range(groups):
+            pieces = [
+                extra[pl.ds(group * SUBLANES + first - READ + i, owners, stride=groups * SUBLANES), :]
+                for i in range(3)
+            ]
+            tiles.append(pieces[0] + pieces[1] + pieces[2])
+        return jnp.concatenate(tiles[:half], axis=0), jnp.concatenate(tiles[half:], axis=0)
+
+    lane = lax.broadcasted_iota(jnp.int32, (pairs, LANES), 1)
+    left = lane < LANES // 2
+
+    def swap(value):
+        return pltpu.roll(value, LANES // 2, 1)
+
+    lower, upper = collect(READ)
+    read = (jnp.where(left, lower, swap(upper)), jnp.where(left, swap(lower), upper))
+    lower, upper = collect(STEP)
+    step = jnp.exp(jnp.where(left, lower, upper))
+    decay_row = jnp.concatenate([decay_log[...], decay_log[...]], axis=1)
+    rotation_row = jnp.concatenate([rotation[...], rotation[...]], axis=1)
+    pole = (
+        jnp.broadcast_to(-jnp.exp(decay_row), step.shape),
+        jnp.broadcast_to(rotation_row, step.shape),
+    )
+    rate = (step * pole[0], step * pole[1])
+
+    row = lax.broadcasted_iota(jnp.int32, (SUBLANES, LANES), 0).astype(jnp.float32)
+    doublings = []
+    size = SUBLANES
+    while size < length:
+        doublings.append(size)
+        size *= 2
+    jumps = jnp.zeros((SUBLANES, LANES), jnp.float32)
+    for place, jump in enumerate(doublings):
+        jumps = jnp.where(row == place, float(jump), jumps)
+    bases = []
+    for p in range(pairs):
+        rate_real, rate_imag = rate[0][p : p + 1], rate[1][p : p + 1]
+        shifts = power(rate_real, rate_imag, jumps)
+        table = [power(rate_real, rate_imag, row)]
+        for place in range(len(doublings)):
+            shift = (shifts[0][place : place + 1], shifts[1][place : place + 1])
+            table += [times(block, shift) for block in table]
+        for place in range(0, len(table), 2):
+            spot = place * SUBLANES
+            for side in range(2):
+                value = jnp.concatenate([table[place][side], table[place + 1][side]], axis=0)
+                high, low = split_halves(value)
+                lanes = slice(side * LANES, (side + 1) * LANES)
+                powers[p, spot : spot + 2 * SUBLANES, lanes] = high
+                powers[p, length + spot : length + spot + 2 * SUBLANES, lanes] = low
+        bases.append(power(rate_real, rate_imag, row * float(length)))
+
+    blocks = []
+    for s in range(owners):
+        mine = got_rows[s * groups : (s + 1) * groups]
+        blocks.append(
+            jnp.concatenate(
+                [mine[:, :SUBLANES], mine[:, SUBLANES : 2 * SUBLANES]], axis=0
+            ).reshape(rows, length)
+        )
     spectra = []
     for k in range(owners + 1):
         real = weighted_sum([(turn(k * s, width)[0], blocks[s]) for s in range(owners)])
@@ -354,27 +433,25 @@
             weight = scale if k in (0, owners) else 2.0 * scale
             cosine, sine = turn(k * b, width)
             terms += [(weight * cosine, turned[k][0]), (weight * sine, turned[k][1])]
-        block = weighted_sum(terms)
-        sent[b, 0:part_count] = block
-        lags[b * part_count : (b + 1) * part_count] = block
+        lags[b * part_count : (b + 1) * part_count] = weighted_sum(terms)
 
     offset = lax.broadcasted_iota(jnp.int32, (owners, length), 1).astype(jnp.float32)
-    start = lax.broadcasted_iota(jnp.int32, (owners, LANES), 0).astype(jnp.float32) * float(length)
-    first = lax.broadcasted_iota(jnp.int32, (owners, LANES), 1) < LANES // 2
+    start = row * float(length)
+    first = left[:owners]
     for p in range(pairs):
-        one = lags[pl.ds(2 * p, owners, stride=part_count), :]
-        two = lags[pl.ds(2 * p + 1, owners, stride=part_count), :]
+        one = lags[pl.ds(p, owners, stride=part_count), :]
+        two = lags[pl.ds(pairs + p, owners, stride=part_count), :]
         high, low = split_halves(
             jnp.concatenate([one, two, one * offset, two * offset], axis=0)
         )
-        left = jnp.concatenate(
+        factor = jnp.concatenate(
             [
                 jnp.concatenate([high, high], axis=1),
                 jnp.concatenate([low, jnp.zeros_like(low)], axis=1),
             ],
             axis=0,
         )
-        raw = jnp.dot(left, powers[p], preferred_element_type=jnp.float32)
+        raw = jnp.dot(factor, powers[p], preferred_element_type=jnp.float32)
         raw = raw[: 4 * owners] + raw[4 * owners :]
 
         def pick(place, side):
@@ -385,72 +462,97 @@
 
         plain = (pick(0, 0), pick(0, 1))
         near = (start * plain[0] + pick(1, 0), start * plain[1] + pick(1, 1))
-        base = (bases[p, :, 0:LANES], bases[p, :, LANES : 2 * LANES])
-        for place, value in enumerate(times(base, plain) + times(base, near)):
+        for place, value in enumerate(times(bases[p], plain) + times(bases[p], near)):
             sums[place, p : p + 1] = jnp.sum(value, axis=0, keepdims=True)
 
-    def param(place):
-        return params[2 * place], params[2 * place + 1]
-
+    size = jnp.exp(rate[0])
+    cosine, sine = cos_sin(rate[1])
+    sine_half = cos_sin(0.5 * rate[1])[1]
+    lift = (grow(rate[0]) * cosine - 2.0 * sine_half * sine_half, size * sine)
+    norm = 1.0 / (pole[0] * pole[0] + pole[1] * pole[1])
+    inverse = (pole[0] * norm, -pole[1] * norm)
+    ratio = times(lift, inverse)
+    coef = times(read, ratio)
+    lifted = times((size * cosine, size * sine), inverse)
     total = (sums[0] * (2.0 * norm_scale), sums[1] * (2.0 * norm_scale))
     lag_total = (sums[2] * (2.0 * norm_scale), sums[3] * (2.0 * norm_scale))
-    on_read = times(total, param(RATIO))
-    on_rate = times(param(COEF), lag_total)
-    through = times(times(total, param(READ)), param(LIFTED))
+    on_read = times(total, ratio)
+    on_read = (on_read[0], -on_read[1])
+    on_rate = times(coef, lag_total)
+    through = times(times(total, read), lifted)
     on_rate = (on_rate[0] + through[0], on_rate[1] + through[1])
-    direct = times(times(total, param(COEF)), param(INVERSE))
-    step = params[2 * STEP]
+    direct = times(times(total, coef), inverse)
     on_pole = (step * on_rate[0] - direct[0], step * on_rate[1] - direct[1])
-    on_step = times(on_rate, param(RATE))[0]
-    on_decay = on_pole[0] * params[2 * POLE]
-    on_rotation = -on_pole[1]
-
-    lane = lax.broadcasted_iota(jnp.int32, (pairs, LANES), 1)
-    pair = lax.broadcasted_iota(jnp.int32, (pairs, LANES), 0)
-    even = jnp.sum(jnp.where(lane < LANES // 2, on_step, 0.0), axis=1, keepdims=True)
-    odd = jnp.sum(jnp.where(lane < LANES // 2, 0.0, on_step), axis=1, keepdims=True)
-    spread = jnp.where(lane == 2 * pair, even, jnp.where(lane == 2 * pair + 1, odd, 0.0))
-    step_row = jnp.sum(spread, axis=0, keepdims=True)
-    decay_row = jnp.sum(on_decay, axis=0, keepdims=True)
-    rotation_row = jnp.sum(on_rotation, axis=0, keepdims=True)
-    decay_row = decay_row + pltpu.roll(decay_row, LANES // 2, 1)
-    rotation_row = rotation_row + pltpu.roll(rotation_row, LANES // 2, 1)
-    state_row = jnp.where(lane[0:1] < LANES // 2, decay_row, rotation_row)
-    place = lax.broadcasted_iota(jnp.int32, (SUBLANES, LANES), 0)
-    tail = jnp.where(place == 0, step_row, jnp.where(place == 1, state_row, 0.0))
+    on_step = times(on_rate, rate)[0]
+    on_decay = jnp.sum(on_pole[0] * pole[0], axis=0, keepdims=True)
+    on_rotation = -jnp.sum(on_pole[1], axis=0, keepdims=True)
+    on_decay = on_decay + swap(on_decay)
+    on_rotation = on_rotation + swap(on_rotation)
+    state, state_exponent = scaled(jnp.where(left[0:1], on_decay, on_rotation))
+
+    lag_values, lag_exponent = scaled(lags[...])
+    lower = jnp.where(left, on_read[0], swap(on_read[1]))
+    upper = jnp.where(left, swap(on_read[0]), on_read[1])
+    grads, grad_exponent = scaled(jnp.concatenate([lower, upper], axis=0))
+    step_column = jnp.concatenate(
+        [
+            jnp.sum(jnp.where(left, on_step, 0.0), axis=1, keepdims=True),
+            jnp.sum(jnp.where(left, 0.0, on_step), axis=1, keepdims=True),
+        ],
+        axis=0,
+    )
+    step_column, step_exponent = scaled(step_column)
+    place_row = lax.broadcasted_iota(jnp.int32, (SUBLANES, LANES), 0)
+    place_lane = lax.broadcasted_iota(jnp.int32, (SUBLANES, LANES), 1)
+    device = lax.axis_index("seq") * groups + lax.axis_index("ch")
+    per_row = LANES // SUBLANES
+    aim = lax.rem(device, per_row) * SUBLANES
+    fixed = jnp.zeros((SUBLANES, LANES), jnp.float32)
+    values = two_pieces(state) + (None, None)
+    values += (lag_exponent, grad_exponent, state_exponent, step_exponent)
+    for spot, value in enumerate(values):
+        if value is not None:
+            fixed = jnp.where(place_row == spot, value, fixed)
+    tails = []
+    for group in range(groups):
+        column = step_column[group * SUBLANES : (group + 1) * SUBLANES]
+        spread = jnp.where(place_lane == place_row + aim, column, 0.0)
+        high, low = two_pieces(jnp.sum(spread, axis=0, keepdims=True))
+        tail = jnp.where(place_row == STEPS - STATE, high, fixed)
+        tails.append(jnp.where(place_row == STEPS - STATE + 1, low, tail))
     for b in range(owners):
-        sent[b, part_count : part_count + pairs] = on_read[0]
-        sent[b, part_count + pairs : 2 * part_count] = -on_read[1]
-        sent[b, 2 * part_count : 2 * part_count + SUBLANES] = tail
-
-
-def transform_tables(owners, length):
-    width = 2 * owners
-    counter = np.arange(length)
-    angles = two_pi * (counter[:, None] * counter[None, :] % length) / length
-    cosine, sine = np.cos(angles), np.sin(angles)
-    matrix = np.block([[cosine, -sine], [sine, cosine]]).astype(np.float32)
-    high = matrix.astype(jnp.bfloat16)
-    low = (matrix - high.astype(np.float32)).astype(jnp.bfloat16)
-    outer = np.arange(owners + 1)
-    angles = two_pi * (outer[:, None] * counter[None, :]) / (width * length)
-    twiddle = np.stack([np.cos(angles), -np.sin(angles)], axis=1).astype(np.float32)
-    return np.stack([high, low]), twiddle
-
-
-def sum_over(value, axis):
-    size = lax.axis_size(axis)
-    if size & (size - 1):
-        return lax.psum(value, axis)
-    reach = 1
-    while reach < size:
-        value = value + lax.ppermute(value, axis, [(i, i ^ reach) for i in range(size)])
-        reach *= 2
-    return value
+        for group in range(groups):
+            spot = b * part_count + group * SUBLANES
+            peer = b * groups + group
+            sent[peer, LAGS:GRADS] = lag_values[spot : spot + SUBLANES]
+            sent[peer, GRADS:STATE] = grads[group * SUBLANES : (group + 1) * SUBLANES]
+            sent[peer, STATE:BACK_ROWS] = tails[group]
+
+
+def unpack_kernel(got, kernel_grad, readout_grad, step_grad, state_grad):
+    peers = got.shape[0]
+    scales = [jnp.exp2(got[:, SCALES + i : SCALES + i + 1, :]) for i in range(4)]
+    channels = peers * SUBLANES
+    kernel_grad[...] = (got[:, LAGS:GRADS, :] * scales[0]).reshape(channels, LANES)
+    grads = (got[:, GRADS:STATE, :] * scales[1]).reshape(channels, LANES)
+    for spot in range(0, channels, LANES):
+        readout_grad[:, spot : spot + LANES] = grads[spot : spot + LANES].T
+
+    def whole(place, scale):
+        high, low = got[:, place : place + 1, :], got[:, place + 1 : place + 2, :]
+        return (high + low * (1.0 / 256.0)) * scale
+
+    state_grad[...] = jnp.sum(whole(STATE, scales[2]), axis=0)
+    steps = whole(STEPS, scales[3])
+    per_row = LANES // SUBLANES
+    for spot in range(0, peers, per_row):
+        lanes = slice(spot * SUBLANES, (spot + per_row) * SUBLANES)
+        step_grad[:, lanes] = jnp.sum(steps[spot : spot + per_row], axis=0)
 
 
 def kernel_device(inputs, out_grad, readout, log_step, decay_log, rotation):
-    owners = lax.axis_size("seq")
+    owners, groups = lax.axis_size("seq"), lax.axis_size("ch")
+    peers = owners * groups
     channels, length = inputs.shape
     states = decay_log.shape[0]
     part_count = channels // owners
@@ -458,71 +560,76 @@
     norm_scale = 1.0 / math.sqrt(owners * length)
     vmem = pl.BlockSpec(memory_space=pltpu.VMEM)
     memory = pltpu.CompilerParams(vmem_limit_bytes=32 * 1024 * 1024)
-
-    pieces = jnp.concatenate(
-        [a.reshape(owners, part_count, length) for a in (inputs, out_grad)], axis=1
-    )
-    got = lax.all_to_all(pieces, "seq", split_axis=0, concat_axis=0, tiled=True)
-
-    first_channel = lax.axis_index("seq") * part_count
-    own_readout = lax.dynamic_slice_in_dim(readout, first_channel, part_count, 1)
-    own_step = lax.dynamic_slice_in_dim(log_step, first_channel, part_count, 0)
-    powers, bases, params = pl.pallas_call(
-        functools.partial(table_kernel, owners, length),
-        out_shape=[
-            jax.ShapeDtypeStruct((pairs, 2 * length, 2 * LANES), jnp.bfloat16),
-            jax.ShapeDtypeStruct((pairs, owners, 2 * LANES), jnp.float32),
-            jax.ShapeDtypeStruct((16, pairs, LANES), jnp.float32),
-        ],
+    f32, bf16 = jnp.float32, jnp.bfloat16
+
+    pieces = pl.pallas_call(
+        functools.partial(pack_kernel, "seq"),
+        out_shape=jax.ShapeDtypeStruct((peers, OUT_ROWS, length), bf16),
         in_specs=[vmem] * 4,
-        out_specs=[vmem] * 3,
-        compiler_params=memory,
-        cost_estimate=pl.CostEstimate(
-            flops=pairs * length * LANES * 8, bytes_accessed=2**21, transcendentals=2**17
-        ),
-    )(
-        own_readout.reshape(2, pairs, LANES),
-        jnp.repeat(own_step.reshape(pairs, 2), states, axis=1),
-        jnp.tile(decay_log, 2)[None],
-        jnp.tile(rotation, 2)[None],
-    )
-
-    matrix, twiddle = transform_tables(owners, length)
-    sent_rows = 2 * part_count + SUBLANES
-    sent = pl.pallas_call(
-        functools.partial(main_kernel, part_count, norm_scale),
-        out_shape=jax.ShapeDtypeStruct((owners, sent_rows, LANES), jnp.float32),
-        in_specs=[vmem] * 6,
         out_specs=vmem,
         scratch_shapes=[
-            pltpu.VMEM((owners * part_count, length), jnp.float32),
-            pltpu.VMEM((4, pairs, LANES), jnp.float32),
+            pltpu.VMEM((peers * SUBLANES, LANES), f32),
+            pltpu.VMEM((2, channels, LANES), f32),
+            pltpu.VMEM((peers, OUT_ROWS, LANES), f32),
         ],
         compiler_params=memory,
-        cost_estimate=pl.CostEstimate(
-            flops=2**28, bytes_accessed=2**22, transcendentals=0
-        ),
-    )(got, jnp.asarray(matrix), jnp.asarray(twiddle), powers, bases, params)
-    back = lax.all_to_all(sent, "seq", split_axis=0, concat_axis=0, tiled=True)
-
-    kernel_grad = back[:, :part_count].reshape(channels, length)
-    readout_grad = back[:, part_count : 2 * part_count].reshape(owners, 2, pairs, LANES)
-    readout_grad = readout_grad.transpose(1, 0, 2, 3).reshape(2, channels, states)
-    step_grad = back[:, 2 * part_count, :part_count].reshape(channels)
-    state = jnp.sum(back[:, 2 * part_count + 1], axis=0).reshape(2, states)
-    return kernel_grad, readout_grad, step_grad, sum_over(state, "ch")
+    )(inputs, out_grad, readout.transpose(0, 2, 1).reshape(LANES, channels), log_step[None])
+    got = lax.all_to_all(pieces, ("seq", "ch"), split_axis=0, concat_axis=0, tiled=True)
+
+    tables = [jnp.asarray(table) for table in transform_tables(owners, length)]
+    tables = pl.pallas_call(
+        hold_kernel,
+        out_shape=[jax.ShapeDtypeStruct(table.shape, table.dtype) for table in tables],
+        in_specs=[vmem] * 2,
+        out_specs=[vmem] * 2,
+        compiler_params=memory,
+    )(*tables)
+    sent = pl.pallas_call(
+        functools.partial(main_kernel, owners, norm_scale),
+        out_shape=jax.ShapeDtypeStruct((peers, BACK_ROWS, LANES), f32),
+        in_specs=[vmem] * 5,
+        out_specs=vmem,
+        scratch_shapes=[
+            pltpu.VMEM((peers * SUBLANES, LANES), f32),
+            pltpu.VMEM((owners * part_count, length), f32),
+            pltpu.VMEM((pairs, 2 * length, 2 * LANES), bf16),
+            pltpu.VMEM((4, pairs, LANES), f32),
+        ],
+        compiler_params=memory,
+    )(got, *tables, decay_log[None], rotation[None])
+    back = lax.all_to_all(
+        sent.astype(jnp.float16), ("seq", "ch"), split_axis=0, concat_axis=0, tiled=True
+    )
+    kernel_grad, readout_grad, step_grad, state_grad = pl.pallas_call(
+        unpack_kernel,
+        out_shape=[
+            jax.ShapeDtypeStruct((channels, length), f32),
+            jax.ShapeDtypeStruct((LANES, channels), f32),
+            jax.ShapeDtypeStruct((1, channels), f32),
+            jax.ShapeDtypeStruct((1, LANES), f32),
+        ],
+        in_specs=[vmem],
+        out_specs=[vmem] * 4,
+        compiler_params=memory,
+    )(back.astype(f32))
+    return (
+        kernel_grad,
+        readout_grad.reshape(2, states, channels).transpose(0, 2, 1),
+        step_grad.reshape(channels),
+        state_grad.reshape(2, states),
+    )
 
 
 def kernel_fits(mesh, inputs, decay_log):
-    owners = mesh.shape["seq"]
-    channels = inputs.shape[0] // mesh.shape["ch"]
-    part_count = channels // owners
+    owners, groups = mesh.shape["seq"], mesh.shape["ch"]
+    channels = inputs.shape[0] // groups
     return (
         inputs.shape[1] == owners * LANES
         and 2 * decay_log.shape[0] == LANES
-        and owners in (SUBLANES, 2 * SUBLANES)
-        and part_count % (2 * SUBLANES) == 0
-        and part_count <= LANES
+        and owners == SUBLANES
+        and groups % 2 == 0
+        and channels == owners * groups * SUBLANES
+        and channels % LANES == 0
     )
 
 

time: 38.4 us -> 38.8 us (1.010)
  waiting for transfers between devices: 4.24 us -> 8.84 us
  local copies, waits for them, and re-layouts: 6.68 us -> 5.09 us
  starting transfers between devices: 8.77 us -> 7.3 us
  other arithmetic: 2.17 us -> 0.72 us
  Pallas kernels: 3.09 us -> 4.26 us
  blocking collectives: 12.3 us -> 11.4 us
    all_to_all x1, waiting for transfers between devices: 3.26 us -> 8.84 us  [kernel_device(): lax.all_to_all(pieces, ('seq', 'ch'), split_axis=0, concat_axis=0, tiled=...]
    another operation x5 -> x0, local copies, waits for them, and re-layouts: 2.12 us -> none  [the longest x2 0.74 us: kernel_device(): jnp.tile(decay_log, 2)[None]]
    concatenate x1 -> x0, other arithmetic: 1.57 us -> none  [kernel_device(): jnp.concatenate([a.reshape(owners, part_count, length) for a in (inputs,...]
    unnamed x7 -> x16, local copies, waits for them, and re-layouts: 2.43 us -> 3.93 us
    ppermute x2 -> x0, starting transfers between devices: 1.49 us -> none  [sum_over(): lax.ppermute(value, axis, [(i, i ^ reach) for i in range(size)])]
    pallas_call x2 -> x4, Pallas kernels: 3.09 us -> 4.26 us  [the longest x1 2.63 us: kernel_device(): pl.pallas_call(functools.partial(main_kernel, owners, norm_scale), out_sh...]
    ppermute x2 -> x0, waiting for transfers between devices: 0.98 us -> none  [sum_over(): lax.ppermute(value, axis, [(i, i ^ reach) for i in range(size)])]
    all_to_all x1, blocking collectives: 12.3 us -> 11.4 us  [kernel_device(): lax.all_to_all(sent.astype(jnp.float16), ('seq', 'ch'), split_axis=0, con...]
  transfers between devices with their start and end apart: 3 -> 1, of which waited for: 3 -> 1; matrix products, arithmetic and copies ran while one was open for 13% -> 0% of each run, Pallas kernels for 4% -> 0%
where the time goes in v2:
time: 38.8 us; the launch traced here: 38.3 us
  blocking collectives  11.4 us (29%)
  waiting for transfers between devices  8.84 us (23%)
  starting transfers between devices  7.3 us (19%)
  local copies, waits for them, and re-layouts  5.09 us (13%)
  Pallas kernels  4.26 us (11%)
  other arithmetic  0.72 us (2%)
  between operations  0.7 us (2%)
    all_to_all x1, blocking collectives, kernel_device(): lax.all_to_all(sent.astype(jnp.float16), ('seq', 'ch'), split_axis=0, con...  11.4 us
    all_to_all x1, waiting for transfers between devices, kernel_device(): lax.all_to_all(pieces, ('seq', 'ch'), split_axis=0, concat_axis=0, tiled=...  8.84 us
    all_to_all x1, starting transfers between devices, kernel_device(): lax.all_to_all(pieces, ('seq', 'ch'), split_axis=0, concat_axis=0, tiled=...  7.3 us
    unnamed x16, local copies, waits for them, and re-layouts  3.93 us
    pallas_call x1, Pallas kernels, kernel_device(): pl.pallas_call(functools.partial(main_kernel, owners, norm_scale), out_sh...  2.63 us
    pallas_call x1, Pallas kernels, kernel_device(): pl.pallas_call(functools.partial(pack_kernel, 'seq'), out_shape=jax.Shape...  0.84 us
  transfers between devices with their start and end apart: 1, of which 1 were waited for; matrix products, arithmetic and copies ran while one was open for 0% of the time, Pallas kernels for 0%

profile of v2, /device:TPU:0, one launch (start us, length us, event | category | flops | bytes accessed | tf_op | source)
XLA Modules:
  0.0 38.3 jit_solution(12983594953857514092)
XLA Ops:
  0.6 0.0 copy-start.5
  0.6 0.7 %copy-done.5 = f32[256]{0:T(256)S(1)} copy-done((f32[256]{0:T(256)S(1)}, f32[256]{0:T(256)}, u32[]{:S(2)}) %copy-start.5) | copy-done | bytes 1048
  1.3 0.0 copy-start.1
  1.3 0.9 %copy-done.1 = f32[2,256,64]{1,2,0:T(8,128)S(1)} copy-done((f32[2,256,64]{1,2,0:T(8,128)S(1)}, f32[2,256,64]{1,2,0:T(8,128)}, u32[]{:S(2)}) %copy-start.1) | copy-done | bytes 131096
  2.2 0.0 copy-start.2
  2.2 0.8 %copy-done.2 = bf16[256,128]{1,0:T(8,128)(2,1)S(1)} copy-done((bf16[256,128]{1,0:T(8,128)(2,1)S(1)}, bf16[256,128]{1,0:T(8,128)(2,1)}, u32[]{:S(2)}) %copy-start.2) | copy-done | bytes 65560
  3.1 0.0 copy-start.3
  3.1 0.8 %copy-done.3 = bf16[256,128]{1,0:T(8,128)(2,1)S(1)} copy-done((bf16[256,128]{1,0:T(8,128)(2,1)S(1)}, bf16[256,128]{1,0:T(8,128)(2,1)}, u32[]{:S(2)}) %copy-start.3) | copy-done | bytes 65560
  3.9 0.8 %shard_map.111 = bf16[32,24,128]{2,1,0:T(8,128)(2,1)} custom-call(bf16[256,128]{1,0:T(8,128)(2,1)S(1)} %copy-done.2, bf16[256,128]{1,0:T(8,128)(2,1)S(1)} %copy-done.3, f32[128,256]{1,0:T(8,128)S(1)} %bitcast.10, f32[1,256]{1,0:T(1,128)S(1)} %bitcast.11), custom_call_target="tpu_custom_call" | custom-call | tf_op jit(solution)/shard_map/pallas_call | solution.py:565
  4.7 0.0 copy-start
  4.7 0.0 copy-start.4
  4.7 7.3 %all-to-all-start = ((bf16[32,24,128]{2,1,0:T(8,128)(2,1)}), bf16[32,24,128]{2,1,0:T(8,128)(2,1)S(1)}, u32[]{:S(2)}, u32[]{:S(2)}) async-start(bf16[32,24,128]{2,1,0:T(8,128)(2,1)} %shard_map.111), calls=%async_computation | async-start | bytes 393216 | tf_op jit(solution)/shard_map/all_to_all | solution.py:577
  12.0 0.0 copy-done
  12.1 0.0 copy-done.4
  12.1 8.8 %all-to-all-done.got = bf16[32,24,128]{2,1,0:T(8,128)(2,1)S(1)} async-done(((bf16[32,24,128]{2,1,0:T(8,128)(2,1)}), bf16[32,24,128]{2,1,0:T(8,128)(2,1)S(1)}, u32[]{:S(2)}, u32[]{:S(2)}) %all-to-all-start) | async-done | bytes 196640 | tf_op jit(solution)/shard_map/all_to_all | solution.py:577
  20.9 0.0 copy-start.6
  20.9 0.0 copy-start.7
  20.9 0.7 %copy-done.6 = f32[64]{0:T(128)S(1)} copy-done((f32[64]{0:T(128)S(1)}, f32[64]{0:T(128)}, u32[]{:S(2)}) %copy-start.6) | copy-done | bytes 280
  21.6 0.0 copy-done.7
  21.6 2.6 %shard_map.113 = f32[32,24,128]{2,1,0:T(8,128)S(1)} custom-call(bf16[32,24,128]{2,1,0:T(8,128)(2,1)S(1)} %all-to-all-done.got, bf16[2,256,256]{2,1,0:T(8,128)(2,1)S(1)} %get-tuple-element.10.matrix, f32[9,2,128]{2,1,0:T(2,128)S(1)} %get-tuple-element.11.twiddle, f32[1,64]{1,0:T(1,128)S(1)} %bitcast.12, f32[1,64]{1,0:T(1,128)S(1)} %bitcast.13), custom_call_target="tpu_custom_call" | custom-call | tf_op jit(solution)/shard_map/pallas_call | solution.py:587
  24.3 11.4 %all_to_all.10 = f16[32,24,128]{2,1,0:T(8,128)(2,1)S(1)} all-to-all(f16[32,24,128]{2,1,0:T(8,128)(2,1)S(1)} %convert_element_type.6), channel_id=1, replica_groups=mesh['seq'=8,'ch'=4] {'seq','ch'}, dimensions={0} | all-to-all | bytes 393216 | tf_op jit(solution)/shard_map/all_to_all | solution.py:600
  35.7 0.8 %shard_map.114 = (f32[256,128]{1,0:T(8,128)}, f32[128,256]{1,0:T(8,128)}, f32[1,256]{1,0:T(1,128)}, f32[1,128]{1,0:T(1,128)S(1)}) custom-call(f32[32,24,128]{2,1,0:T(8,128)S(1)} %convert_element_type.7.got), custom_call_target="tpu_custom_call" | custom-call | tf_op jit(solution)/shard_map/pallas_call | solution.py:603
  36.5 0.5 %broadcast.3 = f32[]{:T(128)} broadcast(f32[]{:T(128)} %constant.9), dimensions={} | broadcast | bytes 8 | tf_op jit(solution)/shard_map/pallas_call | solution.py:603
  37.0 0.7 %reduce.3 = f32[128]{0:T(128)S(1)} reduce(f32[1,128]{1,0:T(1,128)S(1)} %get-tuple-element.15, f32[]{:T(128)} %broadcast.3), dimensions={0}, to_apply=%get-tuple-element.15.reduce_sub_computation.3 | reduce | bytes 1028 | tf_op jit(solution)/shard_map/pallas_call | solution.py:603
  37.7 0.6 %reshape.23 = f32[2,64]{1,0:T(2,128)} reshape(f32[128]{0:T(128)S(1)} %reduce.3) | data formatting | bytes 1024 | tf_op jit(solution)/shard_map/reshape | solution.py:619
  (3 shorter events, 0.1 us)
Async XLA Ops:
  0.6 0.7 %copy-start.5 = (f32[256]{0:T(256)S(1)}, f32[256]{0:T(256)}, u32[]{:S(2)}) copy-start(f32[256]{0:T(256)} %param.11) | copy-start | bytes 3076
  1.3 0.9 %copy-start.1 = (f32[2,256,64]{1,2,0:T(8,128)S(1)}, f32[2,256,64]{1,2,0:T(8,128)}, u32[]{:S(2)}) copy-start(f32[2,256,64]{1,2,0:T(8,128)} %param.10) | copy-start | bytes 393220
  2.2 0.8 %copy-start.2 = (bf16[256,128]{1,0:T(8,128)(2,1)S(1)}, bf16[256,128]{1,0:T(8,128)(2,1)}, u32[]{:S(2)}) copy-start(bf16[256,128]{1,0:T(8,128)(2,1)} %inputs.1) | copy-start | bytes 196612
  3.1 0.8 %copy-start.3 = (bf16[256,128]{1,0:T(8,128)(2,1)S(1)}, bf16[256,128]{1,0:T(8,128)(2,1)}, u32[]{:S(2)}) copy-start(bf16[256,128]{1,0:T(8,128)(2,1)} %out_grad.1) | copy-start | bytes 196612
  4.7 7.3 %copy-start = (bf16[2,256,256]{2,1,0:T(8,128)(2,1)S(1)}, bf16[2,256,256]{2,1,0:T(8,128)(2,1)}, u32[]{:S(2)}) copy-start(bf16[2,256,256]{2,1,0:T(8,128)(2,1)} %constant.4.clone.matrix) | copy-start | bytes 786436
  4.7 7.3 %copy-start.4 = (f32[9,2,128]{2,1,0:T(2,128)S(1)}, f32[9,2,128]{2,1,0:T(2,128)}, u32[]{:S(2)}) copy-start(f32[9,2,128]{2,1,0:T(2,128)} %constant.5.clone.twiddle) | copy-start | bytes 27652
  4.7 16.2 %all-to-all-start = ((bf16[32,24,128]{2,1,0:T(8,128)(2,1)}), bf16[32,24,128]{2,1,0:T(8,128)(2,1)S(1)}, u32[]{:S(2)}, u32[]{:S(2)}) async-start(bf16[32,24,128]{2,1,0:T(8,128)(2,1)} %shard_map.111), calls=%async_computation | async-start | bytes 393216 | tf_op jit(solution)/shard_map/all_to_all | solution.py:577
  20.9 0.7 %copy-start.6 = (f32[64]{0:T(128)S(1)}, f32[64]{0:T(128)}, u32[]{:S(2)}) copy-start(f32[64]{0:T(128)} %param.12) | copy-start | bytes 772
  20.9 0.7 %copy-start.7 = (f32[64]{0:T(128)S(1)}, f32[64]{0:T(128)}, u32[]{:S(2)}) copy-start(f32[64]{0:T(128)} %param.13) | copy-start | bytes 772

commit v3 on v2

--- a/solution.py
+++ b/solution.py
@@ -282,34 +282,46 @@
     )
 
 
-SIGNALS, READ, STEP, OUT_ROWS = 0, 16, 19, 24
-LAGS, GRADS, STATE, STEPS, SCALES, BACK_ROWS = 0, 8, 16, 18, 20, 24
-
-
-def pack_kernel(axis, inputs, out_grad, readout, log_step, out, rows, turned, peers_rows):
-    peers = out.shape[0]
-    own = lax.axis_index(axis)
-    for place, signal in enumerate((inputs, out_grad)):
-        value = signal[...].astype(jnp.float32).reshape(peers, SUBLANES, LANES)
-        peers_rows[:, SIGNALS + place * SUBLANES : SIGNALS + (place + 1) * SUBLANES] = value
-    turned[0] = transposed(readout[...])
-    turned[1] = transposed(jnp.broadcast_to(log_step[...], (LANES, log_step.shape[1])))
-    extra = []
+READ, STEP, ROWS = 16, 19, 20
+LAGS, GRADS, STATE, SINGLES = 0, 8, 16, 18
+STEP_LANES, SCALE_LANES = (0, 8), (16, 17, 18, 19)
+
+
+def pack_kernel(inputs, out_grad, readout, log_step, out, signals, read, step, turned, rows, sems):
+    peers = out.shape[0] // ROWS
+    copies = [
+        pltpu.make_async_copy(source, target, sems.at[i])
+        for i, (source, target) in enumerate(
+            ((readout, read), (log_step, step), (inputs, signals.at[0]), (out_grad, signals.at[1]))
+        )
+    ]
+    for copy in copies:
+        copy.start()
+    copies[0].wait()
+    copies[1].wait()
+    own = lax.axis_index("seq")
+    turned[0] = transposed(read[...])
+    turned[1] = transposed(jnp.broadcast_to(step[...], (LANES, step.shape[1])))
+    for place, value in enumerate(
+        three_pieces(turned[0, pl.ds(own, peers, stride=SUBLANES), :])
+    ):
+        rows[pl.ds(READ + place, peers, stride=ROWS), :] = value
+    pieces = three_pieces(turned[1, pl.ds(own, peers, stride=SUBLANES), :])
+    lane = lax.broadcasted_iota(jnp.int32, (peers, LANES), 1)
+    value = jnp.where(lane == 0, pieces[0], jnp.where(lane == 1, pieces[1], pieces[2]))
+    rows[pl.ds(STEP, peers, stride=ROWS), :] = value
     for place in range(2):
-        value = turned[place, pl.ds(own, peers, stride=SUBLANES), :]
-        extra += three_pieces(value)
-    for place, value in enumerate(extra):
-        rows[pl.ds(place, peers, stride=SUBLANES), :] = value
-    zero = jnp.zeros((peers, LANES), jnp.float32)
-    for place in range(len(extra), SUBLANES):
-        rows[pl.ds(place, peers, stride=SUBLANES), :] = zero
-    peers_rows[:, READ:OUT_ROWS] = rows[...].reshape(peers, SUBLANES, LANES)
-    out[...] = peers_rows[...].astype(jnp.bfloat16)
-
-
-def hold_kernel(matrix, twiddle, out_matrix, out_twiddle):
-    out_matrix[...] = matrix[...]
-    out_twiddle[...] = twiddle[...]
+        copies[2 + place].wait()
+        value = signals[place].astype(jnp.float32)
+        for peer in range(peers):
+            spot = peer * ROWS + place * SUBLANES
+            rows[spot : spot + SUBLANES] = value[peer * SUBLANES : (peer + 1) * SUBLANES]
+    out[...] = rows[...].astype(jnp.bfloat16)
+
+
+def hold_kernel(*refs):
+    for source, target in zip(refs[: len(refs) // 2], refs[len(refs) // 2 :]):
+        target[...] = source[...]
 
 
 def scaled(value):
@@ -324,26 +336,22 @@
 
 
 def main_kernel(
-    owners, norm_scale, got, matrix, twiddle, decay_log, rotation, sent, extra, lags, powers, sums
+    owners, norm_scale, got, matrix, twiddle, decay_log, rotation, sent, rows_in, lags, powers, sums
 ):
-    peers, length = got.shape[0], got.shape[2]
+    peers, length = got.shape[0] // ROWS, got.shape[1]
     groups = peers // owners
     part_count = groups * SUBLANES
     rows = 2 * part_count
     width = 2 * owners
     pairs = part_count // 2
     half = pairs // SUBLANES
-    got_rows = got[...].astype(jnp.float32)
-    extra[...] = got_rows[:, READ:OUT_ROWS].reshape(peers * SUBLANES, LANES)
-
-    def collect(first):
-        tiles = []
-        for group in range(groups):
-            pieces = [
-                extra[pl.ds(group * SUBLANES + first - READ + i, owners, stride=groups * SUBLANES), :]
-                for i in range(3)
-            ]
-            tiles.append(pieces[0] + pieces[1] + pieces[2])
+    rows_in[...] = got[...].astype(jnp.float32)
+
+    def collect(spot):
+        tiles = [
+            rows_in[pl.ds(group * ROWS + spot, owners, stride=groups * ROWS), :]
+            for group in range(groups)
+        ]
         return jnp.concatenate(tiles[:half], axis=0), jnp.concatenate(tiles[half:], axis=0)
 
     lane = lax.broadcasted_iota(jnp.int32, (pairs, LANES), 1)
@@ -352,9 +360,11 @@
     def swap(value):
         return pltpu.roll(value, LANES // 2, 1)
 
-    lower, upper = collect(READ)
+    lower, upper = [sum(side) for side in zip(*(collect(READ + i) for i in range(3)))]
     read = (jnp.where(left, lower, swap(upper)), jnp.where(left, swap(lower), upper))
-    lower, upper = collect(STEP)
+    lower, upper = [
+        sum(side[:, i : i + 1] for i in range(3)) + jnp.zeros_like(side) for side in collect(STEP)
+    ]
     step = jnp.exp(jnp.where(left, lower, upper))
     decay_row = jnp.concatenate([decay_log[...], decay_log[...]], axis=1)
     rotation_row = jnp.concatenate([rotation[...], rotation[...]], axis=1)
@@ -393,11 +403,13 @@
 
     blocks = []
     for s in range(owners):
-        mine = got_rows[s * groups : (s + 1) * groups]
+        spots = [(s * groups + group) * ROWS for group in range(groups)]
         blocks.append(
             jnp.concatenate(
-                [mine[:, :SUBLANES], mine[:, SUBLANES : 2 * SUBLANES]], axis=0
-            ).reshape(rows, length)
+                [rows_in[spot : spot + SUBLANES] for spot in spots]
+                + [rows_in[spot + SUBLANES : spot + 2 * SUBLANES] for spot in spots],
+                axis=0,
+            )
         )
     spectra = []
     for k in range(owners + 1):
@@ -504,50 +516,58 @@
     step_column, step_exponent = scaled(step_column)
     place_row = lax.broadcasted_iota(jnp.int32, (SUBLANES, LANES), 0)
     place_lane = lax.broadcasted_iota(jnp.int32, (SUBLANES, LANES), 1)
-    device = lax.axis_index("seq") * groups + lax.axis_index("ch")
-    per_row = LANES // SUBLANES
-    aim = lax.rem(device, per_row) * SUBLANES
-    fixed = jnp.zeros((SUBLANES, LANES), jnp.float32)
-    values = two_pieces(state) + (None, None)
-    values += (lag_exponent, grad_exponent, state_exponent, step_exponent)
-    for spot, value in enumerate(values):
-        if value is not None:
-            fixed = jnp.where(place_row == spot, value, fixed)
+    scales = jnp.zeros((1, LANES), jnp.float32)
+    for spot, value in zip(
+        SCALE_LANES, (lag_exponent, grad_exponent, state_exponent, step_exponent)
+    ):
+        scales = jnp.where(place_lane[0:1] == spot, value, scales)
+    state_high, state_low = two_pieces(state)
     tails = []
     for group in range(groups):
-        column = step_column[group * SUBLANES : (group + 1) * SUBLANES]
-        spread = jnp.where(place_lane == place_row + aim, column, 0.0)
-        high, low = two_pieces(jnp.sum(spread, axis=0, keepdims=True))
-        tail = jnp.where(place_row == STEPS - STATE, high, fixed)
-        tails.append(jnp.where(place_row == STEPS - STATE + 1, low, tail))
+        pieces = two_pieces(step_column[group * SUBLANES : (group + 1) * SUBLANES])
+        spread = jnp.zeros((SUBLANES, LANES), jnp.float32)
+        for spot, piece in zip(STEP_LANES, pieces):
+            spread = jnp.where(place_lane == place_row + spot, piece, spread)
+        singles = scales + jnp.sum(spread, axis=0, keepdims=True)
+        tails.append(jnp.concatenate([state_high, state_low, singles, singles], axis=0))
     for b in range(owners):
         for group in range(groups):
             spot = b * part_count + group * SUBLANES
-            peer = b * groups + group
-            sent[peer, LAGS:GRADS] = lag_values[spot : spot + SUBLANES]
-            sent[peer, GRADS:STATE] = grads[group * SUBLANES : (group + 1) * SUBLANES]
-            sent[peer, STATE:BACK_ROWS] = tails[group]
-
-
-def unpack_kernel(got, kernel_grad, readout_grad, step_grad, state_grad):
-    peers = got.shape[0]
-    scales = [jnp.exp2(got[:, SCALES + i : SCALES + i + 1, :]) for i in range(4)]
-    channels = peers * SUBLANES
-    kernel_grad[...] = (got[:, LAGS:GRADS, :] * scales[0]).reshape(channels, LANES)
-    grads = (got[:, GRADS:STATE, :] * scales[1]).reshape(channels, LANES)
-    for spot in range(0, channels, LANES):
+            place = (b * groups + group) * ROWS
+            sent[place + LAGS : place + GRADS] = lag_values[spot : spot + SUBLANES]
+            sent[place + GRADS : place + STATE] = grads[group * SUBLANES : (group + 1) * SUBLANES]
+            sent[place + STATE : place + ROWS] = tails[group]
+
+
+def unpack_kernel(got, kernel_grad, readout_grad, step_grad, state_grad, grads):
+    peers = got.shape[0] // ROWS
+    singles = got[pl.ds(SINGLES, peers, stride=ROWS), :]
+    scales = [jnp.exp2(singles[:, spot : spot + 1]) for spot in SCALE_LANES]
+    for peer in range(peers):
+        spot = peer * ROWS
+        lanes = slice(peer * SUBLANES, (peer + 1) * SUBLANES)
+        kernel_grad[lanes] = got[spot + LAGS : spot + GRADS] * scales[0][peer : peer + 1]
+        grads[lanes] = got[spot + GRADS : spot + STATE] * scales[1][peer : peer + 1]
+    for spot in range(0, peers * SUBLANES, LANES):
         readout_grad[:, spot : spot + LANES] = grads[spot : spot + LANES].T
-
-    def whole(place, scale):
-        high, low = got[:, place : place + 1, :], got[:, place + 1 : place + 2, :]
-        return (high + low * (1.0 / 256.0)) * scale
-
-    state_grad[...] = jnp.sum(whole(STATE, scales[2]), axis=0)
-    steps = whole(STEPS, scales[3])
+    high = got[pl.ds(STATE, peers, stride=ROWS), :]
+    low = got[pl.ds(STATE + 1, peers, stride=ROWS), :]
+    state = jnp.sum((high + low * (1.0 / 256.0)) * scales[2], axis=0, keepdims=True)
+    states = state_grad.shape[1]
+    state_grad[0:1] = state[:, :states]
+    state_grad[1:2] = state[:, states:]
     per_row = LANES // SUBLANES
+    lane = lax.broadcasted_iota(jnp.int32, (peers, LANES), 1)
+    row = lax.broadcasted_iota(jnp.int32, (peers, LANES), 0)
+    steps = pltpu.roll(singles, LANES - STEP_LANES[1], 1) * (1.0 / 256.0) + singles
+    steps = jnp.where(lane < SUBLANES, steps * scales[3], 0.0)
+    reach = SUBLANES
+    while reach < LANES:
+        steps = steps + pltpu.roll(steps, reach, 1)
+        reach *= 2
     for spot in range(0, peers, per_row):
-        lanes = slice(spot * SUBLANES, (spot + per_row) * SUBLANES)
-        step_grad[:, lanes] = jnp.sum(steps[spot : spot + per_row], axis=0)
+        mine = jnp.where(row - spot == lane // SUBLANES, steps, 0.0)
+        step_grad[spot * SUBLANES : (spot + per_row) * SUBLANES] = jnp.sum(mine, axis=0)
 
 
 def kernel_device(inputs, out_grad, readout, log_step, decay_log, rotation):
@@ -562,62 +582,67 @@
     memory = pltpu.CompilerParams(vmem_limit_bytes=32 * 1024 * 1024)
     f32, bf16 = jnp.float32, jnp.bfloat16
 
+    def exchange(value):
+        value = value.reshape(peers, ROWS // 2, 2, LANES)
+        value = lax.all_to_all(value, ("seq", "ch"), split_axis=0, concat_axis=0, tiled=True)
+        return value.reshape(peers * ROWS, LANES)
+
+    anywhere = pl.BlockSpec(memory_space=pl.ANY)
     pieces = pl.pallas_call(
-        functools.partial(pack_kernel, "seq"),
-        out_shape=jax.ShapeDtypeStruct((peers, OUT_ROWS, length), bf16),
-        in_specs=[vmem] * 4,
+        pack_kernel,
+        out_shape=jax.ShapeDtypeStruct((peers * ROWS, LANES), bf16),
+        in_specs=[anywhere] * 4,
         out_specs=vmem,
         scratch_shapes=[
-            pltpu.VMEM((peers * SUBLANES, LANES), f32),
+            pltpu.VMEM((2, channels, LANES), bf16),
+            pltpu.VMEM((LANES, channels), f32),
+            pltpu.VMEM((1, channels), f32),
             pltpu.VMEM((2, channels, LANES), f32),
-            pltpu.VMEM((peers, OUT_ROWS, LANES), f32),
+            pltpu.VMEM((peers * ROWS, LANES), f32),
+            pltpu.SemaphoreType.DMA((4,)),
         ],
         compiler_params=memory,
     )(inputs, out_grad, readout.transpose(0, 2, 1).reshape(LANES, channels), log_step[None])
-    got = lax.all_to_all(pieces, ("seq", "ch"), split_axis=0, concat_axis=0, tiled=True)
-
-    tables = [jnp.asarray(table) for table in transform_tables(owners, length)]
-    tables = pl.pallas_call(
+    got = exchange(pieces)
+
+    held = [jnp.asarray(table) for table in transform_tables(owners, length)]
+    held += [decay_log[None], rotation[None]]
+    held = pl.pallas_call(
         hold_kernel,
-        out_shape=[jax.ShapeDtypeStruct(table.shape, table.dtype) for table in tables],
-        in_specs=[vmem] * 2,
-        out_specs=[vmem] * 2,
+        out_shape=[jax.ShapeDtypeStruct(value.shape, value.dtype) for value in held],
+        in_specs=[vmem] * 4,
+        out_specs=[vmem] * 4,
         compiler_params=memory,
-    )(*tables)
+    )(*held)
     sent = pl.pallas_call(
         functools.partial(main_kernel, owners, norm_scale),
-        out_shape=jax.ShapeDtypeStruct((peers, BACK_ROWS, LANES), f32),
+        out_shape=jax.ShapeDtypeStruct((peers * ROWS, LANES), f32),
         in_specs=[vmem] * 5,
         out_specs=vmem,
         scratch_shapes=[
-            pltpu.VMEM((peers * SUBLANES, LANES), f32),
+            pltpu.VMEM((peers * ROWS, LANES), f32),
             pltpu.VMEM((owners * part_count, length), f32),
             pltpu.VMEM((pairs, 2 * length, 2 * LANES), bf16),
             pltpu.VMEM((4, pairs, LANES), f32),
         ],
         compiler_params=memory,
-    )(got, *tables, decay_log[None], rotation[None])
-    back = lax.all_to_all(
-        sent.astype(jnp.float16), ("seq", "ch"), split_axis=0, concat_axis=0, tiled=True
-    )
+    )(got, *held)
+    back = exchange(sent.astype(jnp.float16))
     kernel_grad, readout_grad, step_grad, state_grad = pl.pallas_call(
         unpack_kernel,
         out_shape=[
             jax.ShapeDtypeStruct((channels, length), f32),
             jax.ShapeDtypeStruct((LANES, channels), f32),
-            jax.ShapeDtypeStruct((1, channels), f32),
-            jax.ShapeDtypeStruct((1, LANES), f32),
+            jax.ShapeDtypeStruct((channels,), f32),
+            jax.ShapeDtypeStruct((2, states), f32),
         ],
         in_specs=[vmem],
         out_specs=[vmem] * 4,
+        scratch_shapes=[pltpu.VMEM((channels, LANES), f32)],
         compiler_params=memory,
     )(back.astype(f32))
-    return (
-        kernel_grad,
-        readout_grad.reshape(2, states, channels).transpose(0, 2, 1),
-        step_grad.reshape(channels),
-        state_grad.reshape(2, states),
-    )
+    readout_grad = readout_grad.reshape(2, states, channels).transpose(0, 2, 1)
+    return kernel_grad, readout_grad, step_grad, state_grad
 
 
 def kernel_fits(mesh, inputs, decay_log):

time: 38.8 us -> 35.8 us (0.923)
  local copies, waits for them, and re-layouts: 5.09 us -> 3.91 us
  waiting for transfers between devices: 8.84 us -> 7.88 us
  blocking collectives: 11.4 us -> 10.7 us
  other arithmetic: 0.72 us -> 0.05 us
  Pallas kernels: 4.26 us -> 4.89 us
    all_to_all x1, waiting for transfers between devices: 8.84 us -> 7.88 us  [exchange(): lax.all_to_all(value, ('seq', 'ch'), split_axis=0, concat_axis=0, tiled=T...]
    all_to_all x1, blocking collectives: 11.4 us -> 10.7 us  [exchange(): lax.all_to_all(value, ('seq', 'ch'), split_axis=0, concat_axis=0, tiled=T...]
    pallas_call x1 -> x0, other arithmetic: 0.66 us -> none  [kernel_device(): pl.pallas_call(unpack_kernel, out_shape=[jax.ShapeDtypeStruct((channels,...]
    reshape x1 -> x0, local copies, waits for them, and re-layouts: 0.65 us -> none  [kernel_device(): state_grad.reshape(2, states)]
    pallas_call x1 -> x0, local copies, waits for them, and re-layouts: 0.51 us -> none  [kernel_device(): pl.pallas_call(unpack_kernel, out_shape=[jax.ShapeDtypeStruct((channels,...]
where the time goes in v3:
time: 35.8 us; the launch traced here: 35.5 us
  blocking collectives  10.7 us (30%)
  waiting for transfers between devices  7.88 us (22%)
  starting transfers between devices  7.3 us (20%)
  Pallas kernels  4.89 us (14%)
  local copies, waits for them, and re-layouts  3.91 us (11%)
  between operations  0.73 us (2%)
    all_to_all x1, blocking collectives, exchange(): lax.all_to_all(value, ('seq', 'ch'), split_axis=0, concat_axis=0, tiled=T...  10.7 us
    all_to_all x1, waiting for transfers between devices, exchange(): lax.all_to_all(value, ('seq', 'ch'), split_axis=0, concat_axis=0, tiled=T...  7.88 us
    all_to_all x1, starting transfers between devices, exchange(): lax.all_to_all(value, ('seq', 'ch'), split_axis=0, concat_axis=0, tiled=T...  7.3 us
    unnamed x16, local copies, waits for them, and re-layouts  3.91 us
    pallas_call x1, Pallas kernels, kernel_device(): pl.pallas_call(functools.partial(main_kernel, owners, norm_scale), out_sh...  2.59 us
    pallas_call x1, Pallas kernels, kernel_device(): pl.pallas_call(pack_kernel, out_shape=jax.ShapeDtypeStruct((peers * ROWS,...  1.19 us
    pallas_call x1, Pallas kernels, kernel_device(): pl.pallas_call(unpack_kernel, out_shape=[jax.ShapeDtypeStruct((channels,...  1.09 us
  transfers between devices with their start and end apart: 1, of which 1 were waited for; matrix products, arithmetic and copies ran while one was open for 0% of the time, Pallas kernels for 0%

profile of v3, /device:TPU:0, one launch (start us, length us, event | category | flops | bytes accessed | tf_op | source)
XLA Modules:
  0.0 35.5 jit_solution(1145745176933904615)
XLA Ops:
  0.6 0.0 copy-start.5
  0.6 0.7 %copy-done.5 = f32[256]{0:T(256)S(1)} copy-done((f32[256]{0:T(256)S(1)}, f32[256]{0:T(256)}, u32[]{:S(2)}) %copy-start.5) | copy-done | bytes 1048
  1.3 0.0 copy-start.1
  1.3 0.9 %copy-done.1 = f32[2,256,64]{1,2,0:T(8,128)S(1)} copy-done((f32[2,256,64]{1,2,0:T(8,128)S(1)}, f32[2,256,64]{1,2,0:T(8,128)}, u32[]{:S(2)}) %copy-start.1) | copy-done | bytes 131096
  2.2 0.0 copy-start.2
  2.2 0.8 %copy-done.2 = bf16[256,128]{1,0:T(8,128)(2,1)S(1)} copy-done((bf16[256,128]{1,0:T(8,128)(2,1)S(1)}, bf16[256,128]{1,0:T(8,128)(2,1)}, u32[]{:S(2)}) %copy-start.2) | copy-done | bytes 65560
  3.1 0.0 copy-start.3
  3.1 0.8 %copy-done.3 = bf16[256,128]{1,0:T(8,128)(2,1)S(1)} copy-done((bf16[256,128]{1,0:T(8,128)(2,1)S(1)}, bf16[256,128]{1,0:T(8,128)(2,1)}, u32[]{:S(2)}) %copy-start.3) | copy-done | bytes 65560
  3.9 1.2 %shard_map.111 = bf16[640,128]{1,0:T(8,128)(2,1)} custom-call(bf16[256,128]{1,0:T(8,128)(2,1)S(1)} %copy-done.2, bf16[256,128]{1,0:T(8,128)(2,1)S(1)} %copy-done.3, f32[128,256]{1,0:T(8,128)S(1)} %bitcast.15, f32[1,256]{1,0:T(1,128)S(1)} %bitcast.16), custom_call_target="tpu_custom_call" | custom-call | tf_op jit(solution)/shard_map/pallas_call | solution.py:591
  5.1 0.0 copy-start
  5.1 0.0 copy-start.4
  5.1 7.3 %all-to-all-start = ((bf16[32,10,2,128]{3,2,1,0:T(2,128)(2,1)}), bf16[32,10,2,128]{3,2,1,0:T(2,128)(2,1)S(1)}, u32[]{:S(2)}, u32[]{:S(2)}) async-start(bf16[32,10,2,128]{3,2,1,0:T(2,128)(2,1)} %bitcast.3), calls=%async_computation | async-start | bytes 327680 | tf_op jit(solution)/shard_map/all_to_all | solution.py:587
  12.4 0.0 copy-start.6
  12.4 0.0 copy-start.7
  12.5 0.0 copy-done
  12.5 0.0 copy-done.4
  12.5 0.6 %copy-done.6 = f32[64]{0:T(128)S(1)} copy-done((f32[64]{0:T(128)S(1)}, f32[64]{0:T(128)}, u32[]{:S(2)}) %copy-start.6) | copy-done | bytes 280
  13.1 0.0 copy-done.7
  13.1 7.9 %all-to-all-done = bf16[32,10,2,128]{3,2,1,0:T(2,128)(2,1)S(1)} async-done(((bf16[32,10,2,128]{3,2,1,0:T(2,128)(2,1)}), bf16[32,10,2,128]{3,2,1,0:T(2,128)(2,1)S(1)}, u32[]{:S(2)}, u32[]{:S(2)}) %all-to-all-start) | async-done | bytes 163872 | tf_op jit(solution)/shard_map/all_to_all | solution.py:587
  21.0 2.6 %shard_map.113 = f32[640,128]{1,0:T(8,128)S(1)} custom-call(bf16[640,128]{1,0:T(8,128)(2,1)S(1)} %bitcast.14, bf16[2,256,256]{2,1,0:T(8,128)(2,1)S(1)} %get-tuple-element.12.matrix, f32[9,2,128]{2,1,0:T(2,128)S(1)} %get-tuple-element.13.twiddle, f32[1,64]{1,0:T(1,128)S(1)} %get-tuple-element.14.decay_log, f32[1,64]{1,0:T(1,128)S(1)} %get-tuple-element.15.rotation), custom_call_target="tpu_custom_call" | custom-call | tf_op jit(solution)/shard_map/pallas_call | solution.py:617
  23.6 10.7 %all_to_all.10 = f16[32,10,2,128]{3,2,1,0:T(2,128)(2,1)S(1)} all-to-all(f16[32,10,2,128]{3,2,1,0:T(2,128)(2,1)S(1)} %bitcast.19), channel_id=1, replica_groups=mesh['seq'=8,'ch'=4] {'seq','ch'}, dimensions={0} | all-to-all | bytes 327680 | tf_op jit(solution)/shard_map/all_to_all | solution.py:587
  34.4 1.1 %shard_map.114 = (f32[256,128]{1,0:T(8,128)}, f32[128,256]{1,0:T(8,128)}, f32[256]{0:T(256)}, f32[2,64]{1,0:T(2,128)}) custom-call(f32[640,128]{1,0:T(8,128)S(1)} %convert.1.got), custom_call_target="tpu_custom_call" | custom-call | tf_op jit(solution)/shard_map/pallas_call | solution.py:631
  (3 shorter events, 0.1 us)
Async XLA Ops:
  0.6 0.7 %copy-start.5 = (f32[256]{0:T(256)S(1)}, f32[256]{0:T(256)}, u32[]{:S(2)}) copy-start(f32[256]{0:T(256)} %param.11) | copy-start | bytes 3076
  1.3 0.9 %copy-start.1 = (f32[2,256,64]{1,2,0:T(8,128)S(1)}, f32[2,256,64]{1,2,0:T(8,128)}, u32[]{:S(2)}) copy-start(f32[2,256,64]{1,2,0:T(8,128)} %param.10) | copy-start | bytes 393220
  2.2 0.8 %copy-start.2 = (bf16[256,128]{1,0:T(8,128)(2,1)S(1)}, bf16[256,128]{1,0:T(8,128)(2,1)}, u32[]{:S(2)}) copy-start(bf16[256,128]{1,0:T(8,128)(2,1)} %inputs.1) | copy-start | bytes 196612
  3.1 0.8 %copy-start.3 = (bf16[256,128]{1,0:T(8,128)(2,1)S(1)}, bf16[256,128]{1,0:T(8,128)(2,1)}, u32[]{:S(2)}) copy-start(bf16[256,128]{1,0:T(8,128)(2,1)} %out_grad.1) | copy-start | bytes 196612
  5.1 7.4 %copy-start = (bf16[2,256,256]{2,1,0:T(8,128)(2,1)S(1)}, bf16[2,256,256]{2,1,0:T(8,128)(2,1)}, u32[]{:S(2)}) copy-start(bf16[2,256,256]{2,1,0:T(8,128)(2,1)} %constant.4.clone.refs_0_) | copy-start | bytes 786436
  5.1 7.4 %copy-start.4 = (f32[9,2,128]{2,1,0:T(2,128)S(1)}, f32[9,2,128]{2,1,0:T(2,128)}, u32[]{:S(2)}) copy-start(f32[9,2,128]{2,1,0:T(2,128)} %constant.5.clone.refs_1_) | copy-start | bytes 27652
  5.1 15.9 %all-to-all-start = ((bf16[32,10,2,128]{3,2,1,0:T(2,128)(2,1)}), bf16[32,10,2,128]{3,2,1,0:T(2,128)(2,1)S(1)}, u32[]{:S(2)}, u32[]{:S(2)}) async-start(bf16[32,10,2,128]{3,2,1,0:T(2,128)(2,1)} %bitcast.3), calls=%async_computation | async-start | bytes 327680 | tf_op jit(solution)/shard_map/all_to_all | solution.py:587
  12.4 0.7 %copy-start.6 = (f32[64]{0:T(128)S(1)}, f32[64]{0:T(128)}, u32[]{:S(2)}) copy-start(f32[64]{0:T(128)} %param.12) | copy-start | bytes 772
  12.4 0.7 %copy-start.7 = (f32[64]{0:T(128)S(1)}, f32[64]{0:T(128)}, u32[]{:S(2)}) copy-start(f32[64]{0:T(128)} %param.13) | copy-start | bytes 772

commit v4 on v3

--- a/solution.py
+++ b/solution.py
@@ -601,7 +601,7 @@
             pltpu.VMEM((peers * ROWS, LANES), f32),
             pltpu.SemaphoreType.DMA((4,)),
         ],
-        compiler_params=memory,
+        compiler_params=pltpu.CompilerParams(vmem_limit_bytes=60 * 1024 * 1024),
     )(inputs, out_grad, readout.transpose(0, 2, 1).reshape(LANES, channels), log_step[None])
     got = exchange(pieces)
 

time: 35.8 us -> 33 us (0.922)
  local copies, waits for them, and re-layouts: 3.91 us -> 0.65 us
  Pallas kernels: 4.89 us -> 5.48 us
    unnamed x16 -> x8, local copies, waits for them, and re-layouts: 3.91 us -> 0.65 us
    pallas_call x1, Pallas kernels: 1.19 us -> 1.78 us  [kernel_device(): pl.pallas_call(pack_kernel, out_shape=jax.ShapeDtypeStruct((peers * ROWS,...]
where the time goes in v4:
time: 33 us; the launch traced here: 32.8 us
  blocking collectives  10.7 us (32%)
  waiting for transfers between devices  7.88 us (24%)
  starting transfers between devices  7.3 us (22%)
  Pallas kernels  5.48 us (17%)
  between operations  0.72 us (2%)
  local copies, waits for them, and re-layouts  0.65 us (2%)
    all_to_all x1, blocking collectives, exchange(): lax.all_to_all(value, ('seq', 'ch'), split_axis=0, concat_axis=0, tiled=T...  10.7 us
    all_to_all x1, waiting for transfers between devices, exchange(): lax.all_to_all(value, ('seq', 'ch'), split_axis=0, concat_axis=0, tiled=T...  7.88 us
    all_to_all x1, starting transfers between devices, exchange(): lax.all_to_all(value, ('seq', 'ch'), split_axis=0, concat_axis=0, tiled=T...  7.3 us
    pallas_call x1, Pallas kernels, kernel_device(): pl.pallas_call(functools.partial(main_kernel, owners, norm_scale), out_sh...  2.58 us
    pallas_call x1, Pallas kernels, kernel_device(): pl.pallas_call(pack_kernel, out_shape=jax.ShapeDtypeStruct((peers * ROWS,...  1.78 us
    pallas_call x1, Pallas kernels, kernel_device(): pl.pallas_call(unpack_kernel, out_shape=[jax.ShapeDtypeStruct((channels,...  1.09 us
  transfers between devices with their start and end apart: 1, of which 1 were waited for; matrix products, arithmetic and copies ran while one was open for 0% of the time, Pallas kernels for 0%

profile of v4, /device:TPU:0, one launch (start us, length us, event | category | flops | bytes accessed | tf_op | source)
XLA Modules:
  0.0 32.8 jit_solution(17823816677132902836)
XLA Ops:
  0.6 1.8 %shard_map.111 = bf16[640,128]{1,0:T(8,128)(2,1)} custom-call(bf16[256,128]{1,0:T(8,128)(2,1)} %inputs.1, bf16[256,128]{1,0:T(8,128)(2,1)} %out_grad.1, f32[128,256]{1,0:T(8,128)} %bitcast.20, f32[1,256]{1,0:T(1,128)} %bitcast.21), custom_call_target="tpu_custom_call" | custom-call | tf_op jit(solution)/shard_map/pallas_call | solution.py:591
  2.4 0.0 copy-start
  2.4 0.0 copy-start.1
  2.4 7.3 %all-to-all-start = ((bf16[32,10,2,128]{3,2,1,0:T(2,128)(2,1)}), bf16[32,10,2,128]{3,2,1,0:T(2,128)(2,1)S(1)}, u32[]{:S(2)}, u32[]{:S(2)}) async-start(bf16[32,10,2,128]{3,2,1,0:T(2,128)(2,1)} %bitcast.17), calls=%async_computation | async-start | bytes 327680 | tf_op jit(solution)/shard_map/all_to_all | solution.py:587
  9.8 0.0 copy-start.2
  9.8 0.0 copy-start.3
  9.8 0.0 copy-done
  9.8 0.0 copy-done.1
  9.8 0.6 %copy-done.2 = f32[64]{0:T(128)S(1)} copy-done((f32[64]{0:T(128)S(1)}, f32[64]{0:T(128)}, u32[]{:S(2)}) %copy-start.2) | copy-done | bytes 280
  10.4 0.0 copy-done.3
  10.5 7.9 %all-to-all-done = bf16[32,10,2,128]{3,2,1,0:T(2,128)(2,1)S(1)} async-done(((bf16[32,10,2,128]{3,2,1,0:T(2,128)(2,1)}), bf16[32,10,2,128]{3,2,1,0:T(2,128)(2,1)S(1)}, u32[]{:S(2)}, u32[]{:S(2)}) %all-to-all-start) | async-done | bytes 163872 | tf_op jit(solution)/shard_map/all_to_all | solution.py:587
  18.3 2.6 %shard_map.113 = f32[640,128]{1,0:T(8,128)S(1)} custom-call(bf16[640,128]{1,0:T(8,128)(2,1)S(1)} %bitcast.14, bf16[2,256,256]{2,1,0:T(8,128)(2,1)S(1)} %get-tuple-element.12.matrix, f32[9,2,128]{2,1,0:T(2,128)S(1)} %get-tuple-element.13.twiddle, f32[1,64]{1,0:T(1,128)S(1)} %get-tuple-element.14.decay_log, f32[1,64]{1,0:T(1,128)S(1)} %get-tuple-element.15.rotation), custom_call_target="tpu_custom_call" | custom-call | tf_op jit(solution)/shard_map/pallas_call | solution.py:617
  21.0 10.7 %all_to_all.10 = f16[32,10,2,128]{3,2,1,0:T(2,128)(2,1)S(1)} all-to-all(f16[32,10,2,128]{3,2,1,0:T(2,128)(2,1)S(1)} %bitcast.18), channel_id=1, replica_groups=mesh['seq'=8,'ch'=4] {'seq','ch'}, dimensions={0} | all-to-all | bytes 327680 | tf_op jit(solution)/shard_map/all_to_all | solution.py:587
  31.7 1.1 %shard_map.114 = (f32[256,128]{1,0:T(8,128)}, f32[128,256]{1,0:T(8,128)}, f32[256]{0:T(256)}, f32[2,64]{1,0:T(2,128)}) custom-call(f32[640,128]{1,0:T(8,128)S(1)} %convert.1.got), custom_call_target="tpu_custom_call" | custom-call | tf_op jit(solution)/shard_map/pallas_call | solution.py:631
  (3 shorter events, 0.1 us)
Async XLA Ops:
  2.4 7.4 %copy-start = (bf16[2,256,256]{2,1,0:T(8,128)(2,1)S(1)}, bf16[2,256,256]{2,1,0:T(8,128)(2,1)}, u32[]{:S(2)}) copy-start(bf16[2,256,256]{2,1,0:T(8,128)(2,1)} %constant.4.clone.refs_0_) | copy-start | bytes 786436
  2.4 7.4 %copy-start.1 = (f32[9,2,128]{2,1,0:T(2,128)S(1)}, f32[9,2,128]{2,1,0:T(2,128)}, u32[]{:S(2)}) copy-start(f32[9,2,128]{2,1,0:T(2,128)} %constant.5.clone.refs_1_) | copy-start | bytes 27652
  2.4 15.9 %all-to-all-start = ((bf16[32,10,2,128]{3,2,1,0:T(2,128)(2,1)}), bf16[32,10,2,128]{3,2,1,0:T(2,128)(2,1)S(1)}, u32[]{:S(2)}, u32[]{:S(2)}) async-start(bf16[32,10,2,128]{3,2,1,0:T(2,128)(2,1)} %bitcast.17), calls=%async_computation | async-start | bytes 327680 | tf_op jit(solution)/shard_map/all_to_all | solution.py:587
  9.8 0.7 %copy-start.2 = (f32[64]{0:T(128)S(1)}, f32[64]{0:T(128)}, u32[]{:S(2)}) copy-start(f32[64]{0:T(128)} %param.12) | copy-start | bytes 772
  9.8 0.7 %copy-start.3 = (f32[64]{0:T(128)S(1)}, f32[64]{0:T(128)}, u32[]{:S(2)}) copy-start(f32[64]{0:T(128)} %param.13) | copy-start | bytes 772

commit v5 on v4

--- a/solution.py
+++ b/solution.py
@@ -229,22 +229,61 @@
     )
 
 
-def weighted_sum(terms):
-    total = None
-    for weight, value in terms:
-        if abs(weight) < 1e-12:
-            continue
-        if abs(abs(weight) - 1.0) < 1e-12:
-            term = value if weight > 0 else -value
-        else:
-            term = value * weight
-        total = term if total is None else total + term
-    return total
-
-
-def turn(count, width):
-    angle = two_pi * (count % width) / width
-    return math.cos(angle), math.sin(angle)
+def blocks_forward(x):
+    root = math.sqrt(0.5)
+    cosine, sine = math.cos(math.pi / 8), math.sin(math.pi / 8)
+    total = [x[s] + x[s + 4] for s in range(4)]
+    gap = [x[s] - x[s + 4] for s in range(4)]
+    even, odd = total[0] + total[2], total[1] + total[3]
+    real, imag = [None] * 9, [None] * 9
+    real[0], real[8] = even + odd, even - odd
+    imag[0] = imag[8] = jnp.zeros_like(even)
+    real[4], imag[4] = total[0] - total[2], total[3] - total[1]
+    less, more = root * (gap[1] - gap[3]), root * (gap[1] + gap[3])
+    real[2], imag[2] = gap[0] + less, -gap[2] - more
+    real[6], imag[6] = gap[0] - less, gap[2] - more
+    less, more = root * (x[2] - x[6]), root * (x[2] + x[6])
+    even1 = (x[0] + less, -x[4] - more)
+    even3 = (x[0] - less, x[4] - more)
+    p, q, r, t = x[1] - x[7], x[3] - x[5], x[1] + x[7], x[3] + x[5]
+    odd1 = (cosine * p + sine * q, -sine * r - cosine * t)
+    odd3 = (sine * p - cosine * q, sine * t - cosine * r)
+    real[1], imag[1] = even1[0] + odd1[0], even1[1] + odd1[1]
+    real[7], imag[7] = even1[0] - odd1[0], odd1[1] - even1[1]
+    real[3], imag[3] = even3[0] + odd3[0], even3[1] + odd3[1]
+    real[5], imag[5] = even3[0] - odd3[0], odd3[1] - even3[1]
+    return list(zip(real, imag))
+
+
+def blocks_back(z):
+    root = math.sqrt(0.5)
+    cosine, sine = math.cos(math.pi / 8), math.sin(math.pi / 8)
+    real, imag = [v[0] for v in z], [v[1] for v in z]
+    even, odd = real[0] + real[8], real[0] - real[8]
+    total = [even + real[4], odd + imag[4], even - real[4], odd - imag[4]]
+    less, more = root * (real[2] - real[6]), root * (imag[2] + imag[6])
+    gap = [real[2] + real[6], less + more, imag[2] - imag[6], more - less]
+    x = [total[s] + gap[s] for s in range(4)] + [total[s] - gap[s] for s in range(4)]
+    even1 = (real[1] + real[7], imag[7] - imag[1])
+    even3 = (real[3] + real[5], imag[5] - imag[3])
+    odd1 = (real[1] - real[7], imag[1] + imag[7])
+    odd3 = (real[3] - real[5], imag[3] + imag[5])
+    less, more = root * (even1[0] - even3[0]), root * (even1[1] + even3[1])
+    p = cosine * odd1[0] + sine * odd3[0]
+    q = sine * odd1[0] - cosine * odd3[0]
+    r = sine * odd1[1] + cosine * odd3[1]
+    t = cosine * odd1[1] - sine * odd3[1]
+    extra = [
+        even1[0] + even3[0],
+        p + r,
+        less - more,
+        q + t,
+        even3[1] - even1[1],
+        t - q,
+        -less - more,
+        r - p,
+    ]
+    return [v + w for v, w in zip(x, extra)]
 
 
 def precise_dot(value, matrix):
@@ -253,7 +292,7 @@
     return dot(high, matrix[0]) + dot(low, matrix[0]) + dot(high, matrix[1])
 
 
-def transform_tables(owners, length):
+def transform_tables(owners, length, norm_scale):
     width = 2 * owners
     counter = np.arange(length)
     angles = two_pi * (counter[:, None] * counter[None, :] % length) / length
@@ -263,8 +302,10 @@
     low = (matrix - high.astype(np.float32)).astype(jnp.bfloat16)
     outer = np.arange(owners + 1)
     angles = two_pi * (outer[:, None] * counter[None, :]) / (width * length)
-    twiddle = np.stack([np.cos(angles), -np.sin(angles)], axis=1).astype(np.float32)
-    return np.stack([high, low]), twiddle
+    twiddle = np.stack([np.cos(angles), -np.sin(angles)], axis=1)
+    weight = np.where(outer % owners == 0, 1.0, 2.0) * norm_scale / (width * length)
+    twiddle = np.concatenate([twiddle, twiddle * weight[:, None, None]], axis=1)
+    return np.stack([high, low]), twiddle.astype(np.float32)
 
 
 def three_pieces(value):
@@ -342,7 +383,6 @@
     groups = peers // owners
     part_count = groups * SUBLANES
     rows = 2 * part_count
-    width = 2 * owners
     pairs = part_count // 2
     half = pairs // SUBLANES
     rows_in[...] = got[...].astype(jnp.float32)
@@ -374,22 +414,29 @@
     )
     rate = (step * pole[0], step * pole[1])
 
-    row = lax.broadcasted_iota(jnp.int32, (SUBLANES, LANES), 0).astype(jnp.float32)
-    doublings = []
-    size = SUBLANES
-    while size < length:
-        doublings.append(size)
+    reach = length // 2
+    row = lax.broadcasted_iota(jnp.int32, (SUBLANES, LANES), 0)
+    doubled = []
+    size = 1
+    while size < owners * length:
+        doubled.append(power(rate[0], rate[1], float(size)))
         size *= 2
-    jumps = jnp.zeros((SUBLANES, LANES), jnp.float32)
-    for place, jump in enumerate(doublings):
-        jumps = jnp.where(row == place, float(jump), jumps)
+    block_bit, reach_bit = length.bit_length() - 1, reach.bit_length() - 1
+    bits = [(row & (1 << i)) != 0 for i in range(SUBLANES.bit_length() - 1)]
+
+    def by_rows(p, first):
+        out = None
+        for i, bit in enumerate(bits):
+            real, imag = (side[p : p + 1] for side in doubled[first + i])
+            value = (jnp.where(bit, real, 1.0), jnp.where(bit, imag, 0.0))
+            out = value if out is None else times(out, value)
+        return out
+
     bases = []
     for p in range(pairs):
-        rate_real, rate_imag = rate[0][p : p + 1], rate[1][p : p + 1]
-        shifts = power(rate_real, rate_imag, jumps)
-        table = [power(rate_real, rate_imag, row)]
-        for place in range(len(doublings)):
-            shift = (shifts[0][place : place + 1], shifts[1][place : place + 1])
+        table = [by_rows(p, 0)]
+        for i in range(len(bits), reach_bit):
+            shift = tuple(side[p : p + 1] for side in doubled[i])
             table += [times(block, shift) for block in table]
         for place in range(0, len(table), 2):
             spot = place * SUBLANES
@@ -398,8 +445,9 @@
                 high, low = split_halves(value)
                 lanes = slice(side * LANES, (side + 1) * LANES)
                 powers[p, spot : spot + 2 * SUBLANES, lanes] = high
-                powers[p, length + spot : length + spot + 2 * SUBLANES, lanes] = low
-        bases.append(power(rate_real, rate_imag, row * float(length)))
+                powers[p, reach + spot : reach + spot + 2 * SUBLANES, lanes] = low
+        base = by_rows(p, block_bit)
+        bases.append((base, times(base, tuple(side[p : p + 1] for side in doubled[reach_bit]))))
 
     blocks = []
     for s in range(owners):
@@ -412,14 +460,10 @@
             )
         )
     spectra = []
-    for k in range(owners + 1):
-        real = weighted_sum([(turn(k * s, width)[0], blocks[s]) for s in range(owners)])
-        imag = weighted_sum([(-turn(k * s, width)[1], blocks[s]) for s in range(owners)])
-        if imag is None:
-            imag = jnp.zeros_like(real)
+    for k, value in enumerate(blocks_forward(blocks)):
         if k:
-            real, imag = times((real, imag), (twiddle[k, 0:1], twiddle[k, 1:2]))
-        spectra.append(jnp.concatenate([real, imag], axis=1))
+            value = times(value, (twiddle[k, 0:1], twiddle[k, 1:2]))
+        spectra.append(jnp.concatenate(value, axis=1))
     freq = precise_dot(jnp.concatenate(spectra, axis=0), matrix)
 
     products = []
@@ -435,36 +479,32 @@
     for k in range(owners + 1):
         value = back[k * part_count : (k + 1) * part_count]
         value = (value[:, :length], value[:, length:])
-        if k:
-            value = times(value, (twiddle[k, 0:1], twiddle[k, 1:2]))
-        turned.append(value)
-    scale = norm_scale / (width * length)
-    for b in range(owners):
-        terms = []
-        for k in range(owners + 1):
-            weight = scale if k in (0, owners) else 2.0 * scale
-            cosine, sine = turn(k * b, width)
-            terms += [(weight * cosine, turned[k][0]), (weight * sine, turned[k][1])]
-        lags[b * part_count : (b + 1) * part_count] = weighted_sum(terms)
-
-    offset = lax.broadcasted_iota(jnp.int32, (owners, length), 1).astype(jnp.float32)
-    start = row * float(length)
+        turned.append(times(value, (twiddle[k, 2:3], twiddle[k, 3:4])))
+    for b, value in enumerate(blocks_back(turned)):
+        lags[b * part_count : (b + 1) * part_count] = value
+
+    lane = lax.broadcasted_iota(jnp.int32, (4 * owners, LANES), 1)
+    left_rows = lane < reach
+    left_both = left_rows[: 2 * owners]
+    offset = jnp.where(left_rows, lane, lane - reach).astype(jnp.float32)
+    start = row.astype(jnp.float32) * float(length)
     first = left[:owners]
     for p in range(pairs):
         one = lags[pl.ds(p, owners, stride=part_count), :]
         two = lags[pl.ds(pairs + p, owners, stride=part_count), :]
-        high, low = split_halves(
-            jnp.concatenate([one, two, one * offset, two * offset], axis=0)
+        both = jnp.concatenate([one, two], axis=0)
+        turned_both = pltpu.roll(both, reach, 1)
+        plain = jnp.concatenate(
+            [jnp.where(left_both, both, turned_both), jnp.where(left_both, turned_both, both)], axis=0
         )
-        factor = jnp.concatenate(
-            [
-                jnp.concatenate([high, high], axis=1),
-                jnp.concatenate([low, jnp.zeros_like(low)], axis=1),
-            ],
-            axis=0,
-        )
+        factors = []
+        for value in (plain, plain * offset):
+            high = value.astype(jnp.bfloat16)
+            low = jnp.where(left_rows, value - high.astype(jnp.float32), 0.0)
+            factors.append((high, low.astype(jnp.bfloat16)))
+        factor = jnp.concatenate([factors[i][j] for j in range(2) for i in range(2)], axis=0)
         raw = jnp.dot(factor, powers[p], preferred_element_type=jnp.float32)
-        raw = raw[: 4 * owners] + raw[4 * owners :]
+        raw = raw[: 8 * owners] + raw[8 * owners :]
 
         def pick(place, side):
             lanes = slice(side * LANES, (side + 1) * LANES)
@@ -472,20 +512,23 @@
             bottom = raw[(2 * place + 1) * owners : (2 * place + 2) * owners, lanes]
             return jnp.where(first, top, bottom)
 
-        plain = (pick(0, 0), pick(0, 1))
-        near = (start * plain[0] + pick(1, 0), start * plain[1] + pick(1, 1))
-        for place, value in enumerate(times(bases[p], plain) + times(bases[p], near)):
+        found = [0.0] * 4
+        for part, base in enumerate(bases[p]):
+            near = start + float(part * reach)
+            value = (pick(part, 0), pick(part, 1))
+            lagged = (near * value[0] + pick(2 + part, 0), near * value[1] + pick(2 + part, 1))
+            found = [x + y for x, y in zip(found, times(base, value) + times(base, lagged))]
+        for place, value in enumerate(found):
             sums[place, p : p + 1] = jnp.sum(value, axis=0, keepdims=True)
 
-    size = jnp.exp(rate[0])
-    cosine, sine = cos_sin(rate[1])
     sine_half = cos_sin(0.5 * rate[1])[1]
-    lift = (grow(rate[0]) * cosine - 2.0 * sine_half * sine_half, size * sine)
+    cosine = 1.0 - 2.0 * sine_half * sine_half
+    lift = (grow(rate[0]) * cosine - 2.0 * sine_half * sine_half, doubled[0][1])
     norm = 1.0 / (pole[0] * pole[0] + pole[1] * pole[1])
     inverse = (pole[0] * norm, -pole[1] * norm)
     ratio = times(lift, inverse)
     coef = times(read, ratio)
-    lifted = times((size * cosine, size * sine), inverse)
+    lifted = times(doubled[0], inverse)
     total = (sums[0] * (2.0 * norm_scale), sums[1] * (2.0 * norm_scale))
     lag_total = (sums[2] * (2.0 * norm_scale), sums[3] * (2.0 * norm_scale))
     on_read = times(total, ratio)
@@ -605,7 +648,7 @@
     )(inputs, out_grad, readout.transpose(0, 2, 1).reshape(LANES, channels), log_step[None])
     got = exchange(pieces)
 
-    held = [jnp.asarray(table) for table in transform_tables(owners, length)]
+    held = [jnp.asarray(table) for table in transform_tables(owners, length, norm_scale)]
     held += [decay_log[None], rotation[None]]
     held = pl.pallas_call(
         hold_kernel,
@@ -622,7 +665,7 @@
         scratch_shapes=[
             pltpu.VMEM((peers * ROWS, LANES), f32),
             pltpu.VMEM((owners * part_count, length), f32),
-            pltpu.VMEM((pairs, 2 * length, 2 * LANES), bf16),
+            pltpu.VMEM((pairs, length, 2 * LANES), bf16),
             pltpu.VMEM((4, pairs, LANES), f32),
         ],
         compiler_params=memory,

time: 33 us -> 32.6 us (0.988)
  Pallas kernels: 5.48 us -> 5.02 us
    pallas_call x1, Pallas kernels: 2.58 us -> 2.12 us  [kernel_device(): pl.pallas_call(functools.partial(main_kernel, owners, norm_scale), out_sh...]
where the time goes in v5:
time: 32.6 us; the launch traced here: 32.3 us
  blocking collectives  10.7 us (33%)
  waiting for transfers between devices  7.87 us (24%)
  starting transfers between devices  7.3 us (22%)
  Pallas kernels  5.02 us (15%)
  between operations  0.72 us (2%)
  local copies, waits for them, and re-layouts  0.65 us (2%)
    all_to_all x1, blocking collectives, exchange(): lax.all_to_all(value, ('seq', 'ch'), split_axis=0, concat_axis=0, tiled=T...  10.7 us
    all_to_all x1, waiting for transfers between devices, exchange(): lax.all_to_all(value, ('seq', 'ch'), split_axis=0, concat_axis=0, tiled=T...  7.87 us
    all_to_all x1, starting transfers between devices, exchange(): lax.all_to_all(value, ('seq', 'ch'), split_axis=0, concat_axis=0, tiled=T...  7.3 us
    pallas_call x1, Pallas kernels, kernel_device(): pl.pallas_call(functools.partial(main_kernel, owners, norm_scale), out_sh...  2.12 us
    pallas_call x1, Pallas kernels, kernel_device(): pl.pallas_call(pack_kernel, out_shape=jax.ShapeDtypeStruct((peers * ROWS,...  1.78 us
    pallas_call x1, Pallas kernels, kernel_device(): pl.pallas_call(unpack_kernel, out_shape=[jax.ShapeDtypeStruct((channels,...  1.09 us
  transfers between devices with their start and end apart: 1, of which 1 were waited for; matrix products, arithmetic and copies ran while one was open for 0% of the time, Pallas kernels for 0%

profile of v5, /device:TPU:0, one launch (start us, length us, event | category | flops | bytes accessed | tf_op | source)
XLA Modules:
  0.0 32.3 jit_solution(16453691580975218320)
XLA Ops:
  0.6 1.8 %shard_map.111 = bf16[640,128]{1,0:T(8,128)(2,1)} custom-call(bf16[256,128]{1,0:T(8,128)(2,1)} %inputs.1, bf16[256,128]{1,0:T(8,128)(2,1)} %out_grad.1, f32[128,256]{1,0:T(8,128)} %bitcast.20, f32[1,256]{1,0:T(1,128)} %bitcast.21), custom_call_target="tpu_custom_call" | custom-call | tf_op jit(solution)/shard_map/pallas_call | solution.py:634
  2.4 0.0 copy-start
  2.4 0.0 copy-start.1
  2.4 7.3 %all-to-all-start = ((bf16[32,10,2,128]{3,2,1,0:T(2,128)(2,1)}), bf16[32,10,2,128]{3,2,1,0:T(2,128)(2,1)S(1)}, u32[]{:S(2)}, u32[]{:S(2)}) async-start(bf16[32,10,2,128]{3,2,1,0:T(2,128)(2,1)} %bitcast.17), calls=%async_computation | async-start | bytes 327680 | tf_op jit(solution)/shard_map/all_to_all | solution.py:630
  9.8 0.0 copy-start.2
  9.8 0.0 copy-start.3
  9.8 0.0 copy-done
  9.8 0.0 copy-done.1
  9.8 0.6 %copy-done.2 = f32[64]{0:T(128)S(1)} copy-done((f32[64]{0:T(128)S(1)}, f32[64]{0:T(128)}, u32[]{:S(2)}) %copy-start.2) | copy-done | bytes 280
  10.4 0.0 copy-done.3
  10.5 7.9 %all-to-all-done = bf16[32,10,2,128]{3,2,1,0:T(2,128)(2,1)S(1)} async-done(((bf16[32,10,2,128]{3,2,1,0:T(2,128)(2,1)}), bf16[32,10,2,128]{3,2,1,0:T(2,128)(2,1)S(1)}, u32[]{:S(2)}, u32[]{:S(2)}) %all-to-all-start) | async-done | bytes 163872 | tf_op jit(solution)/shard_map/all_to_all | solution.py:630
  18.3 2.1 %shard_map.113 = f32[640,128]{1,0:T(8,128)S(1)} custom-call(bf16[640,128]{1,0:T(8,128)(2,1)S(1)} %bitcast.14, bf16[2,256,256]{2,1,0:T(8,128)(2,1)S(1)} %get-tuple-element.12.matrix, f32[9,4,128]{2,1,0:T(4,128)S(1)} %get-tuple-element.13.twiddle, f32[1,64]{1,0:T(1,128)S(1)} %get-tuple-element.14.decay_log, f32[1,64]{1,0:T(1,128)S(1)} %get-tuple-element.15.rotation), custom_call_target="tpu_custom_call" | custom-call | tf_op jit(solution)/shard_map/pallas_call | solution.py:660
  20.5 10.7 %all_to_all.10 = f16[32,10,2,128]{3,2,1,0:T(2,128)(2,1)S(1)} all-to-all(f16[32,10,2,128]{3,2,1,0:T(2,128)(2,1)S(1)} %bitcast.18), channel_id=1, replica_groups=mesh['seq'=8,'ch'=4] {'seq','ch'}, dimensions={0} | all-to-all | bytes 327680 | tf_op jit(solution)/shard_map/all_to_all | solution.py:630
  31.2 1.1 %shard_map.114 = (f32[256,128]{1,0:T(8,128)}, f32[128,256]{1,0:T(8,128)}, f32[256]{0:T(256)}, f32[2,64]{1,0:T(2,128)}) custom-call(f32[640,128]{1,0:T(8,128)S(1)} %convert.1.got), custom_call_target="tpu_custom_call" | custom-call | tf_op jit(solution)/shard_map/pallas_call | solution.py:674
  (3 shorter events, 0.1 us)
Async XLA Ops:
  2.4 7.4 %copy-start = (bf16[2,256,256]{2,1,0:T(8,128)(2,1)S(1)}, bf16[2,256,256]{2,1,0:T(8,128)(2,1)}, u32[]{:S(2)}) copy-start(bf16[2,256,256]{2,1,0:T(8,128)(2,1)} %constant.4.clone.refs_0_) | copy-start | bytes 786436
  2.4 7.4 %copy-start.1 = (f32[9,4,128]{2,1,0:T(4,128)S(1)}, f32[9,4,128]{2,1,0:T(4,128)}, u32[]{:S(2)}) copy-start(f32[9,4,128]{2,1,0:T(4,128)} %constant.5.clone.refs_1_) | copy-start | bytes 55300
  2.4 15.9 %all-to-all-start = ((bf16[32,10,2,128]{3,2,1,0:T(2,128)(2,1)}), bf16[32,10,2,128]{3,2,1,0:T(2,128)(2,1)S(1)}, u32[]{:S(2)}, u32[]{:S(2)}) async-start(bf16[32,10,2,128]{3,2,1,0:T(2,128)(2,1)} %bitcast.17), calls=%async_computation | async-start | bytes 327680 | tf_op jit(solution)/shard_map/all_to_all | solution.py:630
  9.8 0.7 %copy-start.2 = (f32[64]{0:T(128)S(1)}, f32[64]{0:T(128)}, u32[]{:S(2)}) copy-start(f32[64]{0:T(128)} %param.12) | copy-start | bytes 772
  9.8 0.7 %copy-start.3 = (f32[64]{0:T(128)S(1)}, f32[64]{0:T(128)}, u32[]{:S(2)}) copy-start(f32[64]{0:T(128)} %param.13) | copy-start | bytes 772

commit v6 on v5

--- a/solution.py
+++ b/solution.py
@@ -286,12 +286,6 @@
     return [v + w for v, w in zip(x, extra)]
 
 
-def precise_dot(value, matrix):
-    high, low = split_halves(value)
-    dot = functools.partial(jnp.dot, preferred_element_type=jnp.float32)
-    return dot(high, matrix[0]) + dot(low, matrix[0]) + dot(high, matrix[1])
-
-
 def transform_tables(owners, length, norm_scale):
     width = 2 * owners
     counter = np.arange(length)
@@ -326,6 +320,8 @@
 READ, STEP, ROWS = 16, 19, 20
 LAGS, GRADS, STATE, SINGLES = 0, 8, 16, 18
 STEP_LANES, SCALE_LANES = (0, 8), (16, 17, 18, 19)
+SPARE = 15.0
+PARTS = 4
 
 
 def pack_kernel(inputs, out_grad, readout, log_step, out, signals, read, step, turned, rows, sems):
@@ -365,10 +361,16 @@
         target[...] = source[...]
 
 
-def scaled(value):
-    most = jnp.max(jnp.max(jnp.abs(value), axis=1, keepdims=True), axis=0, keepdims=True)
-    exponent = jnp.floor(jnp.log(jnp.maximum(most, 1e-30)) * (1.0 / math.log(2.0))) + 1.0
-    return value * jnp.exp2(-exponent), exponent
+def exponent_of(bound):
+    return jnp.floor(jnp.log(jnp.maximum(bound, 1e-30)) * (1.0 / math.log(2.0))) + (2.0 - SPARE)
+
+
+def greatest(value):
+    return jnp.max(jnp.max(value, axis=1, keepdims=True), axis=0, keepdims=True)
+
+
+def size_of(value):
+    return jnp.abs(value[0]) + jnp.abs(value[1])
 
 
 def two_pieces(value):
@@ -377,7 +379,24 @@
 
 
 def main_kernel(
-    owners, norm_scale, got, matrix, twiddle, decay_log, rotation, sent, rows_in, lags, powers, sums
+    owners,
+    norm_scale,
+    got,
+    matrix,
+    twiddle,
+    decay_log,
+    rotation,
+    sent,
+    rows_in,
+    spectra,
+    freq,
+    back,
+    params,
+    doubled,
+    bases,
+    powers,
+    lags,
+    sums,
 ):
     peers, length = got.shape[0] // ROWS, got.shape[1]
     groups = peers // owners
@@ -385,7 +404,17 @@
     rows = 2 * part_count
     pairs = part_count // 2
     half = pairs // SUBLANES
-    rows_in[...] = got[...].astype(jnp.float32)
+    reach = length // 2
+    device = lax.axis_index("seq") * groups + lax.axis_index("ch")
+    lane = lax.broadcasted_iota(jnp.int32, (pairs, LANES), 1)
+    left = lane < LANES // 2
+    row = lax.broadcasted_iota(jnp.int32, (SUBLANES, LANES), 0)
+
+    def swap(value):
+        return pltpu.roll(value, LANES // 2, 1)
+
+    def lanes_of(side):
+        return slice(side * LANES, (side + 1) * LANES)
 
     def collect(spot):
         tiles = [
@@ -394,222 +423,280 @@
         ]
         return jnp.concatenate(tiles[:half], axis=0), jnp.concatenate(tiles[half:], axis=0)
 
-    lane = lax.broadcasted_iota(jnp.int32, (pairs, LANES), 1)
-    left = lane < LANES // 2
-
-    def swap(value):
-        return pltpu.roll(value, LANES // 2, 1)
-
-    lower, upper = [sum(side) for side in zip(*(collect(READ + i) for i in range(3)))]
-    read = (jnp.where(left, lower, swap(upper)), jnp.where(left, swap(lower), upper))
-    lower, upper = [
-        sum(side[:, i : i + 1] for i in range(3)) + jnp.zeros_like(side) for side in collect(STEP)
-    ]
-    step = jnp.exp(jnp.where(left, lower, upper))
-    decay_row = jnp.concatenate([decay_log[...], decay_log[...]], axis=1)
-    rotation_row = jnp.concatenate([rotation[...], rotation[...]], axis=1)
-    pole = (
-        jnp.broadcast_to(-jnp.exp(decay_row), step.shape),
-        jnp.broadcast_to(rotation_row, step.shape),
-    )
-    rate = (step * pole[0], step * pole[1])
-
-    reach = length // 2
-    row = lax.broadcasted_iota(jnp.int32, (SUBLANES, LANES), 0)
-    doubled = []
-    size = 1
-    while size < owners * length:
-        doubled.append(power(rate[0], rate[1], float(size)))
-        size *= 2
+    def make_params():
+        lower, upper = [sum(side) for side in zip(*(collect(READ + i) for i in range(3)))]
+        read = (jnp.where(left, lower, swap(upper)), jnp.where(left, swap(lower), upper))
+        lower, upper = [
+            sum(side[:, i : i + 1] for i in range(3)) + jnp.zeros_like(side)
+            for side in collect(STEP)
+        ]
+        step = jnp.exp(jnp.where(left, lower, upper))
+        decay_row = jnp.concatenate([decay_log[...], decay_log[...]], axis=1)
+        rotation_row = jnp.concatenate([rotation[...], rotation[...]], axis=1)
+        pole = (
+            jnp.broadcast_to(-jnp.exp(decay_row), step.shape),
+            jnp.broadcast_to(rotation_row, step.shape),
+        )
+        rate = (step * pole[0], step * pole[1])
+        place, size = 0, 1
+        while size < owners * length:
+            doubled[place], doubled[place + 1] = power(rate[0], rate[1], float(size))
+            place, size = place + 2, size * 2
+        sine = cos_sin(0.5 * rate[1])[1]
+        cosine = 1.0 - 2.0 * sine * sine
+        lift = (grow(rate[0]) * cosine - 2.0 * sine * sine, doubled[1])
+        norm = 1.0 / (pole[0] * pole[0] + pole[1] * pole[1])
+        inverse = (pole[0] * norm, -pole[1] * norm)
+        ratio = times(lift, inverse)
+        coef = times(read, ratio)
+        lifted = times((doubled[0], doubled[1]), inverse)
+        values = (rate, ratio, coef, times(read, lifted), pole, times(coef, inverse), (step, step))
+        for place, value in enumerate(values):
+            params[2 * place], params[2 * place + 1] = value
+
     block_bit, reach_bit = length.bit_length() - 1, reach.bit_length() - 1
     bits = [(row & (1 << i)) != 0 for i in range(SUBLANES.bit_length() - 1)]
+
+    def doubled_row(p, i):
+        return doubled[2 * i, p : p + 1, :], doubled[2 * i + 1, p : p + 1, :]
 
     def by_rows(p, first):
         out = None
         for i, bit in enumerate(bits):
-            real, imag = (side[p : p + 1] for side in doubled[first + i])
+            real, imag = doubled_row(p, first + i)
             value = (jnp.where(bit, real, 1.0), jnp.where(bit, imag, 0.0))
             out = value if out is None else times(out, value)
         return out
 
-    bases = []
-    for p in range(pairs):
-        table = [by_rows(p, 0)]
-        for i in range(len(bits), reach_bit):
-            shift = tuple(side[p : p + 1] for side in doubled[i])
-            table += [times(block, shift) for block in table]
-        for place in range(0, len(table), 2):
-            spot = place * SUBLANES
+    def make_tables():
+        for p in range(pairs):
+            table = [by_rows(p, 0)]
+            for i in range(len(bits), reach_bit):
+                table += [times(block, doubled_row(p, i)) for block in table]
+            for place in range(0, len(table), 2):
+                for side in range(2):
+                    value = jnp.concatenate([table[place][side], table[place + 1][side]], axis=0)
+                    for i, piece in enumerate(split_halves(value)):
+                        spot = 2 * i * reach + place * SUBLANES
+                        powers[p, spot : spot + 2 * SUBLANES, lanes_of(side)] = piece
+                        spot += reach
+                        powers[p, spot : spot + 2 * SUBLANES, lanes_of(side)] = piece
+            base = by_rows(p, block_bit)
+            bases[p, 0], bases[p, 1] = base
+            bases[p, 2], bases[p, 3] = times(base, doubled_row(p, reach_bit))
+
+    def transform(source, target, count):
+        dot = functools.partial(jnp.dot, preferred_element_type=jnp.float32)
+        cuts = [(owners + 1) * i // PARTS * count for i in range(PARTS + 1)]
+        for part in map(slice, cuts, cuts[1:]):
+            low = source[1, part]
+            target[part] = (
+                dot(source[0, part], matrix[0]) + dot(low, matrix[0]) + dot(source[0, part], matrix[1])
+            )
+
+    def spread_blocks():
+        rows_in[...] = got[...].astype(jnp.float32)
+        blocks = []
+        for s in range(owners):
+            spots = [(s * groups + group) * ROWS for group in range(groups)]
+            blocks.append(
+                jnp.concatenate(
+                    [rows_in[spot : spot + SUBLANES] for spot in spots]
+                    + [rows_in[spot + SUBLANES : spot + 2 * SUBLANES] for spot in spots],
+                    axis=0,
+                )
+            )
+        for k, value in enumerate(blocks_forward(blocks)):
+            if k:
+                value = times(value, (twiddle[k, 0:1], twiddle[k, 1:2]))
             for side in range(2):
-                value = jnp.concatenate([table[place][side], table[place + 1][side]], axis=0)
-                high, low = split_halves(value)
-                lanes = slice(side * LANES, (side + 1) * LANES)
-                powers[p, spot : spot + 2 * SUBLANES, lanes] = high
-                powers[p, reach + spot : reach + spot + 2 * SUBLANES, lanes] = low
-        base = by_rows(p, block_bit)
-        bases.append((base, times(base, tuple(side[p : p + 1] for side in doubled[reach_bit]))))
-
-    blocks = []
-    for s in range(owners):
-        spots = [(s * groups + group) * ROWS for group in range(groups)]
-        blocks.append(
-            jnp.concatenate(
-                [rows_in[spot : spot + SUBLANES] for spot in spots]
-                + [rows_in[spot + SUBLANES : spot + 2 * SUBLANES] for spot in spots],
+                for i, piece in enumerate(split_halves(value[side])):
+                    spectra[i, k * rows : (k + 1) * rows, lanes_of(side)] = piece
+
+    def to_frequencies():
+        transform(spectra, freq, rows)
+        make_params()
+        make_tables()
+
+    def to_lags():
+        for k in range(owners + 1):
+            at_in = freq[k * rows : k * rows + part_count]
+            at_out = freq[k * rows + part_count : (k + 1) * rows]
+            ur, ui = at_in[:, :length], at_in[:, length:]
+            gr, gi = at_out[:, :length], at_out[:, length:]
+            for side, value in enumerate((gr * ur + gi * ui, gr * ui - gi * ur)):
+                for i, piece in enumerate(split_halves(value)):
+                    spectra[i, k * part_count : (k + 1) * part_count, lanes_of(side)] = piece
+        transform(spectra, back, part_count)
+
+    def finish():
+        turned = []
+        for k in range(owners + 1):
+            spots = slice(k * part_count, (k + 1) * part_count)
+            value = (back[spots, lanes_of(0)], back[spots, lanes_of(1)])
+            turned.append(times(value, (twiddle[k, 2:3], twiddle[k, 3:4])))
+        blocks = blocks_back(turned)
+
+        most = jnp.zeros((part_count, LANES), jnp.float32)
+        for b, block in enumerate(blocks):
+            most = jnp.maximum(most, jnp.abs(block))
+            lags[b * part_count : (b + 1) * part_count] = block
+
+        def param(place):
+            return params[2 * place], params[2 * place + 1]
+
+        rate, ratio, coef, through, pole, direct, (step, _) = (param(i) for i in range(7))
+        most = greatest(most)
+        whole = 2.0 * math.sqrt(owners * length)
+        on_rate = size_of(coef) * float(owners * length) + size_of(through)
+        on_pole = step * on_rate + size_of(direct)
+        lag_exponent = exponent_of(most)
+        grad_exponent = exponent_of(most * (whole * greatest(size_of(ratio))))
+        state_exponent = exponent_of(
+            most * (whole * part_count * greatest(on_pole * (1.0 - pole[0])))
+        )
+        step_exponent = exponent_of(
+            most * (whole * (LANES // 2) * greatest(on_rate * size_of(rate)))
+        )
+        lag_scale = jnp.exp2(-lag_exponent)
+        for b, block in enumerate(blocks):
+            for group in range(groups):
+                place = (b * groups + group) * ROWS
+                value = block[group * SUBLANES : (group + 1) * SUBLANES]
+                sent[place + LAGS : place + GRADS] = value * lag_scale
+
+        start = row.astype(jnp.float32) * float(length)
+        first = left[:owners]
+        wide = lax.broadcasted_iota(jnp.int32, (4 * owners, LANES), 1)
+        wide_left = wide < reach
+        offset = jnp.where(wide_left, wide, wide - reach).astype(jnp.float32)
+        both_left = wide_left[: 2 * owners]
+        for p in range(pairs):
+            both = jnp.concatenate(
+                [
+                    lags[pl.ds(first_row, owners, stride=part_count), :]
+                    for first_row in (p, pairs + p)
+                ],
                 axis=0,
             )
-        )
-    spectra = []
-    for k, value in enumerate(blocks_forward(blocks)):
-        if k:
-            value = times(value, (twiddle[k, 0:1], twiddle[k, 1:2]))
-        spectra.append(jnp.concatenate(value, axis=1))
-    freq = precise_dot(jnp.concatenate(spectra, axis=0), matrix)
-
-    products = []
-    for k in range(owners + 1):
-        at_in = freq[k * rows : k * rows + part_count]
-        at_out = freq[k * rows + part_count : (k + 1) * rows]
-        ur, ui = at_in[:, :length], at_in[:, length:]
-        gr, gi = at_out[:, :length], at_out[:, length:]
-        products.append(jnp.concatenate([gr * ur + gi * ui, gr * ui - gi * ur], axis=1))
-    back = precise_dot(jnp.concatenate(products, axis=0), matrix)
-
-    turned = []
-    for k in range(owners + 1):
-        value = back[k * part_count : (k + 1) * part_count]
-        value = (value[:, :length], value[:, length:])
-        turned.append(times(value, (twiddle[k, 2:3], twiddle[k, 3:4])))
-    for b, value in enumerate(blocks_back(turned)):
-        lags[b * part_count : (b + 1) * part_count] = value
-
-    lane = lax.broadcasted_iota(jnp.int32, (4 * owners, LANES), 1)
-    left_rows = lane < reach
-    left_both = left_rows[: 2 * owners]
-    offset = jnp.where(left_rows, lane, lane - reach).astype(jnp.float32)
-    start = row.astype(jnp.float32) * float(length)
-    first = left[:owners]
-    for p in range(pairs):
-        one = lags[pl.ds(p, owners, stride=part_count), :]
-        two = lags[pl.ds(pairs + p, owners, stride=part_count), :]
-        both = jnp.concatenate([one, two], axis=0)
-        turned_both = pltpu.roll(both, reach, 1)
-        plain = jnp.concatenate(
-            [jnp.where(left_both, both, turned_both), jnp.where(left_both, turned_both, both)], axis=0
-        )
-        factors = []
-        for value in (plain, plain * offset):
-            high = value.astype(jnp.bfloat16)
-            low = jnp.where(left_rows, value - high.astype(jnp.float32), 0.0)
-            factors.append((high, low.astype(jnp.bfloat16)))
-        factor = jnp.concatenate([factors[i][j] for j in range(2) for i in range(2)], axis=0)
-        raw = jnp.dot(factor, powers[p], preferred_element_type=jnp.float32)
-        raw = raw[: 8 * owners] + raw[8 * owners :]
-
-        def pick(place, side):
-            lanes = slice(side * LANES, (side + 1) * LANES)
-            top = raw[2 * place * owners : (2 * place + 1) * owners, lanes]
-            bottom = raw[(2 * place + 1) * owners : (2 * place + 2) * owners, lanes]
-            return jnp.where(first, top, bottom)
-
-        found = [0.0] * 4
-        for part, base in enumerate(bases[p]):
-            near = start + float(part * reach)
-            value = (pick(part, 0), pick(part, 1))
-            lagged = (near * value[0] + pick(2 + part, 0), near * value[1] + pick(2 + part, 1))
-            found = [x + y for x, y in zip(found, times(base, value) + times(base, lagged))]
-        for place, value in enumerate(found):
-            sums[place, p : p + 1] = jnp.sum(value, axis=0, keepdims=True)
-
-    sine_half = cos_sin(0.5 * rate[1])[1]
-    cosine = 1.0 - 2.0 * sine_half * sine_half
-    lift = (grow(rate[0]) * cosine - 2.0 * sine_half * sine_half, doubled[0][1])
-    norm = 1.0 / (pole[0] * pole[0] + pole[1] * pole[1])
-    inverse = (pole[0] * norm, -pole[1] * norm)
-    ratio = times(lift, inverse)
-    coef = times(read, ratio)
-    lifted = times(doubled[0], inverse)
-    total = (sums[0] * (2.0 * norm_scale), sums[1] * (2.0 * norm_scale))
-    lag_total = (sums[2] * (2.0 * norm_scale), sums[3] * (2.0 * norm_scale))
-    on_read = times(total, ratio)
-    on_read = (on_read[0], -on_read[1])
-    on_rate = times(coef, lag_total)
-    through = times(times(total, read), lifted)
-    on_rate = (on_rate[0] + through[0], on_rate[1] + through[1])
-    direct = times(times(total, coef), inverse)
-    on_pole = (step * on_rate[0] - direct[0], step * on_rate[1] - direct[1])
-    on_step = times(on_rate, rate)[0]
-    on_decay = jnp.sum(on_pole[0] * pole[0], axis=0, keepdims=True)
-    on_rotation = -jnp.sum(on_pole[1], axis=0, keepdims=True)
-    on_decay = on_decay + swap(on_decay)
-    on_rotation = on_rotation + swap(on_rotation)
-    state, state_exponent = scaled(jnp.where(left[0:1], on_decay, on_rotation))
-
-    lag_values, lag_exponent = scaled(lags[...])
-    lower = jnp.where(left, on_read[0], swap(on_read[1]))
-    upper = jnp.where(left, swap(on_read[0]), on_read[1])
-    grads, grad_exponent = scaled(jnp.concatenate([lower, upper], axis=0))
-    step_column = jnp.concatenate(
-        [
-            jnp.sum(jnp.where(left, on_step, 0.0), axis=1, keepdims=True),
-            jnp.sum(jnp.where(left, 0.0, on_step), axis=1, keepdims=True),
-        ],
-        axis=0,
-    )
-    step_column, step_exponent = scaled(step_column)
-    place_row = lax.broadcasted_iota(jnp.int32, (SUBLANES, LANES), 0)
-    place_lane = lax.broadcasted_iota(jnp.int32, (SUBLANES, LANES), 1)
-    scales = jnp.zeros((1, LANES), jnp.float32)
-    for spot, value in zip(
-        SCALE_LANES, (lag_exponent, grad_exponent, state_exponent, step_exponent)
-    ):
-        scales = jnp.where(place_lane[0:1] == spot, value, scales)
-    state_high, state_low = two_pieces(state)
-    tails = []
-    for group in range(groups):
-        pieces = two_pieces(step_column[group * SUBLANES : (group + 1) * SUBLANES])
-        spread = jnp.zeros((SUBLANES, LANES), jnp.float32)
-        for spot, piece in zip(STEP_LANES, pieces):
-            spread = jnp.where(place_lane == place_row + spot, piece, spread)
-        singles = scales + jnp.sum(spread, axis=0, keepdims=True)
-        tails.append(jnp.concatenate([state_high, state_low, singles, singles], axis=0))
-    for b in range(owners):
+            swapped = swap(both)
+            plain = jnp.concatenate(
+                [jnp.where(both_left, both, swapped), jnp.where(both_left, swapped, both)], axis=0
+            )
+            factor = []
+            for value in (plain, plain * offset):
+                high = value.astype(jnp.bfloat16).astype(jnp.float32)
+                factor.append(jnp.where(wide_left, high, value - high))
+            factor = jnp.concatenate(factor, axis=0).astype(jnp.bfloat16)
+            raw = jnp.dot(
+                jnp.concatenate([factor, factor], axis=1),
+                powers[p],
+                preferred_element_type=jnp.float32,
+            )
+
+            def pick(place, side):
+                top = raw[2 * place * owners : (2 * place + 1) * owners, lanes_of(side)]
+                bottom = raw[(2 * place + 1) * owners : (2 * place + 2) * owners, lanes_of(side)]
+                return jnp.where(first, top, bottom)
+
+            found = None
+            for part in range(2):
+                base = (bases[p, 2 * part], bases[p, 2 * part + 1])
+                near = start + float(part * reach)
+                value = (pick(part, 0), pick(part, 1))
+                lagged = (near * value[0] + pick(2 + part, 0), near * value[1] + pick(2 + part, 1))
+                terms = times(base, value) + times(base, lagged)
+                found = terms if found is None else [x + y for x, y in zip(found, terms)]
+            for place, value in enumerate(found):
+                sums[place, p : p + 1] = jnp.sum(value, axis=0, keepdims=True)
+
+        total = (sums[0] * (2.0 * norm_scale), sums[1] * (2.0 * norm_scale))
+        lag_total = (sums[2] * (2.0 * norm_scale), sums[3] * (2.0 * norm_scale))
+        on_read = times(total, ratio)
+        on_read = (on_read[0], -on_read[1])
+        on_rate = times(coef, lag_total)
+        more = times(total, through)
+        on_rate = (on_rate[0] + more[0], on_rate[1] + more[1])
+        less = times(total, direct)
+        on_pole = (step * on_rate[0] - less[0], step * on_rate[1] - less[1])
+        on_step = times(on_rate, rate)[0]
+        on_decay = jnp.sum(on_pole[0] * pole[0], axis=0, keepdims=True)
+        on_rotation = -jnp.sum(on_pole[1], axis=0, keepdims=True)
+        on_decay = on_decay + swap(on_decay)
+        on_rotation = on_rotation + swap(on_rotation)
+        state = jnp.where(left[0:1], on_decay, on_rotation) * jnp.exp2(-state_exponent)
+
+        grad_scale = jnp.exp2(-grad_exponent)
+        on_read = (on_read[0] * grad_scale, on_read[1] * grad_scale)
+        lower = jnp.where(left, on_read[0], swap(on_read[1]))
+        upper = jnp.where(left, swap(on_read[0]), on_read[1])
+        grads = jnp.concatenate([lower, upper], axis=0)
+        step_column = jnp.concatenate(
+            [
+                jnp.sum(jnp.where(left, on_step, 0.0), axis=1, keepdims=True),
+                jnp.sum(jnp.where(left, 0.0, on_step), axis=1, keepdims=True),
+            ],
+            axis=0,
+        ) * jnp.exp2(-step_exponent)
+        place_lane = lax.broadcasted_iota(jnp.int32, (SUBLANES, LANES), 1)
+        scales = jnp.zeros((1, LANES), jnp.float32)
+        for spot, value in zip(
+            SCALE_LANES, (lag_exponent, grad_exponent, state_exponent, step_exponent)
+        ):
+            scales = jnp.where(place_lane[0:1] == spot, value, scales)
+        state_high, state_low = two_pieces(state)
+        tails = []
         for group in range(groups):
-            spot = b * part_count + group * SUBLANES
-            place = (b * groups + group) * ROWS
-            sent[place + LAGS : place + GRADS] = lag_values[spot : spot + SUBLANES]
-            sent[place + GRADS : place + STATE] = grads[group * SUBLANES : (group + 1) * SUBLANES]
-            sent[place + STATE : place + ROWS] = tails[group]
-
-
-def unpack_kernel(got, kernel_grad, readout_grad, step_grad, state_grad, grads):
+            pieces = two_pieces(step_column[group * SUBLANES : (group + 1) * SUBLANES])
+            spread = jnp.zeros((SUBLANES, LANES), jnp.float32)
+            for spot, piece in zip(STEP_LANES, pieces):
+                spread = jnp.where(place_lane == row + spot, piece, spread)
+            singles = scales + jnp.sum(spread, axis=0, keepdims=True)
+            tails.append(jnp.concatenate([state_high, state_low, singles, singles], axis=0))
+        for b in range(owners):
+            for group in range(groups):
+                place = (b * groups + group) * ROWS
+                sent[place + GRADS : place + STATE] = grads[
+                    group * SUBLANES : (group + 1) * SUBLANES
+                ]
+                sent[place + STATE : place + ROWS] = tails[group]
+
+    for section in (spread_blocks, to_frequencies, to_lags, finish):
+        section()
+
+
+def unpack_kernel(got, kernel_grad, readout_grad, step_grad, state_grad, wide, grads):
     peers = got.shape[0] // ROWS
+    per_row = LANES // SUBLANES
     singles = got[pl.ds(SINGLES, peers, stride=ROWS), :]
-    scales = [jnp.exp2(singles[:, spot : spot + 1]) for spot in SCALE_LANES]
-    for peer in range(peers):
-        spot = peer * ROWS
-        lanes = slice(peer * SUBLANES, (peer + 1) * SUBLANES)
-        kernel_grad[lanes] = got[spot + LAGS : spot + GRADS] * scales[0][peer : peer + 1]
-        grads[lanes] = got[spot + GRADS : spot + STATE] * scales[1][peer : peer + 1]
-    for spot in range(0, peers * SUBLANES, LANES):
-        readout_grad[:, spot : spot + LANES] = grads[spot : spot + LANES].T
+    exponents = [jnp.broadcast_to(singles[:, spot : spot + 1], (peers, LANES)) for spot in SCALE_LANES]
+    scales = [jnp.exp2(value) for value in exponents]
+    for i in range(2):
+        wide[i] = scales[i]
+    for spot in range(0, peers, per_row):
+        part = slice(spot * SUBLANES, (spot + per_row) * SUBLANES)
+        for i, first, target in ((1, GRADS, grads), (0, LAGS, kernel_grad)):
+            for peer in range(spot, spot + per_row):
+                place = peer * ROWS + first
+                target[peer * SUBLANES : (peer + 1) * SUBLANES] = (
+                    got[place : place + SUBLANES] * wide[i, peer : peer + 1, :]
+                )
+        readout_grad[:, part] = grads[part].T
+
     high = got[pl.ds(STATE, peers, stride=ROWS), :]
     low = got[pl.ds(STATE + 1, peers, stride=ROWS), :]
-    state = jnp.sum((high + low * (1.0 / 256.0)) * scales[2], axis=0, keepdims=True)
+    total = jnp.sum((high + low * (1.0 / 256.0)) * scales[2], axis=0, keepdims=True)
     states = state_grad.shape[1]
-    state_grad[0:1] = state[:, :states]
-    state_grad[1:2] = state[:, states:]
-    per_row = LANES // SUBLANES
+    state_grad[0:1] = total[:, :states]
+    state_grad[1:2] = total[:, states:]
     lane = lax.broadcasted_iota(jnp.int32, (peers, LANES), 1)
     row = lax.broadcasted_iota(jnp.int32, (peers, LANES), 0)
-    steps = pltpu.roll(singles, LANES - STEP_LANES[1], 1) * (1.0 / 256.0) + singles
-    steps = jnp.where(lane < SUBLANES, steps * scales[3], 0.0)
-    reach = SUBLANES
-    while reach < LANES:
-        steps = steps + pltpu.roll(steps, reach, 1)
-        reach *= 2
+    high, low = (
+        jnp.take_along_axis(singles, lane % SUBLANES + first, axis=1) for first in STEP_LANES
+    )
+    value = (high + low * (1.0 / 256.0)) * scales[3]
     for spot in range(0, peers, per_row):
-        mine = jnp.where(row - spot == lane // SUBLANES, steps, 0.0)
+        mine = jnp.where(row - spot == lane // SUBLANES, value, 0.0)
         step_grad[spot * SUBLANES : (spot + per_row) * SUBLANES] = jnp.sum(mine, axis=0)
 
 
@@ -664,8 +751,14 @@
         out_specs=vmem,
         scratch_shapes=[
             pltpu.VMEM((peers * ROWS, LANES), f32),
+            pltpu.VMEM((2, (owners + 1) * 2 * part_count, 2 * LANES), bf16),
+            pltpu.VMEM(((owners + 1) * 2 * part_count, 2 * LANES), f32),
+            pltpu.VMEM(((owners + 1) * part_count, 2 * LANES), f32),
+            pltpu.VMEM((14, pairs, LANES), f32),
+            pltpu.VMEM((2 * (owners * length).bit_length(), pairs, LANES), f32),
+            pltpu.VMEM((pairs, 4, owners, LANES), f32),
+            pltpu.VMEM((pairs, 2 * length, 2 * LANES), bf16),
             pltpu.VMEM((owners * part_count, length), f32),
-            pltpu.VMEM((pairs, length, 2 * LANES), bf16),
             pltpu.VMEM((4, pairs, LANES), f32),
         ],
         compiler_params=memory,
@@ -681,7 +774,10 @@
         ],
         in_specs=[vmem],
         out_specs=[vmem] * 4,
-        scratch_shapes=[pltpu.VMEM((channels, LANES), f32)],
+        scratch_shapes=[
+            pltpu.VMEM((2, peers, LANES), f32),
+            pltpu.VMEM((channels, LANES), f32),
+        ],
         compiler_params=memory,
     )(back.astype(f32))
     readout_grad = readout_grad.reshape(2, states, channels).transpose(0, 2, 1)

time: 32.6 us -> 32.2 us (0.988)
  Pallas kernels: 5.02 us -> 4.61 us
where the time goes in v6:
time: 32.2 us; the launch traced here: 31.9 us
  blocking collectives  10.7 us (33%)
  waiting for transfers between devices  7.87 us (24%)
  starting transfers between devices  7.3 us (23%)
  Pallas kernels  4.61 us (14%)
  between operations  0.72 us (2%)
  local copies, waits for them, and re-layouts  0.65 us (2%)
    all_to_all x1, blocking collectives, exchange(): lax.all_to_all(value, ('seq', 'ch'), split_axis=0, concat_axis=0, tiled=T...  10.7 us
    all_to_all x1, waiting for transfers between devices, exchange(): lax.all_to_all(value, ('seq', 'ch'), split_axis=0, concat_axis=0, tiled=T...  7.87 us
    all_to_all x1, starting transfers between devices, exchange(): lax.all_to_all(value, ('seq', 'ch'), split_axis=0, concat_axis=0, tiled=T...  7.3 us
    pallas_call x1, Pallas kernels, kernel_device(): pl.pallas_call(functools.partial(main_kernel, owners, norm_scale), out_sh...  1.95 us
    pallas_call x1, Pallas kernels, kernel_device(): pl.pallas_call(pack_kernel, out_shape=jax.ShapeDtypeStruct((peers * ROWS,...  1.78 us
    pallas_call x1, Pallas kernels, kernel_device(): pl.pallas_call(unpack_kernel, out_shape=[jax.ShapeDtypeStruct((channels,...  0.85 us
    unnamed x8, local copies, waits for them, and re-layouts  0.65 us
  transfers between devices with their start and end apart: 1, of which 1 were waited for; matrix products, arithmetic and copies ran while one was open for 0% of the time, Pallas kernels for 0%

profile of v6, /device:TPU:0, one launch (start us, length us, event | category | flops | bytes accessed | tf_op | source)
XLA Modules:
  0.0 31.9 jit_solution(16222376065579463243)
XLA Ops:
  0.6 1.8 %shard_map.111 = bf16[640,128]{1,0:T(8,128)(2,1)} custom-call(bf16[256,128]{1,0:T(8,128)(2,1)} %inputs.1, bf16[256,128]{1,0:T(8,128)(2,1)} %out_grad.1, f32[128,256]{1,0:T(8,128)} %bitcast.20, f32[1,256]{1,0:T(1,128)} %bitcast.21), custom_call_target="tpu_custom_call" | custom-call | tf_op jit(solution)/shard_map/pallas_call | solution.py:721
  2.4 0.0 copy-start
  2.4 0.0 copy-start.1
  2.4 7.3 %all-to-all-start = ((bf16[32,10,2,128]{3,2,1,0:T(2,128)(2,1)}), bf16[32,10,2,128]{3,2,1,0:T(2,128)(2,1)S(1)}, u32[]{:S(2)}, u32[]{:S(2)}) async-start(bf16[32,10,2,128]{3,2,1,0:T(2,128)(2,1)} %bitcast.17), calls=%async_computation | async-start | bytes 327680 | tf_op jit(solution)/shard_map/all_to_all | solution.py:717
  9.8 0.0 copy-start.2
  9.8 0.0 copy-start.3
  9.8 0.0 copy-done
  9.8 0.0 copy-done.1
  9.8 0.6 %copy-done.2 = f32[64]{0:T(128)S(1)} copy-done((f32[64]{0:T(128)S(1)}, f32[64]{0:T(128)}, u32[]{:S(2)}) %copy-start.2) | copy-done | bytes 280
  10.4 0.0 copy-done.3
  10.5 7.9 %all-to-all-done = bf16[32,10,2,128]{3,2,1,0:T(2,128)(2,1)S(1)} async-done(((bf16[32,10,2,128]{3,2,1,0:T(2,128)(2,1)}), bf16[32,10,2,128]{3,2,1,0:T(2,128)(2,1)S(1)}, u32[]{:S(2)}, u32[]{:S(2)}) %all-to-all-start) | async-done | bytes 163872 | tf_op jit(solution)/shard_map/all_to_all | solution.py:717
  18.3 2.0 %shard_map.113 = f32[640,128]{1,0:T(8,128)S(1)} custom-call(bf16[640,128]{1,0:T(8,128)(2,1)S(1)} %bitcast.14, bf16[2,256,256]{2,1,0:T(8,128)(2,1)S(1)} %get-tuple-element.12.matrix, f32[9,4,128]{2,1,0:T(4,128)S(1)} %get-tuple-element.13.twiddle, f32[1,64]{1,0:T(1,128)S(1)} %get-tuple-element.14.decay_log, f32[1,64]{1,0:T(1,128)S(1)} %get-tuple-element.15.rotation), custom_call_target="tpu_custom_call" | custom-call | tf_op jit(solution)/shard_map/pallas_call | solution.py:747
  20.3 10.7 %all_to_all.10 = f16[32,10,2,128]{3,2,1,0:T(2,128)(2,1)S(1)} all-to-all(f16[32,10,2,128]{3,2,1,0:T(2,128)(2,1)S(1)} %bitcast.18), channel_id=1, replica_groups=mesh['seq'=8,'ch'=4] {'seq','ch'}, dimensions={0} | all-to-all | bytes 327680 | tf_op jit(solution)/shard_map/all_to_all | solution.py:717
  31.1 0.9 %shard_map.114 = (f32[256,128]{1,0:T(8,128)}, f32[128,256]{1,0:T(8,128)}, f32[256]{0:T(256)}, f32[2,64]{1,0:T(2,128)}) custom-call(f32[640,128]{1,0:T(8,128)S(1)} %convert.1.got), custom_call_target="tpu_custom_call" | custom-call | tf_op jit(solution)/shard_map/pallas_call | solution.py:767
  (3 shorter events, 0.1 us)
Async XLA Ops:
  2.4 7.4 %copy-start = (bf16[2,256,256]{2,1,0:T(8,128)(2,1)S(1)}, bf16[2,256,256]{2,1,0:T(8,128)(2,1)}, u32[]{:S(2)}) copy-start(bf16[2,256,256]{2,1,0:T(8,128)(2,1)} %constant.4.clone.refs_0_) | copy-start | bytes 786436
  2.4 7.4 %copy-start.1 = (f32[9,4,128]{2,1,0:T(4,128)S(1)}, f32[9,4,128]{2,1,0:T(4,128)}, u32[]{:S(2)}) copy-start(f32[9,4,128]{2,1,0:T(4,128)} %constant.5.clone.refs_1_) | copy-start | bytes 55300
  2.4 15.9 %all-to-all-start = ((bf16[32,10,2,128]{3,2,1,0:T(2,128)(2,1)}), bf16[32,10,2,128]{3,2,1,0:T(2,128)(2,1)S(1)}, u32[]{:S(2)}, u32[]{:S(2)}) async-start(bf16[32,10,2,128]{3,2,1,0:T(2,128)(2,1)} %bitcast.17), calls=%async_computation | async-start | bytes 327680 | tf_op jit(solution)/shard_map/all_to_all | solution.py:717
  9.8 0.7 %copy-start.2 = (f32[64]{0:T(128)S(1)}, f32[64]{0:T(128)}, u32[]{:S(2)}) copy-start(f32[64]{0:T(128)} %param.12) | copy-start | bytes 772
  9.8 0.7 %copy-start.3 = (f32[64]{0:T(128)S(1)}, f32[64]{0:T(128)}, u32[]{:S(2)}) copy-start(f32[64]{0:T(128)} %param.13) | copy-start | bytes 772

commit v7 on v6

--- a/solution.py
+++ b/solution.py
@@ -405,7 +405,6 @@
     pairs = part_count // 2
     half = pairs // SUBLANES
     reach = length // 2
-    device = lax.axis_index("seq") * groups + lax.axis_index("ch")
     lane = lax.broadcasted_iota(jnp.int32, (pairs, LANES), 1)
     left = lane < LANES // 2
     row = lax.broadcasted_iota(jnp.int32, (SUBLANES, LANES), 0)
@@ -418,7 +417,7 @@
 
     def collect(spot):
         tiles = [
-            rows_in[pl.ds(group * ROWS + spot, owners, stride=groups * ROWS), :]
+            rows_in[pl.ds(group * owners * ROWS + spot, owners, stride=ROWS), :]
             for group in range(groups)
         ]
         return jnp.concatenate(tiles[:half], axis=0), jnp.concatenate(tiles[half:], axis=0)
@@ -498,7 +497,7 @@
         rows_in[...] = got[...].astype(jnp.float32)
         blocks = []
         for s in range(owners):
-            spots = [(s * groups + group) * ROWS for group in range(groups)]
+            spots = [(group * owners + s) * ROWS for group in range(groups)]
             blocks.append(
                 jnp.concatenate(
                     [rows_in[spot : spot + SUBLANES] for spot in spots]
@@ -561,7 +560,7 @@
         lag_scale = jnp.exp2(-lag_exponent)
         for b, block in enumerate(blocks):
             for group in range(groups):
-                place = (b * groups + group) * ROWS
+                place = (group * owners + b) * ROWS
                 value = block[group * SUBLANES : (group + 1) * SUBLANES]
                 sent[place + LAGS : place + GRADS] = value * lag_scale
 
@@ -655,7 +654,7 @@
             tails.append(jnp.concatenate([state_high, state_low, singles, singles], axis=0))
         for b in range(owners):
             for group in range(groups):
-                place = (b * groups + group) * ROWS
+                place = (group * owners + b) * ROWS
                 sent[place + GRADS : place + STATE] = grads[
                     group * SUBLANES : (group + 1) * SUBLANES
                 ]
@@ -714,7 +713,7 @@
 
     def exchange(value):
         value = value.reshape(peers, ROWS // 2, 2, LANES)
-        value = lax.all_to_all(value, ("seq", "ch"), split_axis=0, concat_axis=0, tiled=True)
+        value = lax.all_to_all(value, ("ch", "seq"), split_axis=0, concat_axis=0, tiled=True)
         return value.reshape(peers * ROWS, LANES)
 
     anywhere = pl.BlockSpec(memory_space=pl.ANY)

time: 32.2 us -> 31.5 us (0.978)
  waiting for transfers between devices: 7.87 us -> 7.22 us
    all_to_all x1, waiting for transfers between devices: 7.87 us -> 7.22 us  [exchange(): lax.all_to_all(value, ('ch', 'seq'), split_axis=0, concat_axis=0, tiled=T...]
where the time goes in v7:
time: 31.5 us; the launch traced here: 31.2 us
  blocking collectives  10.7 us (34%)
  starting transfers between devices  7.3 us (23%)
  waiting for transfers between devices  7.22 us (23%)
  Pallas kernels  4.59 us (15%)
  between operations  0.72 us (2%)
  local copies, waits for them, and re-layouts  0.65 us (2%)
    all_to_all x1, blocking collectives, exchange(): lax.all_to_all(value, ('ch', 'seq'), split_axis=0, concat_axis=0, tiled=T...  10.7 us
    all_to_all x1, starting transfers between devices, exchange(): lax.all_to_all(value, ('ch', 'seq'), split_axis=0, concat_axis=0, tiled=T...  7.3 us
    all_to_all x1, waiting for transfers between devices, exchange(): lax.all_to_all(value, ('ch', 'seq'), split_axis=0, concat_axis=0, tiled=T...  7.22 us
    pallas_call x1, Pallas kernels, kernel_device(): pl.pallas_call(functools.partial(main_kernel, owners, norm_scale), out_sh...  1.93 us
    pallas_call x1, Pallas kernels, kernel_device(): pl.pallas_call(pack_kernel, out_shape=jax.ShapeDtypeStruct((peers * ROWS,...  1.78 us
    pallas_call x1, Pallas kernels, kernel_device(): pl.pallas_call(unpack_kernel, out_shape=[jax.ShapeDtypeStruct((channels,...  0.85 us
    unnamed x8, local copies, waits for them, and re-layouts  0.65 us
  transfers between devices with their start and end apart: 1, of which 1 were waited for; matrix products, arithmetic and copies ran while one was open for 0% of the time, Pallas kernels for 0%

profile of v7, /device:TPU:0, one launch (start us, length us, event | category | flops | bytes accessed | tf_op | source)
XLA Modules:
  0.0 31.2 jit_solution(9598888233081416238)
XLA Ops:
  0.6 1.8 %shard_map.111 = bf16[640,128]{1,0:T(8,128)(2,1)} custom-call(bf16[256,128]{1,0:T(8,128)(2,1)} %inputs.1, bf16[256,128]{1,0:T(8,128)(2,1)} %out_grad.1, f32[128,256]{1,0:T(8,128)} %bitcast.20, f32[1,256]{1,0:T(1,128)} %bitcast.21), custom_call_target="tpu_custom_call" | custom-call | tf_op jit(solution)/shard_map/pallas_call | solution.py:720
  2.4 0.0 copy-start
  2.4 0.0 copy-start.1
  2.4 7.3 %all-to-all-start = ((bf16[32,10,2,128]{3,2,1,0:T(2,128)(2,1)}), bf16[32,10,2,128]{3,2,1,0:T(2,128)(2,1)S(1)}, u32[]{:S(2)}, u32[]{:S(2)}) async-start(bf16[32,10,2,128]{3,2,1,0:T(2,128)(2,1)} %bitcast.17), calls=%async_computation | async-start | bytes 327680 | tf_op jit(solution)/shard_map/all_to_all | solution.py:716
  9.8 0.0 copy-start.2
  9.8 0.0 copy-start.3
  9.8 0.0 copy-done
  9.8 0.0 copy-done.1
  9.8 0.6 %copy-done.2 = f32[64]{0:T(128)S(1)} copy-done((f32[64]{0:T(128)S(1)}, f32[64]{0:T(128)}, u32[]{:S(2)}) %copy-start.2) | copy-done | bytes 280
  10.4 0.0 copy-done.3
  10.5 7.2 %all-to-all-done = bf16[32,10,2,128]{3,2,1,0:T(2,128)(2,1)S(1)} async-done(((bf16[32,10,2,128]{3,2,1,0:T(2,128)(2,1)}), bf16[32,10,2,128]{3,2,1,0:T(2,128)(2,1)S(1)}, u32[]{:S(2)}, u32[]{:S(2)}) %all-to-all-start) | async-done | bytes 163872 | tf_op jit(solution)/shard_map/all_to_all | solution.py:716
  17.7 1.9 %shard_map.113 = f32[640,128]{1,0:T(8,128)S(1)} custom-call(bf16[640,128]{1,0:T(8,128)(2,1)S(1)} %bitcast.14, bf16[2,256,256]{2,1,0:T(8,128)(2,1)S(1)} %get-tuple-element.12.matrix, f32[9,4,128]{2,1,0:T(4,128)S(1)} %get-tuple-element.13.twiddle, f32[1,64]{1,0:T(1,128)S(1)} %get-tuple-element.14.decay_log, f32[1,64]{1,0:T(1,128)S(1)} %get-tuple-element.15.rotation), custom_call_target="tpu_custom_call" | custom-call | tf_op jit(solution)/shard_map/pallas_call | solution.py:746
  19.6 10.7 %all_to_all.10 = f16[32,10,2,128]{3,2,1,0:T(2,128)(2,1)S(1)} all-to-all(f16[32,10,2,128]{3,2,1,0:T(2,128)(2,1)S(1)} %bitcast.18), channel_id=1, replica_groups=mesh['seq'=8,'ch'=4] {'ch','seq'}, dimensions={0} | all-to-all | bytes 327680 | tf_op jit(solution)/shard_map/all_to_all | solution.py:716
  30.4 0.9 %shard_map.114 = (f32[256,128]{1,0:T(8,128)}, f32[128,256]{1,0:T(8,128)}, f32[256]{0:T(256)}, f32[2,64]{1,0:T(2,128)}) custom-call(f32[640,128]{1,0:T(8,128)S(1)} %convert.1.got), custom_call_target="tpu_custom_call" | custom-call | tf_op jit(solution)/shard_map/pallas_call | solution.py:766
  (3 shorter events, 0.1 us)
Async XLA Ops:
  2.4 7.4 %copy-start = (bf16[2,256,256]{2,1,0:T(8,128)(2,1)S(1)}, bf16[2,256,256]{2,1,0:T(8,128)(2,1)}, u32[]{:S(2)}) copy-start(bf16[2,256,256]{2,1,0:T(8,128)(2,1)} %constant.4.clone.refs_0_) | copy-start | bytes 786436
  2.4 7.4 %copy-start.1 = (f32[9,4,128]{2,1,0:T(4,128)S(1)}, f32[9,4,128]{2,1,0:T(4,128)}, u32[]{:S(2)}) copy-start(f32[9,4,128]{2,1,0:T(4,128)} %constant.5.clone.refs_1_) | copy-start | bytes 55300
  2.4 15.2 %all-to-all-start = ((bf16[32,10,2,128]{3,2,1,0:T(2,128)(2,1)}), bf16[32,10,2,128]{3,2,1,0:T(2,128)(2,1)S(1)}, u32[]{:S(2)}, u32[]{:S(2)}) async-start(bf16[32,10,2,128]{3,2,1,0:T(2,128)(2,1)} %bitcast.17), calls=%async_computation | async-start | bytes 327680 | tf_op jit(solution)/shard_map/all_to_all | solution.py:716
  9.8 0.7 %copy-start.2 = (f32[64]{0:T(128)S(1)}, f32[64]{0:T(128)}, u32[]{:S(2)}) copy-start(f32[64]{0:T(128)} %param.12) | copy-start | bytes 772
  9.8 0.7 %copy-start.3 = (f32[64]{0:T(128)S(1)}, f32[64]{0:T(128)}, u32[]{:S(2)}) copy-start(f32[64]{0:T(128)} %param.13) | copy-start | bytes 772

commit v8 on v7

--- a/solution.py
+++ b/solution.py
@@ -324,12 +324,21 @@
 PARTS = 4
 
 
-def pack_kernel(inputs, out_grad, readout, log_step, out, signals, read, step, turned, rows, sems):
+def pack_kernel(inputs, out_grad, readout, log_step, *refs):
+    count = (len(refs) - 7) // 2
+    sources, (out, *held) = refs[:count], refs[count : 2 * count + 1]
+    signals, read, step, turned, rows, sems = refs[2 * count + 1 :]
     peers = out.shape[0] // ROWS
     copies = [
         pltpu.make_async_copy(source, target, sems.at[i])
         for i, (source, target) in enumerate(
-            ((readout, read), (log_step, step), (inputs, signals.at[0]), (out_grad, signals.at[1]))
+            (
+                (readout, read),
+                (log_step, step),
+                (inputs, signals.at[0]),
+                (out_grad, signals.at[1]),
+                *zip(sources, held),
+            )
         )
     ]
     for copy in copies:
@@ -354,11 +363,8 @@
             spot = peer * ROWS + place * SUBLANES
             rows[spot : spot + SUBLANES] = value[peer * SUBLANES : (peer + 1) * SUBLANES]
     out[...] = rows[...].astype(jnp.bfloat16)
-
-
-def hold_kernel(*refs):
-    for source, target in zip(refs[: len(refs) // 2], refs[len(refs) // 2 :]):
-        target[...] = source[...]
+    for copy in copies[4:]:
+        copy.wait()
 
 
 def exponent_of(bound):
@@ -717,32 +723,28 @@
         return value.reshape(peers * ROWS, LANES)
 
     anywhere = pl.BlockSpec(memory_space=pl.ANY)
-    pieces = pl.pallas_call(
+    held = [jnp.asarray(table) for table in transform_tables(owners, length, norm_scale)]
+    held += [decay_log[None], rotation[None]]
+    sources = (
+        inputs, out_grad, readout.transpose(0, 2, 1).reshape(LANES, channels), log_step[None], *held
+    )
+    pieces, *held = pl.pallas_call(
         pack_kernel,
-        out_shape=jax.ShapeDtypeStruct((peers * ROWS, LANES), bf16),
-        in_specs=[anywhere] * 4,
-        out_specs=vmem,
+        out_shape=[jax.ShapeDtypeStruct((peers * ROWS, LANES), bf16)]
+        + [jax.ShapeDtypeStruct(value.shape, value.dtype) for value in held],
+        in_specs=[anywhere] * len(sources),
+        out_specs=[vmem] * (1 + len(held)),
         scratch_shapes=[
             pltpu.VMEM((2, channels, LANES), bf16),
             pltpu.VMEM((LANES, channels), f32),
             pltpu.VMEM((1, channels), f32),
             pltpu.VMEM((2, channels, LANES), f32),
             pltpu.VMEM((peers * ROWS, LANES), f32),
-            pltpu.SemaphoreType.DMA((4,)),
+            pltpu.SemaphoreType.DMA((len(sources),)),
         ],
-        compiler_params=pltpu.CompilerParams(vmem_limit_bytes=60 * 1024 * 1024),
-    )(inputs, out_grad, readout.transpose(0, 2, 1).reshape(LANES, channels), log_step[None])
+        compiler_params=memory,
+    )(*(pltpu.with_memory_space_constraint(value, pltpu.HBM) for value in sources))
     got = exchange(pieces)
-
-    held = [jnp.asarray(table) for table in transform_tables(owners, length, norm_scale)]
-    held += [decay_log[None], rotation[None]]
-    held = pl.pallas_call(
-        hold_kernel,
-        out_shape=[jax.ShapeDtypeStruct(value.shape, value.dtype) for value in held],
-        in_specs=[vmem] * 4,
-        out_specs=[vmem] * 4,
-        compiler_params=memory,
-    )(*held)
     sent = pl.pallas_call(
         functools.partial(main_kernel, owners, norm_scale),
         out_shape=jax.ShapeDtypeStruct((peers * ROWS, LANES), f32),

time: 31.5 us -> 30.6 us (0.971)
  blocking collectives: 10.7 us -> 25.7 us
  starting transfers between devices: 7.3 us -> 0 us
  waiting for transfers between devices: 7.22 us -> 0 us
  local copies, waits for them, and re-layouts: 0.65 us -> 0 us
  Pallas kernels: 4.59 us -> 3.98 us
    all_to_all x1 -> x2, blocking collectives: 10.7 us -> 25.7 us  [exchange(): lax.all_to_all(value, ('ch', 'seq'), split_axis=0, concat_axis=0, tiled=T...]
    all_to_all x1 -> x0, starting transfers between devices: 7.3 us -> none  [exchange(): lax.all_to_all(value, ('ch', 'seq'), split_axis=0, concat_axis=0, tiled=T...]
    all_to_all x1 -> x0, waiting for transfers between devices: 7.22 us -> none  [exchange(): lax.all_to_all(value, ('ch', 'seq'), split_axis=0, concat_axis=0, tiled=T...]
    unnamed x8 -> x0, local copies, waits for them, and re-layouts: 0.65 us -> none
    pallas_call x2 -> x1, Pallas kernels: 1.8 us -> 1.18 us  [kernel_device(): pl.pallas_call(pack_kernel, out_shape=[jax.ShapeDtypeStruct((peers * ROWS...]
  transfers between devices with their start and end apart: 1 -> 0, of which waited for: 1 -> 0; matrix products, arithmetic and copies ran while one was open for 0% -> 0% of each run, Pallas kernels for 0% -> 0%
where the time goes in v8:
time: 30.6 us; the launch traced here: 30.4 us
  blocking collectives  25.7 us (84%)
  Pallas kernels  3.98 us (13%)
  between operations  0.66 us (2%)
    all_to_all x2, blocking collectives, exchange(): lax.all_to_all(value, ('ch', 'seq'), split_axis=0, concat_axis=0, tiled=T...  25.7 us
    pallas_call x1, Pallas kernels, kernel_device(): pl.pallas_call(functools.partial(main_kernel, owners, norm_scale), out_sh...  1.95 us
    pallas_call x1, Pallas kernels, kernel_device(): pl.pallas_call(pack_kernel, out_shape=[jax.ShapeDtypeStruct((peers * ROWS...  1.18 us
    pallas_call x1, Pallas kernels, kernel_device(): pl.pallas_call(unpack_kernel, out_shape=[jax.ShapeDtypeStruct((channels,...  0.85 us

profile of v8, /device:TPU:0, one launch (start us, length us, event | category | flops | bytes accessed | tf_op | source)
XLA Modules:
  0.0 30.4 jit_solution(4416752910463823091)
XLA Ops:
  0.6 1.2 %shard_map.111 = (bf16[640,128]{1,0:T(8,128)(2,1)S(1)}, bf16[2,256,256]{2,1,0:T(8,128)(2,1)S(1)}, f32[9,4,128]{2,1,0:T(4,128)S(1)}, f32[1,64]{1,0:T(1,128)S(1)}, f32[1,64]{1,0:T(1,128)S(1)}) custom-call(bf16[256,128]{1,0:T(8,128)(2,1)} %inputs.1, bf16[256,128]{1,0:T(8,128)(2,1)} %out_grad.1, f32[128,256]{1,0:T(8,128)} %bitcast.18, f32[1,256]{1,0:T(1,128)} %bitcast.19, ...), custom_call_target="tpu_custom_call" | custom-call | tf_op jit(solution)/shard_map/pallas_call | solution.py:731
  1.8 15.0 %all_to_all.10 = bf16[32,10,2,128]{3,2,1,0:T(2,128)(2,1)S(1)} all-to-all(bf16[32,10,2,128]{3,2,1,0:T(2,128)(2,1)S(1)} %bitcast.15), channel_id=1, replica_groups=mesh['seq'=8,'ch'=4] {'ch','seq'}, dimensions={0} | all-to-all | bytes 327680 | tf_op jit(solution)/shard_map/all_to_all | solution.py:722
  16.8 2.0 %shard_map.112 = f32[640,128]{1,0:T(8,128)S(1)} custom-call(bf16[640,128]{1,0:T(8,128)(2,1)S(1)} %bitcast.14, bf16[2,256,256]{2,1,0:T(8,128)(2,1)S(1)} %get-tuple-element.14.matrix, f32[9,4,128]{2,1,0:T(4,128)S(1)} %get-tuple-element.15.twiddle, f32[1,64]{1,0:T(1,128)S(1)} %get-tuple-element.16.decay_log, f32[1,64]{1,0:T(1,128)S(1)} %get-tuple-element.17.rotation), custom_call_target="tpu_custom_call" | custom-call | tf_op jit(solution)/shard_map/pallas_call | solution.py:748
  18.8 10.7 %all_to_all.11 = f16[32,10,2,128]{3,2,1,0:T(2,128)(2,1)S(1)} all-to-all(f16[32,10,2,128]{3,2,1,0:T(2,128)(2,1)S(1)} %bitcast.16), channel_id=1, replica_groups=mesh['seq'=8,'ch'=4] {'ch','seq'}, dimensions={0} | all-to-all | bytes 327680 | tf_op jit(solution)/shard_map/all_to_all | solution.py:722
  29.6 0.9 %shard_map.113 = (f32[256,128]{1,0:T(8,128)}, f32[128,256]{1,0:T(8,128)}, f32[256]{0:T(256)}, f32[2,64]{1,0:T(2,128)}) custom-call(f32[640,128]{1,0:T(8,128)S(1)} %convert.1.got), custom_call_target="tpu_custom_call" | custom-call | tf_op jit(solution)/shard_map/pallas_call | solution.py:768
  (2 shorter events, 0.0 us)

commit v9 on v8

--- a/solution.py
+++ b/solution.py
@@ -322,6 +322,7 @@
 STEP_LANES, SCALE_LANES = (0, 8), (16, 17, 18, 19)
 SPARE = 15.0
 PARTS = 4
+FRESH = 4
 
 
 def pack_kernel(inputs, out_grad, readout, log_step, *refs):
@@ -343,25 +344,26 @@
     ]
     for copy in copies:
         copy.start()
-    copies[0].wait()
-    copies[1].wait()
+    for copy in copies[:4]:
+        copy.wait()
     own = lax.axis_index("seq")
-    turned[0] = transposed(read[...])
-    turned[1] = transposed(jnp.broadcast_to(step[...], (LANES, step.shape[1])))
-    for place, value in enumerate(
-        three_pieces(turned[0, pl.ds(own, peers, stride=SUBLANES), :])
-    ):
+    turned[...] = transposed(read[...])
+    channels = step.shape[1]
+    peer = lax.broadcasted_iota(jnp.int32, (peers, channels), 0)
+    channel = lax.broadcasted_iota(jnp.int32, (peers, channels), 1)
+    mine = jnp.where(channel == peer * SUBLANES + own, step[...], 0.0)
+    mine = jnp.broadcast_to(jnp.sum(mine, axis=1, keepdims=True), (peers, LANES))
+    for place, signal in enumerate((signals[0], signals[1])):
+        value = signal.astype(jnp.float32)
+        for peer in range(peers):
+            spot = peer * ROWS + place * SUBLANES
+            rows[spot : spot + SUBLANES] = value[peer * SUBLANES : (peer + 1) * SUBLANES]
+    for place, value in enumerate(three_pieces(turned[pl.ds(own, peers, stride=SUBLANES), :])):
         rows[pl.ds(READ + place, peers, stride=ROWS), :] = value
-    pieces = three_pieces(turned[1, pl.ds(own, peers, stride=SUBLANES), :])
+    pieces = three_pieces(mine)
     lane = lax.broadcasted_iota(jnp.int32, (peers, LANES), 1)
     value = jnp.where(lane == 0, pieces[0], jnp.where(lane == 1, pieces[1], pieces[2]))
     rows[pl.ds(STEP, peers, stride=ROWS), :] = value
-    for place in range(2):
-        copies[2 + place].wait()
-        value = signals[place].astype(jnp.float32)
-        for peer in range(peers):
-            spot = peer * ROWS + place * SUBLANES
-            rows[spot : spot + SUBLANES] = value[peer * SUBLANES : (peer + 1) * SUBLANES]
     out[...] = rows[...].astype(jnp.bfloat16)
     for copy in copies[4:]:
         copy.wait()
@@ -445,7 +447,11 @@
         rate = (step * pole[0], step * pole[1])
         place, size = 0, 1
         while size < owners * length:
-            doubled[place], doubled[place + 1] = power(rate[0], rate[1], float(size))
+            if place // 2 % FRESH == 0:
+                value = power(rate[0], rate[1], float(size))
+            else:
+                value = (value[0] * value[0] - value[1] * value[1], 2.0 * value[0] * value[1])
+            doubled[place], doubled[place + 1] = value
             place, size = place + 2, size * 2
         sine = cos_sin(0.5 * rate[1])[1]
         cosine = 1.0 - 2.0 * sine * sine
@@ -636,13 +642,11 @@
         lower = jnp.where(left, on_read[0], swap(on_read[1]))
         upper = jnp.where(left, swap(on_read[0]), on_read[1])
         grads = jnp.concatenate([lower, upper], axis=0)
-        step_column = jnp.concatenate(
-            [
-                jnp.sum(jnp.where(left, on_step, 0.0), axis=1, keepdims=True),
-                jnp.sum(jnp.where(left, 0.0, on_step), axis=1, keepdims=True),
-            ],
-            axis=0,
-        ) * jnp.exp2(-step_exponent)
+        step_scale = jnp.broadcast_to(jnp.exp2(-step_exponent), (pairs, LANES))
+        step_columns = [
+            jnp.broadcast_to(jnp.sum(value, axis=1, keepdims=True), (pairs, LANES)) * step_scale
+            for value in (jnp.where(left, on_step, 0.0), jnp.where(left, 0.0, on_step))
+        ]
         place_lane = lax.broadcasted_iota(jnp.int32, (SUBLANES, LANES), 1)
         scales = jnp.zeros((1, LANES), jnp.float32)
         for spot, value in zip(
@@ -652,7 +656,8 @@
         state_high, state_low = two_pieces(state)
         tails = []
         for group in range(groups):
-            pieces = two_pieces(step_column[group * SUBLANES : (group + 1) * SUBLANES])
+            spot = group % half * SUBLANES
+            pieces = two_pieces(step_columns[group // half][spot : spot + SUBLANES])
             spread = jnp.zeros((SUBLANES, LANES), jnp.float32)
             for spot, piece in zip(STEP_LANES, pieces):
                 spread = jnp.where(place_lane == row + spot, piece, spread)
@@ -738,7 +743,7 @@
             pltpu.VMEM((2, channels, LANES), bf16),
             pltpu.VMEM((LANES, channels), f32),
             pltpu.VMEM((1, channels), f32),
-            pltpu.VMEM((2, channels, LANES), f32),
+            pltpu.VMEM((channels, LANES), f32),
             pltpu.VMEM((peers * ROWS, LANES), f32),
             pltpu.SemaphoreType.DMA((len(sources),)),
         ],

time: 30.6 us -> 30.5 us (level)
  no operation moved by 1% of the time
where the time goes in v9:
time: 30.5 us; the launch traced here: 30.3 us
  blocking collectives  25.7 us (84%)
  Pallas kernels  3.86 us (13%)
  between operations  0.66 us (2%)
    all_to_all x2, blocking collectives, exchange(): lax.all_to_all(value, ('ch', 'seq'), split_axis=0, concat_axis=0, tiled=T...  25.7 us
    pallas_call x1, Pallas kernels, kernel_device(): pl.pallas_call(functools.partial(main_kernel, owners, norm_scale), out_sh...  1.83 us
    pallas_call x1, Pallas kernels, kernel_device(): pl.pallas_call(pack_kernel, out_shape=[jax.ShapeDtypeStruct((peers * ROWS...  1.19 us
    pallas_call x1, Pallas kernels, kernel_device(): pl.pallas_call(unpack_kernel, out_shape=[jax.ShapeDtypeStruct((channels,...  0.85 us

profile of v9, /device:TPU:0, one launch (start us, length us, event | category | flops | bytes accessed | tf_op | source)
XLA Modules:
  0.0 30.3 jit_solution(5326395084189814524)
XLA Ops:
  0.6 1.2 %shard_map.111 = (bf16[640,128]{1,0:T(8,128)(2,1)S(1)}, bf16[2,256,256]{2,1,0:T(8,128)(2,1)S(1)}, f32[9,4,128]{2,1,0:T(4,128)S(1)}, f32[1,64]{1,0:T(1,128)S(1)}, f32[1,64]{1,0:T(1,128)S(1)}) custom-call(bf16[256,128]{1,0:T(8,128)(2,1)} %inputs.1, bf16[256,128]{1,0:T(8,128)(2,1)} %out_grad.1, f32[128,256]{1,0:T(8,128)} %bitcast.18, f32[1,256]{1,0:T(1,128)} %bitcast.19, ...), custom_call_target="tpu_custom_call" | custom-call | tf_op jit(solution)/shard_map/pallas_call | solution.py:736
  1.8 15.0 %all_to_all.10 = bf16[32,10,2,128]{3,2,1,0:T(2,128)(2,1)S(1)} all-to-all(bf16[32,10,2,128]{3,2,1,0:T(2,128)(2,1)S(1)} %bitcast.15), channel_id=1, replica_groups=mesh['seq'=8,'ch'=4] {'ch','seq'}, dimensions={0} | all-to-all | bytes 327680 | tf_op jit(solution)/shard_map/all_to_all | solution.py:727
  16.8 1.8 %shard_map.112 = f32[640,128]{1,0:T(8,128)S(1)} custom-call(bf16[640,128]{1,0:T(8,128)(2,1)S(1)} %bitcast.14, bf16[2,256,256]{2,1,0:T(8,128)(2,1)S(1)} %get-tuple-element.14.matrix, f32[9,4,128]{2,1,0:T(4,128)S(1)} %get-tuple-element.15.twiddle, f32[1,64]{1,0:T(1,128)S(1)} %get-tuple-element.16.decay_log, f32[1,64]{1,0:T(1,128)S(1)} %get-tuple-element.17.rotation), custom_call_target="tpu_custom_call" | custom-call | tf_op jit(solution)/shard_map/pallas_call | solution.py:753
  18.7 10.7 %all_to_all.11 = f16[32,10,2,128]{3,2,1,0:T(2,128)(2,1)S(1)} all-to-all(f16[32,10,2,128]{3,2,1,0:T(2,128)(2,1)S(1)} %bitcast.16), channel_id=1, replica_groups=mesh['seq'=8,'ch'=4] {'ch','seq'}, dimensions={0} | all-to-all | bytes 327680 | tf_op jit(solution)/shard_map/all_to_all | solution.py:727
  29.4 0.9 %shard_map.113 = (f32[256,128]{1,0:T(8,128)}, f32[128,256]{1,0:T(8,128)}, f32[256]{0:T(256)}, f32[2,64]{1,0:T(2,128)}) custom-call(f32[640,128]{1,0:T(8,128)S(1)} %convert.1.got), custom_call_target="tpu_custom_call" | custom-call | tf_op jit(solution)/shard_map/pallas_call | solution.py:773
  (2 shorter events, 0.0 us)

commit v10 on v9

--- a/solution.py
+++ b/solution.py
@@ -311,13 +311,45 @@
     return pieces
 
 
+def swap(value):
+    return pltpu.roll(value, LANES // 2, 1)
+
+
+def rest_lanes(lane):
+    return lane < 3, (lane >= LANES // 2) & (lane < LANES // 2 + 3)
+
+
+def pack_rests(high, rest, pieces):
+    lane = lax.broadcasted_iota(jnp.int32, high.shape, 1)
+    shared, replaced = rest_lanes(lane)
+    steps = jnp.where(high == 0.0, 0.0, rest / jnp.where(high == 0.0, 1.0, high))
+    steps = jnp.floor(steps * (256.0 * REST_STEPS) + 0.5)
+    rest = jnp.where(shared, steps * (2.0 * REST_STEPS + 1.0) + swap(steps), rest)
+    for i, piece in enumerate(pieces):
+        rest = jnp.where(lane == LANES // 2 + i, piece, rest)
+    return rest
+
+
+def unpack_rests(high, rest):
+    lane = lax.broadcasted_iota(jnp.int32, high.shape, 1)
+    shared, replaced = rest_lanes(lane)
+    step = sum(rest[:, LANES // 2 + i : LANES // 2 + i + 1] for i in range(3))
+    both = jnp.where(shared, rest, swap(rest))
+    first = jnp.floor(both * (1.0 / (2.0 * REST_STEPS + 1.0)) + 0.5)
+    second = both - first * (2.0 * REST_STEPS + 1.0)
+    steps = jnp.where(shared, first, second) * (1.0 / (256.0 * REST_STEPS))
+    return jnp.where(shared | replaced, high * steps, rest), jnp.broadcast_to(step, high.shape)
+
+
 def transposed(value):
     return jnp.concatenate(
         [value[:, spot : spot + LANES].T for spot in range(0, value.shape[1], LANES)], axis=0
     )
 
 
-READ, STEP, ROWS = 16, 19, 20
+READ, REST, OUT_ROWS = 16, 17, 18
+REST_STEPS = 7.0
+ROWS = 20
 LAGS, GRADS, STATE, SINGLES = 0, 8, 16, 18
 STEP_LANES, SCALE_LANES = (0, 8), (16, 17, 18, 19)
 SPARE = 15.0
@@ -329,7 +361,7 @@
     count = (len(refs) - 7) // 2
     sources, (out, *held) = refs[:count], refs[count : 2 * count + 1]
     signals, read, step, turned, rows, sems = refs[2 * count + 1 :]
-    peers = out.shape[0] // ROWS
+    peers = out.shape[0] // OUT_ROWS
     copies = [
         pltpu.make_async_copy(source, target, sems.at[i])
         for i, (source, target) in enumerate(
@@ -356,14 +388,12 @@
     for place, signal in enumerate((signals[0], signals[1])):
         value = signal.astype(jnp.float32)
         for peer in range(peers):
-            spot = peer * ROWS + place * SUBLANES
+            spot = peer * OUT_ROWS + place * SUBLANES
             rows[spot : spot + SUBLANES] = value[peer * SUBLANES : (peer + 1) * SUBLANES]
-    for place, value in enumerate(three_pieces(turned[pl.ds(own, peers, stride=SUBLANES), :])):
-        rows[pl.ds(READ + place, peers, stride=ROWS), :] = value
-    pieces = three_pieces(mine)
-    lane = lax.broadcasted_iota(jnp.int32, (peers, LANES), 1)
-    value = jnp.where(lane == 0, pieces[0], jnp.where(lane == 1, pieces[1], pieces[2]))
-    rows[pl.ds(STEP, peers, stride=ROWS), :] = value
+    value = turned[pl.ds(own, peers, stride=SUBLANES), :]
+    high = value.astype(jnp.bfloat16).astype(jnp.float32)
+    rows[pl.ds(READ, peers, stride=OUT_ROWS), :] = high
+    rows[pl.ds(REST, peers, stride=OUT_ROWS), :] = pack_rests(high, value - high, three_pieces(mine))
     out[...] = rows[...].astype(jnp.bfloat16)
     for copy in copies[4:]:
         copy.wait()
@@ -406,7 +436,7 @@
     lags,
     sums,
 ):
-    peers, length = got.shape[0] // ROWS, got.shape[1]
+    peers, length = got.shape[0] // OUT_ROWS, got.shape[1]
     groups = peers // owners
     part_count = groups * SUBLANES
     rows = 2 * part_count
@@ -417,27 +447,24 @@
     left = lane < LANES // 2
     row = lax.broadcasted_iota(jnp.int32, (SUBLANES, LANES), 0)
 
-    def swap(value):
-        return pltpu.roll(value, LANES // 2, 1)
-
     def lanes_of(side):
         return slice(side * LANES, (side + 1) * LANES)
 
     def collect(spot):
         tiles = [
-            rows_in[pl.ds(group * owners * ROWS + spot, owners, stride=ROWS), :]
+            rows_in[pl.ds(group * owners * OUT_ROWS + spot, owners, stride=OUT_ROWS), :]
             for group in range(groups)
         ]
         return jnp.concatenate(tiles[:half], axis=0), jnp.concatenate(tiles[half:], axis=0)
 
     def make_params():
-        lower, upper = [sum(side) for side in zip(*(collect(READ + i) for i in range(3)))]
+        sides = []
+        for high, rest in zip(collect(READ), collect(REST)):
+            rest, step = unpack_rests(high, rest)
+            sides.append((high + rest, step))
+        (lower, lower_step), (upper, upper_step) = sides
         read = (jnp.where(left, lower, swap(upper)), jnp.where(left, swap(lower), upper))
-        lower, upper = [
-            sum(side[:, i : i + 1] for i in range(3)) + jnp.zeros_like(side)
-            for side in collect(STEP)
-        ]
-        step = jnp.exp(jnp.where(left, lower, upper))
+        step = jnp.exp(jnp.where(left, lower_step, upper_step))
         decay_row = jnp.concatenate([decay_log[...], decay_log[...]], axis=1)
         rotation_row = jnp.concatenate([rotation[...], rotation[...]], axis=1)
         pole = (
@@ -509,7 +536,7 @@
         rows_in[...] = got[...].astype(jnp.float32)
         blocks = []
         for s in range(owners):
-            spots = [(group * owners + s) * ROWS for group in range(groups)]
+            spots = [(group * owners + s) * OUT_ROWS for group in range(groups)]
             blocks.append(
                 jnp.concatenate(
                     [rows_in[spot : spot + SUBLANES] for spot in spots]
@@ -723,9 +750,10 @@
     f32, bf16 = jnp.float32, jnp.bfloat16
 
     def exchange(value):
-        value = value.reshape(peers, ROWS // 2, 2, LANES)
+        rows = value.shape[0] // peers
+        value = value.reshape(peers, rows // 2, 2, LANES)
         value = lax.all_to_all(value, ("ch", "seq"), split_axis=0, concat_axis=0, tiled=True)
-        return value.reshape(peers * ROWS, LANES)
+        return value.reshape(peers * rows, LANES)
 
     anywhere = pl.BlockSpec(memory_space=pl.ANY)
     held = [jnp.asarray(table) for table in transform_tables(owners, length, norm_scale)]
@@ -735,7 +763,7 @@
     )
     pieces, *held = pl.pallas_call(
         pack_kernel,
-        out_shape=[jax.ShapeDtypeStruct((peers * ROWS, LANES), bf16)]
+        out_shape=[jax.ShapeDtypeStruct((peers * OUT_ROWS, LANES), bf16)]
         + [jax.ShapeDtypeStruct(value.shape, value.dtype) for value in held],
         in_specs=[anywhere] * len(sources),
         out_specs=[vmem] * (1 + len(held)),
@@ -744,7 +772,7 @@
             pltpu.VMEM((LANES, channels), f32),
             pltpu.VMEM((1, channels), f32),
             pltpu.VMEM((channels, LANES), f32),
-            pltpu.VMEM((peers * ROWS, LANES), f32),
+            pltpu.VMEM((peers * OUT_ROWS, LANES), f32),
             pltpu.SemaphoreType.DMA((len(sources),)),
         ],
         compiler_params=memory,
@@ -756,7 +784,7 @@
         in_specs=[vmem] * 5,
         out_specs=vmem,
         scratch_shapes=[
-            pltpu.VMEM((peers * ROWS, LANES), f32),
+            pltpu.VMEM((peers * OUT_ROWS, LANES), f32),
             pltpu.VMEM((2, (owners + 1) * 2 * part_count, 2 * LANES), bf16),
             pltpu.VMEM(((owners + 1) * 2 * part_count, 2 * LANES), f32),
             pltpu.VMEM(((owners + 1) * part_count, 2 * LANES), f32),

time: 30.5 us -> 30.1 us (0.987)
    all_to_all x2, blocking collectives: 25.7 us -> 25.4 us  [exchange(): lax.all_to_all(value, ('ch', 'seq'), split_axis=0, concat_axis=0, tiled=T...]
where the time goes in v10:
time: 30.1 us; the launch traced here: 30 us
  blocking collectives  25.4 us (84%)
  Pallas kernels  3.89 us (13%)
  between operations  0.66 us (2%)
    all_to_all x2, blocking collectives, exchange(): lax.all_to_all(value, ('ch', 'seq'), split_axis=0, concat_axis=0, tiled=T...  25.4 us
    pallas_call x1, Pallas kernels, kernel_device(): pl.pallas_call(functools.partial(main_kernel, owners, norm_scale), out_sh...  1.8 us
    pallas_call x1, Pallas kernels, kernel_device(): pl.pallas_call(pack_kernel, out_shape=[jax.ShapeDtypeStruct((peers * OUT_...  1.24 us
    pallas_call x1, Pallas kernels, kernel_device(): pl.pallas_call(unpack_kernel, out_shape=[jax.ShapeDtypeStruct((channels,...  0.85 us

profile of v10, /device:TPU:0, one launch (start us, length us, event | category | flops | bytes accessed | tf_op | source)
XLA Modules:
  0.0 30.0 jit_solution(9721858138190215105)
XLA Ops:
  0.6 1.2 %shard_map.111 = (bf16[576,128]{1,0:T(8,128)(2,1)S(1)}, bf16[2,256,256]{2,1,0:T(8,128)(2,1)S(1)}, f32[9,4,128]{2,1,0:T(4,128)S(1)}, f32[1,64]{1,0:T(1,128)S(1)}, f32[1,64]{1,0:T(1,128)S(1)}) custom-call(bf16[256,128]{1,0:T(8,128)(2,1)} %inputs.1, bf16[256,128]{1,0:T(8,128)(2,1)} %out_grad.1, f32[128,256]{1,0:T(8,128)} %bitcast.18, f32[1,256]{1,0:T(1,128)} %bitcast.19, ...), custom_call_target="tpu_custom_call" | custom-call | tf_op jit(solution)/shard_map/pallas_call | solution.py:764
  1.9 14.9 %all_to_all.10 = bf16[32,9,2,128]{3,2,1,0:T(2,128)(2,1)S(1)} all-to-all(bf16[32,9,2,128]{3,2,1,0:T(2,128)(2,1)S(1)} %bitcast.15), channel_id=1, replica_groups=mesh['seq'=8,'ch'=4] {'ch','seq'}, dimensions={0} | all-to-all | bytes 294912 | tf_op jit(solution)/shard_map/all_to_all | solution.py:755
  16.8 1.8 %shard_map.112 = f32[640,128]{1,0:T(8,128)S(1)} custom-call(bf16[576,128]{1,0:T(8,128)(2,1)S(1)} %bitcast.14, bf16[2,256,256]{2,1,0:T(8,128)(2,1)S(1)} %get-tuple-element.14.matrix, f32[9,4,128]{2,1,0:T(4,128)S(1)} %get-tuple-element.15.twiddle, f32[1,64]{1,0:T(1,128)S(1)} %get-tuple-element.16.decay_log, f32[1,64]{1,0:T(1,128)S(1)} %get-tuple-element.17.rotation), custom_call_target="tpu_custom_call" | custom-call | tf_op jit(solution)/shard_map/pallas_call | solution.py:781
  18.7 10.4 %all_to_all.11 = f16[32,10,2,128]{3,2,1,0:T(2,128)(2,1)S(1)} all-to-all(f16[32,10,2,128]{3,2,1,0:T(2,128)(2,1)S(1)} %bitcast.16), channel_id=1, replica_groups=mesh['seq'=8,'ch'=4] {'ch','seq'}, dimensions={0} | all-to-all | bytes 327680 | tf_op jit(solution)/shard_map/all_to_all | solution.py:755
  29.1 0.9 %shard_map.113 = (f32[256,128]{1,0:T(8,128)}, f32[128,256]{1,0:T(8,128)}, f32[256]{0:T(256)}, f32[2,64]{1,0:T(2,128)}) custom-call(f32[640,128]{1,0:T(8,128)S(1)} %convert.1.got), custom_call_target="tpu_custom_call" | custom-call | tf_op jit(solution)/shard_map/pallas_call | solution.py:801
  (2 shorter events, 0.0 us)

commit v11 on v10

--- a/solution.py
+++ b/solution.py
@@ -354,7 +354,7 @@
 STEP_LANES, SCALE_LANES = (0, 8), (16, 17, 18, 19)
 SPARE = 15.0
 PARTS = 4
-FRESH = 4
+FRESH = 5
 
 
 def pack_kernel(inputs, out_grad, readout, log_step, *refs):
@@ -708,17 +708,21 @@
     singles = got[pl.ds(SINGLES, peers, stride=ROWS), :]
     exponents = [jnp.broadcast_to(singles[:, spot : spot + 1], (peers, LANES)) for spot in SCALE_LANES]
     scales = [jnp.exp2(value) for value in exponents]
-    for i in range(2):
-        wide[i] = scales[i]
+    wide[...] = scales[0]
+    lane = lax.broadcasted_iota(jnp.int32, (peers, LANES), 1)
+    row = lax.broadcasted_iota(jnp.int32, (peers, LANES), 0)
+
+    def by_channel(value, spot):
+        mine = jnp.where(row - spot == lane // SUBLANES, value, 0.0)
+        return jnp.sum(mine, axis=0, keepdims=True)
+
     for spot in range(0, peers, per_row):
         part = slice(spot * SUBLANES, (spot + per_row) * SUBLANES)
-        for i, first, target in ((1, GRADS, grads), (0, LAGS, kernel_grad)):
-            for peer in range(spot, spot + per_row):
-                place = peer * ROWS + first
-                target[peer * SUBLANES : (peer + 1) * SUBLANES] = (
-                    got[place : place + SUBLANES] * wide[i, peer : peer + 1, :]
-                )
-        readout_grad[:, part] = grads[part].T
+        for peer in range(spot, spot + per_row):
+            place, own = peer * ROWS, slice(peer * SUBLANES, (peer + 1) * SUBLANES)
+            grads[own] = got[place + GRADS : place + STATE]
+            kernel_grad[own] = got[place + LAGS : place + GRADS] * wide[peer : peer + 1, :]
+        readout_grad[:, part] = grads[part].T * by_channel(scales[1], spot)
 
     high = got[pl.ds(STATE, peers, stride=ROWS), :]
     low = got[pl.ds(STATE + 1, peers, stride=ROWS), :]
@@ -726,15 +730,13 @@
     states = state_grad.shape[1]
     state_grad[0:1] = total[:, :states]
     state_grad[1:2] = total[:, states:]
-    lane = lax.broadcasted_iota(jnp.int32, (peers, LANES), 1)
-    row = lax.broadcasted_iota(jnp.int32, (peers, LANES), 0)
     high, low = (
         jnp.take_along_axis(singles, lane % SUBLANES + first, axis=1) for first in STEP_LANES
     )
     value = (high + low * (1.0 / 256.0)) * scales[3]
     for spot in range(0, peers, per_row):
-        mine = jnp.where(row - spot == lane // SUBLANES, value, 0.0)
-        step_grad[spot * SUBLANES : (spot + per_row) * SUBLANES] = jnp.sum(mine, axis=0)
+        part = slice(spot * SUBLANES, (spot + per_row) * SUBLANES)
+        step_grad[part] = by_channel(value, spot).reshape(LANES)
 
 
 def kernel_device(inputs, out_grad, readout, log_step, decay_log, rotation):
@@ -809,7 +811,7 @@
         in_specs=[vmem],
         out_specs=[vmem] * 4,
         scratch_shapes=[
-            pltpu.VMEM((2, peers, LANES), f32),
+            pltpu.VMEM((peers, LANES), f32),
             pltpu.VMEM((channels, LANES), f32),
         ],
         compiler_params=memory,

time: 30.1 us -> 30.1 us (level)
  no operation moved by 1% of the time
where the time goes in v11:
time: 30.1 us; the launch traced here: 29.9 us
  blocking collectives  25.4 us (84%)
  Pallas kernels  3.85 us (13%)
  between operations  0.66 us (2%)
    all_to_all x2, blocking collectives, exchange(): lax.all_to_all(value, ('ch', 'seq'), split_axis=0, concat_axis=0, tiled=T...  25.4 us
    pallas_call x1, Pallas kernels, kernel_device(): pl.pallas_call(functools.partial(main_kernel, owners, norm_scale), out_sh...  1.8 us
    pallas_call x1, Pallas kernels, kernel_device(): pl.pallas_call(pack_kernel, out_shape=[jax.ShapeDtypeStruct((peers * OUT_...  1.24 us
    pallas_call x1, Pallas kernels, kernel_device(): pl.pallas_call(unpack_kernel, out_shape=[jax.ShapeDtypeStruct((channels,...  0.81 us

profile of v11, /device:TPU:0, one launch (start us, length us, event | category | flops | bytes accessed | tf_op | source)
XLA Modules:
  0.0 29.9 jit_solution(16757424069413940676)
XLA Ops:
  0.6 1.2 %shard_map.111 = (bf16[576,128]{1,0:T(8,128)(2,1)S(1)}, bf16[2,256,256]{2,1,0:T(8,128)(2,1)S(1)}, f32[9,4,128]{2,1,0:T(4,128)S(1)}, f32[1,64]{1,0:T(1,128)S(1)}, f32[1,64]{1,0:T(1,128)S(1)}) custom-call(bf16[256,128]{1,0:T(8,128)(2,1)} %inputs.1, bf16[256,128]{1,0:T(8,128)(2,1)} %out_grad.1, f32[128,256]{1,0:T(8,128)} %bitcast.18, f32[1,256]{1,0:T(1,128)} %bitcast.19, ...), custom_call_target="tpu_custom_call" | custom-call | tf_op jit(solution)/shard_map/pallas_call | solution.py:766
  1.9 14.9 %all_to_all.10 = bf16[32,9,2,128]{3,2,1,0:T(2,128)(2,1)S(1)} all-to-all(bf16[32,9,2,128]{3,2,1,0:T(2,128)(2,1)S(1)} %bitcast.15), channel_id=1, replica_groups=mesh['seq'=8,'ch'=4] {'ch','seq'}, dimensions={0} | all-to-all | bytes 294912 | tf_op jit(solution)/shard_map/all_to_all | solution.py:757
  16.8 1.8 %shard_map.112 = f32[640,128]{1,0:T(8,128)S(1)} custom-call(bf16[576,128]{1,0:T(8,128)(2,1)S(1)} %bitcast.14, bf16[2,256,256]{2,1,0:T(8,128)(2,1)S(1)} %get-tuple-element.14.matrix, f32[9,4,128]{2,1,0:T(4,128)S(1)} %get-tuple-element.15.twiddle, f32[1,64]{1,0:T(1,128)S(1)} %get-tuple-element.16.decay_log, f32[1,64]{1,0:T(1,128)S(1)} %get-tuple-element.17.rotation), custom_call_target="tpu_custom_call" | custom-call | tf_op jit(solution)/shard_map/pallas_call | solution.py:783
  18.7 10.4 %all_to_all.11 = f16[32,10,2,128]{3,2,1,0:T(2,128)(2,1)S(1)} all-to-all(f16[32,10,2,128]{3,2,1,0:T(2,128)(2,1)S(1)} %bitcast.16), channel_id=1, replica_groups=mesh['seq'=8,'ch'=4] {'ch','seq'}, dimensions={0} | all-to-all | bytes 327680 | tf_op jit(solution)/shard_map/all_to_all | solution.py:757
  29.1 0.8 %shard_map.113 = (f32[256,128]{1,0:T(8,128)}, f32[128,256]{1,0:T(8,128)}, f32[256]{0:T(256)}, f32[2,64]{1,0:T(2,128)}) custom-call(f32[640,128]{1,0:T(8,128)S(1)} %convert.1.got), custom_call_target="tpu_custom_call" | custom-call | tf_op jit(solution)/shard_map/pallas_call | solution.py:803
  (2 shorter events, 0.0 us)

commit v12 on v11

--- a/solution.py
+++ b/solution.py
@@ -319,15 +319,10 @@
     return lane < 3, (lane >= LANES // 2) & (lane < LANES // 2 + 3)
 
 
-def pack_rests(high, rest, pieces):
-    lane = lax.broadcasted_iota(jnp.int32, high.shape, 1)
-    shared, replaced = rest_lanes(lane)
-    steps = jnp.where(high == 0.0, 0.0, rest / jnp.where(high == 0.0, 1.0, high))
-    steps = jnp.floor(steps * (256.0 * REST_STEPS) + 0.5)
-    rest = jnp.where(shared, steps * (2.0 * REST_STEPS + 1.0) + swap(steps), rest)
-    for i, piece in enumerate(pieces):
-        rest = jnp.where(lane == LANES // 2 + i, piece, rest)
-    return rest
+def rest_steps(value):
+    high = value.astype(jnp.bfloat16).astype(jnp.float32)
+    steps = jnp.where(high == 0.0, 0.0, (value - high) / jnp.where(high == 0.0, 1.0, high))
+    return jnp.floor(steps * (256.0 * REST_STEPS) + 0.5)
 
 
 def unpack_rests(high, rest):
@@ -354,6 +349,7 @@
 STEP_LANES, SCALE_LANES = (0, 8), (16, 17, 18, 19)
 SPARE = 15.0
 PARTS = 4
+EARLY = 9
 FRESH = 5
 
 
@@ -383,8 +379,18 @@
     channels = step.shape[1]
     peer = lax.broadcasted_iota(jnp.int32, (peers, channels), 0)
     channel = lax.broadcasted_iota(jnp.int32, (peers, channels), 1)
-    mine = jnp.where(channel == peer * SUBLANES + own, step[...], 0.0)
-    mine = jnp.broadcast_to(jnp.sum(mine, axis=1, keepdims=True), (peers, LANES))
+    sent_channel = channel == peer * SUBLANES + own
+
+    def pick(row):
+        value = jnp.sum(jnp.where(sent_channel, row, 0.0), axis=1, keepdims=True)
+        return jnp.broadcast_to(value, (peers, LANES))
+
+    half = LANES // 2
+    shared = rest_steps(read[0:SUBLANES]) * (2.0 * REST_STEPS + 1.0)
+    shared = shared + rest_steps(read[half : half + SUBLANES])
+    pieces = three_pieces(pick(step[...]))
+    placed = [(i, pick(shared[i : i + 1])) for i in range(3)]
+    placed += [(half + i, piece) for i, piece in enumerate(pieces)]
     for place, signal in enumerate((signals[0], signals[1])):
         value = signal.astype(jnp.float32)
         for peer in range(peers):
@@ -393,7 +399,11 @@
     value = turned[pl.ds(own, peers, stride=SUBLANES), :]
     high = value.astype(jnp.bfloat16).astype(jnp.float32)
     rows[pl.ds(READ, peers, stride=OUT_ROWS), :] = high
-    rows[pl.ds(REST, peers, stride=OUT_ROWS), :] = pack_rests(high, value - high, three_pieces(mine))
+    rest = value - high
+    lane = lax.broadcasted_iota(jnp.int32, (peers, LANES), 1)
+    for place, other in placed:
+        rest = jnp.where(lane == place, other, rest)
+    rows[pl.ds(REST, peers, stride=OUT_ROWS), :] = rest
     out[...] = rows[...].astype(jnp.bfloat16)
     for copy in copies[4:]:
         copy.wait()
@@ -433,6 +443,7 @@
     doubled,
     bases,
     powers,
+    early_powers,
     lags,
     sums,
 ):
@@ -492,6 +503,9 @@
         for place, value in enumerate(values):
             params[2 * place], params[2 * place + 1] = value
 
+    early = min(EARLY, pairs)
+    products = 4 * early * reach
+    nothing = twiddle[0, 1, 0].astype(jnp.int32) * (2 * SUBLANES)
     block_bit, reach_bit = length.bit_length() - 1, reach.bit_length() - 1
     bits = [(row & (1 << i)) != 0 for i in range(SUBLANES.bit_length() - 1)]
 
@@ -515,22 +529,23 @@
                 for side in range(2):
                     value = jnp.concatenate([table[place][side], table[place + 1][side]], axis=0)
                     for i, piece in enumerate(split_halves(value)):
-                        spot = 2 * i * reach + place * SUBLANES
-                        powers[p, spot : spot + 2 * SUBLANES, lanes_of(side)] = piece
-                        spot += reach
-                        powers[p, spot : spot + 2 * SUBLANES, lanes_of(side)] = piece
+                        for spot in (2 * i * reach, (2 * i + 1) * reach):
+                            spot += p * 4 * reach + place * SUBLANES
+                            if p < early:
+                                rows_at = pl.multiple_of(nothing + spot, 2 * SUBLANES)
+                                early_powers[pl.ds(rows_at, 2 * SUBLANES), lanes_of(side)] = piece
+                            else:
+                                powers[spot : spot + 2 * SUBLANES, lanes_of(side)] = piece
             base = by_rows(p, block_bit)
             bases[p, 0], bases[p, 1] = base
             bases[p, 2], bases[p, 3] = times(base, doubled_row(p, reach_bit))
 
-    def transform(source, target, count):
+    def transform(pieces, target, count):
         dot = functools.partial(jnp.dot, preferred_element_type=jnp.float32)
         cuts = [(owners + 1) * i // PARTS * count for i in range(PARTS + 1)]
         for part in map(slice, cuts, cuts[1:]):
-            low = source[1, part]
-            target[part] = (
-                dot(source[0, part], matrix[0]) + dot(low, matrix[0]) + dot(source[0, part], matrix[1])
-            )
+            high, low = pieces(part)
+            target[part] = dot(high, matrix[0]) + dot(low, matrix[0]) + dot(high, matrix[1])
 
     def spread_blocks():
         rows_in[...] = got[...].astype(jnp.float32)
@@ -552,7 +567,7 @@
                     spectra[i, k * rows : (k + 1) * rows, lanes_of(side)] = piece
 
     def to_frequencies():
-        transform(spectra, freq, rows)
+        transform(lambda part: (spectra[0, part], spectra[1, part]), freq, rows)
         make_params()
         make_tables()
 
@@ -564,8 +579,16 @@
             gr, gi = at_out[:, :length], at_out[:, length:]
             for side, value in enumerate((gr * ur + gi * ui, gr * ui - gi * ur)):
                 for i, piece in enumerate(split_halves(value)):
-                    spectra[i, k * part_count : (k + 1) * part_count, lanes_of(side)] = piece
-        transform(spectra, back, part_count)
+                    spot = products + (i * (owners + 1) + k) * part_count
+                    early_powers[spot : spot + part_count, lanes_of(side)] = piece
+
+        def pieces(part):
+            low = products + (owners + 1) * part_count
+            return tuple(
+                early_powers[first + part.start : first + part.stop] for first in (products, low)
+            )
+
+        transform(pieces, back, part_count)
 
     def finish():
         turned = []
@@ -628,7 +651,7 @@
             factor = jnp.concatenate(factor, axis=0).astype(jnp.bfloat16)
             raw = jnp.dot(
                 jnp.concatenate([factor, factor], axis=1),
-                powers[p],
+                (early_powers if p < early else powers)[p * 4 * reach : (p + 1) * 4 * reach],
                 preferred_element_type=jnp.float32,
             )
 
@@ -793,7 +816,8 @@
             pltpu.VMEM((14, pairs, LANES), f32),
             pltpu.VMEM((2 * (owners * length).bit_length(), pairs, LANES), f32),
             pltpu.VMEM((pairs, 4, owners, LANES), f32),
-            pltpu.VMEM((pairs, 2 * length, 2 * LANES), bf16),
+            pltpu.VMEM((2 * pairs * length, 2 * LANES), bf16),
+            pltpu.VMEM((2 * pairs * length + 2 * (owners + 1) * part_count, 2 * LANES), bf16),
             pltpu.VMEM((owners * part_count, length), f32),
             pltpu.VMEM((4, pairs, LANES), f32),
         ],

time: 30.1 us -> 30 us (level)
  no operation moved by 1% of the time
where the time goes in v12:
time: 30 us; the launch traced here: 29.9 us
  blocking collectives  25.4 us (85%)
  Pallas kernels  3.78 us (13%)
  between operations  0.66 us (2%)
    all_to_all x2, blocking collectives, exchange(): lax.all_to_all(value, ('ch', 'seq'), split_axis=0, concat_axis=0, tiled=T...  25.4 us
    pallas_call x1, Pallas kernels, kernel_device(): pl.pallas_call(functools.partial(main_kernel, owners, norm_scale), out_sh...  1.75 us
    pallas_call x1, Pallas kernels, kernel_device(): pl.pallas_call(pack_kernel, out_shape=[jax.ShapeDtypeStruct((peers * OUT_...  1.22 us
    pallas_call x1, Pallas kernels, kernel_device(): pl.pallas_call(unpack_kernel, out_shape=[jax.ShapeDtypeStruct((channels,...  0.81 us

profile of v12, /device:TPU:0, one launch (start us, length us, event | category | flops | bytes accessed | tf_op | source)
XLA Modules:
  0.0 29.9 jit_solution(11143537048633140489)
XLA Ops:
  0.6 1.2 %shard_map.111 = (bf16[576,128]{1,0:T(8,128)(2,1)S(1)}, bf16[2,256,256]{2,1,0:T(8,128)(2,1)S(1)}, f32[9,4,128]{2,1,0:T(4,128)S(1)}, f32[1,64]{1,0:T(1,128)S(1)}, f32[1,64]{1,0:T(1,128)S(1)}) custom-call(bf16[256,128]{1,0:T(8,128)(2,1)} %inputs.1, bf16[256,128]{1,0:T(8,128)(2,1)} %out_grad.1, f32[128,256]{1,0:T(8,128)} %bitcast.18, f32[1,256]{1,0:T(1,128)} %bitcast.19, ...), custom_call_target="tpu_custom_call" | custom-call | tf_op jit(solution)/shard_map/pallas_call | solution.py:789
  1.9 14.9 %all_to_all.10 = bf16[32,9,2,128]{3,2,1,0:T(2,128)(2,1)S(1)} all-to-all(bf16[32,9,2,128]{3,2,1,0:T(2,128)(2,1)S(1)} %bitcast.15), channel_id=1, replica_groups=mesh['seq'=8,'ch'=4] {'ch','seq'}, dimensions={0} | all-to-all | bytes 294912 | tf_op jit(solution)/shard_map/all_to_all | solution.py:780
  16.8 1.7 %shard_map.112 = f32[640,128]{1,0:T(8,128)S(1)} custom-call(bf16[576,128]{1,0:T(8,128)(2,1)S(1)} %bitcast.14, bf16[2,256,256]{2,1,0:T(8,128)(2,1)S(1)} %get-tuple-element.14.matrix, f32[9,4,128]{2,1,0:T(4,128)S(1)} %get-tuple-element.15.twiddle, f32[1,64]{1,0:T(1,128)S(1)} %get-tuple-element.16.decay_log, f32[1,64]{1,0:T(1,128)S(1)} %get-tuple-element.17.rotation), custom_call_target="tpu_custom_call" | custom-call | tf_op jit(solution)/shard_map/pallas_call | solution.py:806
  18.6 10.4 %all_to_all.11 = f16[32,10,2,128]{3,2,1,0:T(2,128)(2,1)S(1)} all-to-all(f16[32,10,2,128]{3,2,1,0:T(2,128)(2,1)S(1)} %bitcast.16), channel_id=1, replica_groups=mesh['seq'=8,'ch'=4] {'ch','seq'}, dimensions={0} | all-to-all | bytes 327680 | tf_op jit(solution)/shard_map/all_to_all | solution.py:780
  29.1 0.8 %shard_map.113 = (f32[256,128]{1,0:T(8,128)}, f32[128,256]{1,0:T(8,128)}, f32[256]{0:T(256)}, f32[2,64]{1,0:T(2,128)}) custom-call(f32[640,128]{1,0:T(8,128)S(1)} %convert.1.got), custom_call_target="tpu_custom_call" | custom-call | tf_op jit(solution)/shard_map/pallas_call | solution.py:827
  (2 shorter events, 0.0 us)

commit v13 on v12

--- a/solution.py
+++ b/solution.py
@@ -601,7 +601,13 @@
         most = jnp.zeros((part_count, LANES), jnp.float32)
         for b, block in enumerate(blocks):
             most = jnp.maximum(most, jnp.abs(block))
-            lags[b * part_count : (b + 1) * part_count] = block
+
+        for group in range(groups):
+            spots = slice(group * SUBLANES, (group + 1) * SUBLANES)
+            tiles = jnp.stack([block[spots] for block in blocks])
+            lags[group * owners * SUBLANES : (group + 1) * owners * SUBLANES] = jnp.swapaxes(
+                tiles, 0, 1
+            ).reshape(owners * SUBLANES, length)
 
         def param(place):
             return params[2 * place], params[2 * place + 1]
@@ -635,8 +641,8 @@
         for p in range(pairs):
             both = jnp.concatenate(
                 [
-                    lags[pl.ds(first_row, owners, stride=part_count), :]
-                    for first_row in (p, pairs + p)
+                    lags[channel * owners : (channel + 1) * owners]
+                    for channel in (p, pairs + p)
                 ],
                 axis=0,
             )

time: 30 us -> 30 us (level)
  no operation moved by 1% of the time
where the time goes in v13:
time: 30 us; the launch traced here: 29.8 us
  blocking collectives  25.4 us (85%)
  Pallas kernels  3.75 us (12%)
  between operations  0.66 us (2%)
    all_to_all x2, blocking collectives, exchange(): lax.all_to_all(value, ('ch', 'seq'), split_axis=0, concat_axis=0, tiled=T...  25.4 us
    pallas_call x1, Pallas kernels, kernel_device(): pl.pallas_call(functools.partial(main_kernel, owners, norm_scale), out_sh...  1.72 us
    pallas_call x1, Pallas kernels, kernel_device(): pl.pallas_call(pack_kernel, out_shape=[jax.ShapeDtypeStruct((peers * OUT_...  1.22 us
    pallas_call x1, Pallas kernels, kernel_device(): pl.pallas_call(unpack_kernel, out_shape=[jax.ShapeDtypeStruct((channels,...  0.81 us

profile of v13, /device:TPU:0, one launch (start us, length us, event | category | flops | bytes accessed | tf_op | source)
XLA Modules:
  0.0 29.8 jit_solution(15888122049485445561)
XLA Ops:
  0.6 1.2 %shard_map.111 = (bf16[576,128]{1,0:T(8,128)(2,1)S(1)}, bf16[2,256,256]{2,1,0:T(8,128)(2,1)S(1)}, f32[9,4,128]{2,1,0:T(4,128)S(1)}, f32[1,64]{1,0:T(1,128)S(1)}, f32[1,64]{1,0:T(1,128)S(1)}) custom-call(bf16[256,128]{1,0:T(8,128)(2,1)} %inputs.1, bf16[256,128]{1,0:T(8,128)(2,1)} %out_grad.1, f32[128,256]{1,0:T(8,128)} %bitcast.18, f32[1,256]{1,0:T(1,128)} %bitcast.19, ...), custom_call_target="tpu_custom_call" | custom-call | tf_op jit(solution)/shard_map/pallas_call | solution.py:795
  1.9 14.9 %all_to_all.10 = bf16[32,9,2,128]{3,2,1,0:T(2,128)(2,1)S(1)} all-to-all(bf16[32,9,2,128]{3,2,1,0:T(2,128)(2,1)S(1)} %bitcast.15), channel_id=1, replica_groups=mesh['seq'=8,'ch'=4] {'ch','seq'}, dimensions={0} | all-to-all | bytes 294912 | tf_op jit(solution)/shard_map/all_to_all | solution.py:786
  16.8 1.7 %shard_map.112 = f32[640,128]{1,0:T(8,128)S(1)} custom-call(bf16[576,128]{1,0:T(8,128)(2,1)S(1)} %bitcast.14, bf16[2,256,256]{2,1,0:T(8,128)(2,1)S(1)} %get-tuple-element.14.matrix, f32[9,4,128]{2,1,0:T(4,128)S(1)} %get-tuple-element.15.twiddle, f32[1,64]{1,0:T(1,128)S(1)} %get-tuple-element.16.decay_log, f32[1,64]{1,0:T(1,128)S(1)} %get-tuple-element.17.rotation), custom_call_target="tpu_custom_call" | custom-call | tf_op jit(solution)/shard_map/pallas_call | solution.py:812
  18.6 10.4 %all_to_all.11 = f16[32,10,2,128]{3,2,1,0:T(2,128)(2,1)S(1)} all-to-all(f16[32,10,2,128]{3,2,1,0:T(2,128)(2,1)S(1)} %bitcast.16), channel_id=1, replica_groups=mesh['seq'=8,'ch'=4] {'ch','seq'}, dimensions={0} | all-to-all | bytes 327680 | tf_op jit(solution)/shard_map/all_to_all | solution.py:786
  29.0 0.8 %shard_map.113 = (f32[256,128]{1,0:T(8,128)}, f32[128,256]{1,0:T(8,128)}, f32[256]{0:T(256)}, f32[2,64]{1,0:T(2,128)}) custom-call(f32[640,128]{1,0:T(8,128)S(1)} %convert.1.got), custom_call_target="tpu_custom_call" | custom-call | tf_op jit(solution)/shard_map/pallas_call | solution.py:833
  (2 shorter events, 0.0 us)

commit v14 on v13

--- a/solution.py
+++ b/solution.py
@@ -349,7 +349,6 @@
 STEP_LANES, SCALE_LANES = (0, 8), (16, 17, 18, 19)
 SPARE = 15.0
 PARTS = 4
-EARLY = 9
 FRESH = 5
 
 
@@ -443,7 +442,6 @@
     doubled,
     bases,
     powers,
-    early_powers,
     lags,
     sums,
 ):
@@ -503,9 +501,6 @@
         for place, value in enumerate(values):
             params[2 * place], params[2 * place + 1] = value
 
-    early = min(EARLY, pairs)
-    products = 4 * early * reach
-    nothing = twiddle[0, 1, 0].astype(jnp.int32) * (2 * SUBLANES)
     block_bit, reach_bit = length.bit_length() - 1, reach.bit_length() - 1
     bits = [(row & (1 << i)) != 0 for i in range(SUBLANES.bit_length() - 1)]
 
@@ -529,23 +524,22 @@
                 for side in range(2):
                     value = jnp.concatenate([table[place][side], table[place + 1][side]], axis=0)
                     for i, piece in enumerate(split_halves(value)):
-                        for spot in (2 * i * reach, (2 * i + 1) * reach):
-                            spot += p * 4 * reach + place * SUBLANES
-                            if p < early:
-                                rows_at = pl.multiple_of(nothing + spot, 2 * SUBLANES)
-                                early_powers[pl.ds(rows_at, 2 * SUBLANES), lanes_of(side)] = piece
-                            else:
-                                powers[spot : spot + 2 * SUBLANES, lanes_of(side)] = piece
+                        spot = 2 * i * reach + place * SUBLANES
+                        powers[p, spot : spot + 2 * SUBLANES, lanes_of(side)] = piece
+                        spot += reach
+                        powers[p, spot : spot + 2 * SUBLANES, lanes_of(side)] = piece
             base = by_rows(p, block_bit)
             bases[p, 0], bases[p, 1] = base
             bases[p, 2], bases[p, 3] = times(base, doubled_row(p, reach_bit))
 
-    def transform(pieces, target, count):
+    def transform(source, target, count):
         dot = functools.partial(jnp.dot, preferred_element_type=jnp.float32)
         cuts = [(owners + 1) * i // PARTS * count for i in range(PARTS + 1)]
         for part in map(slice, cuts, cuts[1:]):
-            high, low = pieces(part)
-            target[part] = dot(high, matrix[0]) + dot(low, matrix[0]) + dot(high, matrix[1])
+            low = source[1, part]
+            target[part] = (
+                dot(source[0, part], matrix[0]) + dot(low, matrix[0]) + dot(source[0, part], matrix[1])
+            )
 
     def spread_blocks():
         rows_in[...] = got[...].astype(jnp.float32)
@@ -567,7 +561,7 @@
                     spectra[i, k * rows : (k + 1) * rows, lanes_of(side)] = piece
 
     def to_frequencies():
-        transform(lambda part: (spectra[0, part], spectra[1, part]), freq, rows)
+        transform(spectra, freq, rows)
         make_params()
         make_tables()
 
@@ -579,16 +573,8 @@
             gr, gi = at_out[:, :length], at_out[:, length:]
             for side, value in enumerate((gr * ur + gi * ui, gr * ui - gi * ur)):
                 for i, piece in enumerate(split_halves(value)):
-                    spot = products + (i * (owners + 1) + k) * part_count
-                    early_powers[spot : spot + part_count, lanes_of(side)] = piece
-
-        def pieces(part):
-            low = products + (owners + 1) * part_count
-            return tuple(
-                early_powers[first + part.start : first + part.stop] for first in (products, low)
-            )
-
-        transform(pieces, back, part_count)
+                    spectra[i, k * part_count : (k + 1) * part_count, lanes_of(side)] = piece
+        transform(spectra, back, part_count)
 
     def finish():
         turned = []
@@ -657,7 +643,7 @@
             factor = jnp.concatenate(factor, axis=0).astype(jnp.bfloat16)
             raw = jnp.dot(
                 jnp.concatenate([factor, factor], axis=1),
-                (early_powers if p < early else powers)[p * 4 * reach : (p + 1) * 4 * reach],
+                powers[p],
                 preferred_element_type=jnp.float32,
             )
 
@@ -822,8 +808,7 @@
             pltpu.VMEM((14, pairs, LANES), f32),
             pltpu.VMEM((2 * (owners * length).bit_length(), pairs, LANES), f32),
             pltpu.VMEM((pairs, 4, owners, LANES), f32),
-            pltpu.VMEM((2 * pairs * length, 2 * LANES), bf16),
-            pltpu.VMEM((2 * pairs * length + 2 * (owners + 1) * part_count, 2 * LANES), bf16),
+            pltpu.VMEM((pairs, 2 * length, 2 * LANES), bf16),
             pltpu.VMEM((owners * part_count, length), f32),
             pltpu.VMEM((4, pairs, LANES), f32),
         ],

time: 30 us -> 30 us (level)
  no operation moved by 1% of the time
where the time goes in v14:
time: 30 us; the launch traced here: 29.9 us
  blocking collectives  25.4 us (85%)
  Pallas kernels  3.79 us (13%)
  between operations  0.66 us (2%)
    all_to_all x2, blocking collectives, exchange(): lax.all_to_all(value, ('ch', 'seq'), split_axis=0, concat_axis=0, tiled=T...  25.4 us
    pallas_call x1, Pallas kernels, kernel_device(): pl.pallas_call(functools.partial(main_kernel, owners, norm_scale), out_sh...  1.76 us
    pallas_call x1, Pallas kernels, kernel_device(): pl.pallas_call(pack_kernel, out_shape=[jax.ShapeDtypeStruct((peers * OUT_...  1.22 us
    pallas_call x1, Pallas kernels, kernel_device(): pl.pallas_call(unpack_kernel, out_shape=[jax.ShapeDtypeStruct((channels,...  0.81 us

profile of v14, /device:TPU:0, one launch (start us, length us, event | category | flops | bytes accessed | tf_op | source)
XLA Modules:
  0.0 29.9 jit_solution(12779974274100165095)
XLA Ops:
  0.6 1.2 %shard_map.111 = (bf16[576,128]{1,0:T(8,128)(2,1)S(1)}, bf16[2,256,256]{2,1,0:T(8,128)(2,1)S(1)}, f32[9,4,128]{2,1,0:T(4,128)S(1)}, f32[1,64]{1,0:T(1,128)S(1)}, f32[1,64]{1,0:T(1,128)S(1)}) custom-call(bf16[256,128]{1,0:T(8,128)(2,1)} %inputs.1, bf16[256,128]{1,0:T(8,128)(2,1)} %out_grad.1, f32[128,256]{1,0:T(8,128)} %bitcast.18, f32[1,256]{1,0:T(1,128)} %bitcast.19, ...), custom_call_target="tpu_custom_call" | custom-call | tf_op jit(solution)/shard_map/pallas_call | solution.py:781
  1.9 14.9 %all_to_all.10 = bf16[32,9,2,128]{3,2,1,0:T(2,128)(2,1)S(1)} all-to-all(bf16[32,9,2,128]{3,2,1,0:T(2,128)(2,1)S(1)} %bitcast.15), channel_id=1, replica_groups=mesh['seq'=8,'ch'=4] {'ch','seq'}, dimensions={0} | all-to-all | bytes 294912 | tf_op jit(solution)/shard_map/all_to_all | solution.py:772
  16.8 1.8 %shard_map.112 = f32[640,128]{1,0:T(8,128)S(1)} custom-call(bf16[576,128]{1,0:T(8,128)(2,1)S(1)} %bitcast.14, bf16[2,256,256]{2,1,0:T(8,128)(2,1)S(1)} %get-tuple-element.14.matrix, f32[9,4,128]{2,1,0:T(4,128)S(1)} %get-tuple-element.15.twiddle, f32[1,64]{1,0:T(1,128)S(1)} %get-tuple-element.16.decay_log, f32[1,64]{1,0:T(1,128)S(1)} %get-tuple-element.17.rotation), custom_call_target="tpu_custom_call" | custom-call | tf_op jit(solution)/shard_map/pallas_call | solution.py:798
  18.6 10.4 %all_to_all.11 = f16[32,10,2,128]{3,2,1,0:T(2,128)(2,1)S(1)} all-to-all(f16[32,10,2,128]{3,2,1,0:T(2,128)(2,1)S(1)} %bitcast.16), channel_id=1, replica_groups=mesh['seq'=8,'ch'=4] {'ch','seq'}, dimensions={0} | all-to-all | bytes 327680 | tf_op jit(solution)/shard_map/all_to_all | solution.py:772
  29.1 0.8 %shard_map.113 = (f32[256,128]{1,0:T(8,128)}, f32[128,256]{1,0:T(8,128)}, f32[256]{0:T(256)}, f32[2,64]{1,0:T(2,128)}) custom-call(f32[640,128]{1,0:T(8,128)S(1)} %convert.1.got), custom_call_target="tpu_custom_call" | custom-call | tf_op jit(solution)/shard_map/pallas_call | solution.py:818
  (2 shorter events, 0.0 us)

commit v15 on v13

--- a/solution.py
+++ b/solution.py
@@ -348,7 +348,7 @@
 LAGS, GRADS, STATE, SINGLES = 0, 8, 16, 18
 STEP_LANES, SCALE_LANES = (0, 8), (16, 17, 18, 19)
 SPARE = 15.0
-PARTS = 4
+PARTS = 3
 EARLY = 9
 FRESH = 5
 

time: 30 us -> 29.9 us (level)
  no operation moved by 1% of the time
where the time goes in v15:
time: 29.9 us; the launch traced here: 29.8 us
  blocking collectives  25.4 us (85%)
  Pallas kernels  3.69 us (12%)
  between operations  0.66 us (2%)
    all_to_all x2, blocking collectives, exchange(): lax.all_to_all(value, ('ch', 'seq'), split_axis=0, concat_axis=0, tiled=T...  25.4 us
    pallas_call x1, Pallas kernels, kernel_device(): pl.pallas_call(functools.partial(main_kernel, owners, norm_scale), out_sh...  1.66 us
    pallas_call x1, Pallas kernels, kernel_device(): pl.pallas_call(pack_kernel, out_shape=[jax.ShapeDtypeStruct((peers * OUT_...  1.22 us
    pallas_call x1, Pallas kernels, kernel_device(): pl.pallas_call(unpack_kernel, out_shape=[jax.ShapeDtypeStruct((channels,...  0.81 us

profile of v15, /device:TPU:0, one launch (start us, length us, event | category | flops | bytes accessed | tf_op | source)
XLA Modules:
  0.0 29.8 jit_solution(5569301399728657689)
XLA Ops:
  0.6 1.2 %shard_map.111 = (bf16[576,128]{1,0:T(8,128)(2,1)S(1)}, bf16[2,256,256]{2,1,0:T(8,128)(2,1)S(1)}, f32[9,4,128]{2,1,0:T(4,128)S(1)}, f32[1,64]{1,0:T(1,128)S(1)}, f32[1,64]{1,0:T(1,128)S(1)}) custom-call(bf16[256,128]{1,0:T(8,128)(2,1)} %inputs.1, bf16[256,128]{1,0:T(8,128)(2,1)} %out_grad.1, f32[128,256]{1,0:T(8,128)} %bitcast.18, f32[1,256]{1,0:T(1,128)} %bitcast.19, ...), custom_call_target="tpu_custom_call" | custom-call | tf_op jit(solution)/shard_map/pallas_call | solution.py:795
  1.9 14.9 %all_to_all.10 = bf16[32,9,2,128]{3,2,1,0:T(2,128)(2,1)S(1)} all-to-all(bf16[32,9,2,128]{3,2,1,0:T(2,128)(2,1)S(1)} %bitcast.15), channel_id=1, replica_groups=mesh['seq'=8,'ch'=4] {'ch','seq'}, dimensions={0} | all-to-all | bytes 294912 | tf_op jit(solution)/shard_map/all_to_all | solution.py:786
  16.8 1.7 %shard_map.112 = f32[640,128]{1,0:T(8,128)S(1)} custom-call(bf16[576,128]{1,0:T(8,128)(2,1)S(1)} %bitcast.14, bf16[2,256,256]{2,1,0:T(8,128)(2,1)S(1)} %get-tuple-element.14.matrix, f32[9,4,128]{2,1,0:T(4,128)S(1)} %get-tuple-element.15.twiddle, f32[1,64]{1,0:T(1,128)S(1)} %get-tuple-element.16.decay_log, f32[1,64]{1,0:T(1,128)S(1)} %get-tuple-element.17.rotation), custom_call_target="tpu_custom_call" | custom-call | tf_op jit(solution)/shard_map/pallas_call | solution.py:812
  18.5 10.4 %all_to_all.11 = f16[32,10,2,128]{3,2,1,0:T(2,128)(2,1)S(1)} all-to-all(f16[32,10,2,128]{3,2,1,0:T(2,128)(2,1)S(1)} %bitcast.16), channel_id=1, replica_groups=mesh['seq'=8,'ch'=4] {'ch','seq'}, dimensions={0} | all-to-all | bytes 327680 | tf_op jit(solution)/shard_map/all_to_all | solution.py:786
  29.0 0.8 %shard_map.113 = (f32[256,128]{1,0:T(8,128)}, f32[128,256]{1,0:T(8,128)}, f32[256]{0:T(256)}, f32[2,64]{1,0:T(2,128)}) custom-call(f32[640,128]{1,0:T(8,128)S(1)} %convert.1.got), custom_call_target="tpu_custom_call" | custom-call | tf_op jit(solution)/shard_map/pallas_call | solution.py:833
  (2 shorter events, 0.0 us)
